TPU v7x, 512 devices: a whole 4x4x16 slice. The times are simulated.
512 devices in a mesh: tensor: 16 (over x, z_hi), feature: 8 (over y, core), dp: 4 (over z_lo).
Axes of the slice: x: 4, y: 4, z: 16 (z_hi: 4, z_lo: 4; z = z_hi * 4 + z_lo), core: 2. Of those that a mesh axis runs over, the one named last changes fastest.
Arguments:
- mlp_input: bfloat16 [64, 4096], P(None, ('feature', 'dp')), may hold values from -6 to 6
- gate_weight: bfloat16 [4096, 28672], P(('feature', 'dp'), 'tensor'), may hold values from -0.09375 to 0.09375
- up_weight: bfloat16 [4096, 28672], P(('feature', 'dp'), 'tensor'), may hold values from -0.09375 to 0.09375
- down_weight: bfloat16 [28672, 4096], P('tensor', ('feature', 'dp')), may hold values from -0.03125 to 0.03125
- down_encoder: bfloat16 [65536, 4096], P('tensor', ('feature', 'dp')), may hold values from -6 to 6
- feature_ids: int32 [32], replicated, may hold values from 0 to 65535
- up_decoder: bfloat16 [131072, 4096], P('tensor', ('feature', 'dp')), may hold values from -0.09375 to 0.09375
- latent_ids: int32 [64, 64], replicated, may hold values from 0 to 131071, as said below
- latent_acts: float32 [64, 64], P('dp', 'tensor'), may hold values from 0.5 to 4
Outputs:
- attribution: float32 [32, 64, 64], P('feature', 'dp', 'tensor')
Inputs may be any that keep to these rules, and one draw needn't show every extreme that they name: `latent_ids`: the 64 latents of one token are distinct.
All inputs are finite; a program needn't handle non-finite values.
Results may differ from a plain program's by a relative error of at most 0.0029.
Values may be sent and summed in bfloat16 or wider, within the bound.
No kernel may reach another device: no remote copies, remote signals or barrier semaphores. Data moves between devices by JAX's collectives and lax.ppermute only.
A program may use at most 64 MiB of HBM per device.

v0:
```python
import math

import jax
import jax.numpy as jnp
from jax import lax
from jax.sharding import PartitionSpec as P


def factors(gate_pre, up_pre):
    sigmoid_gate = jax.nn.sigmoid(gate_pre)
    gate_factor = up_pre * sigmoid_gate * (1.0 + gate_pre * (1.0 - sigmoid_gate))
    up_factor = gate_pre * sigmoid_gate
    return (gate_factor, up_factor)


def arrange_blocks(partial_value, count_tensor, count_feature, count_data):
    features = partial_value.shape[0]
    tokens = partial_value.shape[1]
    slots = partial_value.shape[2]
    arranged = partial_value.reshape(
        count_feature,
        features // count_feature,
        count_data,
        tokens // count_data,
        count_tensor,
        slots // count_tensor,
    )
    arranged = arranged.transpose(4, 0, 2, 1, 3, 5)
    return arranged.reshape(
        count_tensor * count_feature * count_data,
        features // count_feature,
        tokens // count_data,
        slots // count_tensor,
    )


def on_device(
    mlp_input,
    gate_weight,
    up_weight,
    down_weight,
    down_encoder,
    feature_ids,
    up_decoder,
    latent_ids,
    latent_acts,
):
    contract = (((1,), (1,)), ((), ()))
    tensor_rank = lax.axis_index("tensor")
    tokens = mlp_input.shape[0]
    dblk = gate_weight.shape[0]
    ffblk = gate_weight.shape[1]
    features = feature_ids.shape[0]
    count_tensor = lax.axis_size("tensor")
    count_feature = lax.axis_size("feature")
    count_data = lax.axis_size("dp")
    enc_rows = down_encoder.shape[0]
    local_ids = feature_ids - tensor_rank * enc_rows
    picker = (local_ids[:, None] == jnp.arange(enc_rows, dtype=jnp.int32)[None, :]).astype(
        jnp.bfloat16
    )
    chosen = lax.psum(jnp.dot(picker, down_encoder, preferred_element_type=jnp.float32), "tensor")
    cotangent = chosen.astype(jnp.bfloat16)
    neuron_part = lax.dot_general(
        cotangent, down_weight, contract, preferred_element_type=jnp.float32
    )
    gate_part = jnp.dot(mlp_input, gate_weight, preferred_element_type=jnp.float32)
    up_part = jnp.dot(mlp_input, up_weight, preferred_element_type=jnp.float32)
    gate_pre, up_pre, neuron_grad = lax.psum((gate_part, up_part, neuron_part), ("feature", "dp"))
    gate_factor, up_factor = factors(gate_pre, up_pre)
    per_block = math.gcd(features, 8)
    grouped_rows = neuron_grad.reshape(features // per_block, per_block, ffblk)

    def feature_block(grad_rows):
        grad_gate = (
            (grad_rows[:, None, :] * gate_factor[None])
            .astype(jnp.bfloat16)
            .reshape(per_block * tokens, ffblk)
        )
        grad_up = (
            (grad_rows[:, None, :] * up_factor[None])
            .astype(jnp.bfloat16)
            .reshape(per_block * tokens, ffblk)
        )
        width_grad = lax.dot_general(
            grad_gate, gate_weight, contract, preferred_element_type=jnp.float32
        )
        width_grad = width_grad + lax.dot_general(
            grad_up, up_weight, contract, preferred_element_type=jnp.float32
        )
        return width_grad.reshape(per_block, tokens, dblk)

    width_part = lax.map(feature_block, grouped_rows).reshape(features, tokens, dblk)
    dec_rows = up_decoder.shape[0]
    local_latents = latent_ids - tensor_rank * dec_rows
    owner_mask = jnp.logical_and(local_latents >= 0, local_latents < dec_rows)
    picked = jnp.take(up_decoder, jnp.clip(local_latents, 0, dec_rows - 1), axis=0)
    picked = picked * owner_mask[:, :, None].astype(jnp.bfloat16)
    width_full = lax.psum(width_part, "tensor")
    partial_value = jnp.einsum(
        "ftd,tkd->ftk", width_full, picked.astype(jnp.float32), precision=lax.Precision.HIGHEST
    )
    arranged = arrange_blocks(partial_value, count_tensor, count_feature, count_data)
    own_block = lax.psum_scatter(
        arranged, ("tensor", "feature", "dp"), scatter_dimension=0, tiled=True
    )[0]
    return own_block * latent_acts[None, :, :]


def solution(mesh):
    in_specs = (
        P(None, ("feature", "dp")),
        P(("feature", "dp"), "tensor"),
        P(("feature", "dp"), "tensor"),
        P("tensor", ("feature", "dp")),
        P("tensor", ("feature", "dp")),
        P(),
        P("tensor", ("feature", "dp")),
        P(),
        P("dp", "tensor"),
    )
    out_specs = P("feature", "dp", "tensor")
    return jax.shard_map(
        on_device, mesh=mesh, in_specs=in_specs, out_specs=out_specs, check_vma=False
    )
```

profile of v0, /device:TPU:4, one launch (start us, length us, event | category | flops | bytes accessed | tf_op | source)
XLA Modules:
  0.0 1137.0 jit_solution(10292003025647488974)
XLA Ops:
  6.5 0.0 copy-start
  6.5 0.0 copy-start.1
  6.5 0.0 copy-start.3
  6.5 0.0 all-reduce.10.cloned.1.call-start
  6.6 0.8 broadcast_subtract_fusion
  7.4 1.6 fusion.5
  9.0 95.6 %psum.35 = bf16[32,128]{1,0:T(8,128)(2,1)S(1)} all-reduce(f32[32,128]{1,0:T(8,128)S(1)} %fusion.5), channel_id=1, replica_groups=mesh['tensor'=16,'feature'=8,'dp'=4] {'tensor'}, use_global_device_ids=true, to_apply=%region_0.0 | all-reduce | flops 4096 | bytes 24576 | tf_op jit(solution)/shard_map/psum | solution.py:62
  104.6 2.0 fusion.12
  106.6 0.0 copy-done.1
  106.6 1.7 fusion.13
  108.3 0.0 copy-done.3
  108.3 1.0 convolution_bitcast_fusion
  109.3 0.0 all-reduce.10.cloned.1.call-update
  109.3 0.0 all-reduce.6.cloned.1.call-start
  109.3 287.5 %all-reduce.10.cloned.1.call-done = (f32[4,8,1792]{2,1,0:T(8,128)}, f32[64,1792]{1,0:T(8,128)}, f32[64,1792]{1,0:T(8,128)}) async-done(((f32[4,8,1792]{2,1,0:T(8,128)}, f32[64,1792]{1,0:T(8,128)}, f32[64,1792]{1,0:T(8,128)}), (f32[4,8,1792]{2,1,0:T(8,128)}, f32[64,1792]{1,0:T(8,128)}, f32[64,1792]{1,0:T(8,128)})) %all-reduce.10.cloned.1.call-update) | async-done | bytes 1146896 | tf_op jit(solution)/shard_map/psum | solution.py:69
  396.8 1.4 fusion.6
  398.2 0.0 copy-start.4
  398.2 16.5 %while.10 = (s32[]{:T(128)}, f32[4,8,64,128]{3,1,0,2:T(8,128)}, f32[4,8,1792]{2,1,0:T(8,128)}, f32[64,1792]{1,0:T(8,128)S(1)}, bf16[128,1792]{1,0:T(8,128)(2,1)S...) while((s32[]{:T(128)}, f32[4,8,64,128]{3,1,0,2:T(8,128)}, f32[4,8,1792]{2,1,0:T(8,128)}, ...), condition=%wide.region_5.6_spmd, body=%wide.region_4.5_spmd.sunk | while | flops 473497600 | bytes 12493429 | solution.py:93
  398.2 0.8 dynamic-slice_bitcast_fusion.3
  399.1 0.7 multiply_convert_fusion.3
  399.8 0.0 copy-start.2
  399.8 0.6 fusion.35
  400.4 0.4 copy-done.2
  400.8 0.6 convolution_add_fusion.2
  401.4 0.9 copy_dynamic-update-slice_fusion.2
  402.3 0.8 dynamic-slice_bitcast_fusion.3
  403.1 0.7 multiply_convert_fusion.3
  403.9 0.0 copy-start.2
  403.9 0.6 fusion.35
  404.5 0.4 copy-done.2
  404.9 0.6 convolution_add_fusion.2
  405.6 0.9 copy_dynamic-update-slice_fusion.2
  406.4 0.8 dynamic-slice_bitcast_fusion.3
  407.3 0.7 multiply_convert_fusion.3
  408.0 0.0 copy-start.2
  408.0 0.6 fusion.35
  408.7 0.4 copy-done.2
  409.0 0.6 convolution_add_fusion.2
  409.7 0.9 copy_dynamic-update-slice_fusion.2
  410.6 0.8 dynamic-slice_bitcast_fusion.3
  411.4 0.7 multiply_convert_fusion.3
  412.2 0.0 copy-start.2
  412.2 0.6 fusion.35
  412.8 0.4 copy-done.2
  413.2 0.6 convolution_add_fusion.2
  413.8 0.9 copy_dynamic-update-slice_fusion.2
  414.7 0.0 all-reduce.6.cloned.1.call-update
  414.7 0.0 all-reduce.8.cloned.1.call-start
  414.8 0.0 copy-done.4
  414.8 0.1 reshape.43
  414.9 0.0 copy-done
  414.9 12.1 %gather_fusion = bf16[4096,128]{1,0:T(8,128)(2,1)S(1)} fusion(bf16[8192,128]{1,0:T(8,128)(2,1)S(1)} %copy-done, s32[4096]{0:T(1024)S(1)} %broadcast_clamp_fusion), kind=kCustom, calls=%fused_computation | custom fusion | bytes 2113536 | tf_op jit(solution)/shard_map/jit(_take)/gather | solution.py:97
  427.1 196.8 %all-reduce.6.cloned.1.call-done = f32[32,64,128]{2,0,1:T(8,128)} async-done(((f32[32,64,128]{2,0,1:T(8,128)}), f32[32,64,128]{2,0,1:T(8,128)}) %all-reduce.6.cloned.1.call-update) | async-done | bytes 1048592 | tf_op jit(solution)/shard_map/psum | solution.py:99
  623.8 4.4 convolution_bitcast_fusion.1
  628.2 1.8 copy.18
  630.0 3.2 reshape.39
  633.2 3.4 copy.19
  636.5 4.7 copy.20
  641.2 0.0 copy-start.5
  641.2 0.0 all-reduce.8.cloned.1.call-update
  641.2 487.9 %all-reduce.8.cloned.1.call-done = f32[512,4,16,4]{2,3,1,0:T(4,128)} async-done(((f32[512,4,16,4]{2,3,1,0:T(4,128)}), f32[512,4,16,4]{2,3,1,0:T(4,128)}) %all-reduce.8.cloned.1.call-update) | async-done | bytes 524304
  1129.1 0.0 copy-done.5
  1129.1 1.3 fusion.8
  (3 shorter events, 0.0 us)
Async XLA Ops:
  6.5 408.4 %copy-start = (bf16[8192,128]{1,0:T(8,128)(2,1)S(1)}, bf16[8192,128]{1,0:T(8,128)(2,1)}, u32[]{:S(2)}) copy-start(bf16[8192,128]{1,0:T(8,128)(2,1)} %param.17) | copy-start | bytes 6291460
  6.5 100.1 %copy-start.1 = (bf16[128,1792]{1,0:T(8,128)(2,1)S(1)}, bf16[128,1792]{1,0:T(8,128)(2,1)}, u32[]{:S(2)}) copy-start(bf16[128,1792]{1,0:T(8,128)(2,1)} %param.12) | copy-start | bytes 1376260
  6.5 101.7 %copy-start.3 = (bf16[1792,128]{1,0:T(8,128)(2,1)S(1)}, bf16[1792,128]{1,0:T(8,128)(2,1)}, u32[]{:S(2)}) copy-start(bf16[1792,128]{1,0:T(8,128)(2,1)} %param.14) | copy-start | bytes 1376260
  6.5 390.3 %all-reduce.10.cloned.1.call-start = ((), (), s32[]{:S(2)}) async-start(), calls=%async_computation.2 | async-start | bytes 2293760 | tf_op jit(solution)/shard_map/psum | solution.py:69
  109.3 514.5 %all-reduce.6.cloned.1.call-start = ((), (), s32[]{:S(2)}) async-start(), calls=%async_computation | async-start | bytes 2097152 | tf_op jit(solution)/shard_map/psum | solution.py:99
  398.2 16.6 %copy-start.4 = (s32[64,64]{1,0:T(8,128)S(1)}, s32[64,64]{1,0:T(8,128)}, u32[]{:S(2)}) copy-start(s32[64,64]{1,0:T(8,128)} %param.18) | copy-start | bytes 49156
  399.8 1.0 copy-start.2
  403.9 1.0 copy-start.2
  408.0 1.0 copy-start.2
  412.2 1.0 copy-start.2
  414.7 714.4 %all-reduce.8.cloned.1.call-start = ((), (), s32[]{:S(2)}) async-start(), calls=%async_computation.1 | async-start | bytes 8388608
  641.2 487.9 %copy-start.5 = (f32[16,4]{0,1:T(4,128)S(1)}, f32[16,4]{0,1:T(4,128)}, u32[]{:S(2)}) copy-start(f32[16,4]{0,1:T(4,128)} %param.19) | copy-start | bytes 772
Sparse Core Ops, SparseCore 0:
  109.4 287.3 all-reduce.9
  414.9 208.9 all-reduce.5
  641.4 487.7 all-reduce.7
where the time goes:
time: 1140 us
  waiting for transfers between devices  972 us (85%)
  blocking collectives  95.6 us (8%)
  local copies, waits for them, and re-layouts  33.6 us (3%)
  matrix products  15.8 us (1%)
  between operations  13.2 us (1%)
    unnamed x4, waiting for transfers between devices  488 us
    psum x1, waiting for transfers between devices, on_device(): lax.psum((gate_part, up_part, neuron_part), ('feature', 'dp'))  288 us
    psum x1, waiting for transfers between devices, on_device(): width_full = lax.psum(width_part, 'tensor')  197 us
    psum x1, blocking collectives, on_device(): lax.psum(jnp.dot(picker, down_encoder, preferred_element_type=jnp.float32...  95.6 us
  transfers between devices with their start and end apart: 3, of which 3 were waited for; matrix products, arithmetic and copies ran while one was open for 1% of the time, Pallas kernels for 0%

commit v1 on v0

v1 whole, which is shorter than its diff:
```python
import functools

import jax
import jax.numpy as jnp
from jax import lax
from jax.experimental import pallas as pl
from jax.experimental.pallas import tpu as pltpu
from jax.sharding import Mesh
from jax.sharding import PartitionSpec as P

F32 = jnp.float32
BF16 = jnp.bfloat16
CAP = 352
VMEM_LIMIT = 48 * 1024 * 1024


def nt(a, b):
    return lax.dot_general(a, b, (((1,), (1,)), ((), ())), preferred_element_type=F32)


def nn(a, b):
    return lax.dot_general(a, b, (((1,), (0,)), ((), ())), preferred_element_type=F32)


def plan_kernel(owners, dec_rows, where_ref, ids_ref, pos_ref, list_ref):
    rows, lanes = ids_ref.shape
    ids = ids_ref[...]
    owner = lax.div(ids, dec_rows)
    upto = lax.broadcasted_iota(jnp.int32, (lanes, lanes), 0) <= lax.broadcasted_iota(
        jnp.int32, (lanes, lanes), 1
    )
    upto = upto.astype(F32).astype(BF16)
    before = lax.broadcasted_iota(jnp.int32, (rows, rows), 1) < lax.broadcasted_iota(
        jnp.int32, (rows, rows), 0
    )
    before = before.astype(F32).astype(BF16)
    ones = jnp.ones((lanes, lanes), BF16)
    pos = jnp.zeros((rows, lanes), F32)
    for o in range(owners):
        hit = (owner == o).astype(F32)
        hit16 = hit.astype(BF16)
        total = nn(hit16, ones).astype(BF16)
        count = nn(hit16, upto) + nn(before, total)
        pos = pos + hit * (count - 1.0)
    pos_ref[...] = pos.astype(jnp.int32)
    rank = where_ref[0]
    start = where_ref[1] * CAP
    mine = jnp.where(owner == rank, pos - start.astype(F32), -1.0)
    local = (ids - rank * dec_rows).astype(F32)
    slot = lax.broadcasted_iota(jnp.int32, (CAP, lanes), 0).astype(F32)
    acc = jnp.zeros((CAP, lanes), F32)
    for r in range(rows):
        acc = acc + jnp.where(mine[r : r + 1, :] == slot, local[r : r + 1, :], 0.0)
    list_ref[...] = jnp.sum(acc, axis=1, keepdims=True).astype(jnp.int32)


def plan(ids, rank, turn, owners, dec_rows):
    flat = ids.reshape(-1, 128)
    pos, rows = pl.pallas_call(
        functools.partial(plan_kernel, owners, dec_rows),
        out_shape=(
            jax.ShapeDtypeStruct(flat.shape, jnp.int32),
            jax.ShapeDtypeStruct((CAP, 1), jnp.int32),
        ),
        in_specs=[
            pl.BlockSpec(memory_space=pltpu.SMEM),
            pl.BlockSpec(memory_space=pltpu.VMEM),
        ],
        out_specs=(pl.BlockSpec(memory_space=pltpu.VMEM), pl.BlockSpec(memory_space=pltpu.VMEM)),
        compiler_params=pltpu.CompilerParams(vmem_limit_bytes=VMEM_LIMIT),
    )(jnp.stack([rank, turn]).astype(jnp.int32), flat)
    return pos.reshape(-1), rows.reshape(-1)


def forward_kernel(half, core_ref, x_ref, cot_ref, gate_ref, up_ref, down_ref, rec_ref, out_ref):
    core = core_ref[0]
    tokens = x_ref.shape[0]
    features = cot_ref.shape[0]
    dblk = x_ref.shape[1]
    group = 2 * tokens + features
    x_own = x_ref[...]
    x_far = rec_ref[3 * half : 3 * half + tokens, :]
    cot_own = cot_ref[:, :dblk]
    cot_far = cot_ref[:, dblk:]
    for i in range(half // 128):
        col = pl.ds(pl.multiple_of(core * half + i * 128, 128), 128)
        far = slice(i * 128, (i + 1) * 128)
        base = i * group
        out_ref[base : base + tokens, :] = nn(x_own, gate_ref[:, col]) + nn(x_far, rec_ref[far, :])
        far = slice(half + i * 128, half + (i + 1) * 128)
        out_ref[base + tokens : base + 2 * tokens, :] = nn(x_own, up_ref[:, col]) + nn(
            x_far, rec_ref[far, :]
        )
        far = slice(2 * half + i * 128, 2 * half + (i + 1) * 128)
        out_ref[base + 2 * tokens : base + group, :] = nt(cot_own, down_ref[col, :]) + nt(
            cot_far, rec_ref[far, :]
        )
    used = (half // 128) * group
    if out_ref.shape[0] > used:
        out_ref[used:, :] = jnp.zeros((out_ref.shape[0] - used, 128), F32)


def main_kernel(
    half, tokens, features, core_ref, pre_ref, gate_ref, up_ref, rec_ref, own_ref, far_ref,
    mine_ref, theirs_ref, weight, grads,
):
    core = core_ref[0]
    step = pl.program_id(0)
    tile = own_ref.shape[0] // 64
    dblk = gate_ref.shape[0]
    group = 2 * tokens + features

    @pl.when(step == 0)
    def _():
        cols = pl.ds(pl.multiple_of(core * half, 128), half)
        weight[:dblk, :half] = gate_ref[:, cols]
        weight[:dblk, half:] = up_ref[:, cols]
        for i in range(half // 128):
            far = slice(i * 128, (i + 1) * 128)
            weight[dblk:, far] = rec_ref[far, :]
            far = slice(half + i * 128, half + (i + 1) * 128)
            weight[dblk:, far] = rec_ref[far, :]

    for i in range(half // 128):
        base = i * group
        gate_pre = pre_ref[pl.ds(pl.multiple_of(base + step * tile, 8), tile), :]
        up_pre = pre_ref[pl.ds(pl.multiple_of(base + tokens + step * tile, 8), tile), :]
        neuron = pre_ref[base + 2 * tokens : base + group, :]
        s = jax.nn.sigmoid(gate_pre)
        gate_factor = up_pre * s * (1.0 + gate_pre * (1.0 - s))
        up_factor = gate_pre * s
        for j in range(features):
            row = neuron[j : j + 1, :]
            to = slice(j * tile, (j + 1) * tile)
            grads[to, i * 128 : (i + 1) * 128] = (row * gate_factor).astype(BF16)
            grads[to, half + i * 128 : half + (i + 1) * 128] = (row * up_factor).astype(BF16)
    width = nt(grads[...], weight[...])
    high = width.astype(BF16)
    low = (width - high.astype(F32)).astype(BF16)
    dec = jnp.concatenate([own_ref[...], far_ref[...]], axis=1)
    lane = lax.broadcasted_iota(jnp.int32, (64, 128), 1)
    first = lax.broadcasted_iota(jnp.int32, (32, 128), 1) < 64
    which = lax.rem(lane, tile)
    for y in range(features // 8):
        part = slice(y * 128, (y + 1) * 128)
        both = jnp.concatenate([high[part, :], low[part, :]], axis=0)
        full = nt(dec, both)
        full = full[:, :128] + full[:, 128:]
        sel = full[:64, :]
        for t in range(1, tile):
            sel = jnp.where(which == t, full[t * 64 : (t + 1) * 64, :], sel)
        a, b = sel[:32, :], sel[32:, :]
        zero = jnp.where(first, a, pltpu.roll(b, 64, 1))
        one = jnp.where(first, pltpu.roll(a, 64, 1), b)
        keep = jnp.where(core == 0, zero, one)
        send = jnp.where(core == 0, one, zero)
        for x in range(4):
            to = pl.ds(pl.multiple_of(((x * 4 + y) * 4 + step) * 8, 8), 8)
            mine_ref[to, :] = keep[x * 8 : (x + 1) * 8, :]
            theirs_ref[to, :] = send[x * 8 : (x + 1) * 8, :]


def swap(value):
    return lax.ppermute(value, "c", [(0, 1), (1, 0)])


def on_device(
    mlp_input,
    gate_weight,
    up_weight,
    down_weight,
    down_encoder,
    feature_ids,
    up_decoder,
    latent_ids,
    latent_acts,
):
    tokens, dblk = mlp_input.shape
    half = gate_weight.shape[1] // 2
    features = feature_ids.shape[0]
    slots = latent_ids.shape[1]
    owners = 16
    core = lax.axis_index("c").astype(jnp.int32)
    rank = (lax.axis_index("x") * 4 + lax.axis_index("h")).astype(jnp.int32)
    core_arg = core[None]
    other = 1 - core

    enc_rows = down_encoder.shape[0]
    local = feature_ids - rank * enc_rows
    picker = (local[:, None] == jnp.arange(enc_rows, dtype=jnp.int32)[None, :]).astype(BF16)
    chosen = jnp.dot(picker, down_encoder, preferred_element_type=F32).astype(BF16)
    chosen_far = swap(chosen)

    def columns(w):
        part = lax.dynamic_slice(w, (0, other * half), (dblk, half))
        return part.reshape(dblk, half // 128, 128).transpose(1, 0, 2).reshape(half, 128)

    pack = jnp.concatenate(
        [
            columns(gate_weight),
            columns(up_weight),
            lax.dynamic_slice(down_weight, (other * half, 0), (half, dblk)),
            mlp_input,
        ],
        axis=0,
    )
    rec = swap(pack)

    dec_rows = up_decoder.shape[0]
    ordered = latent_ids.reshape(tokens, slots // 4, 2, 2).transpose(0, 3, 1, 2).reshape(-1)
    pos, rows = plan(ordered, rank, jnp.int32(0), owners, dec_rows)
    owner = ordered // dec_rows
    picked = jnp.take(up_decoder, rows, axis=0, mode="clip")
    packet = jnp.concatenate([picked, chosen, chosen_far], axis=0)

    def spread(value):
        return lax.all_gather(lax.all_gather(value, "h"), "x").reshape(owners, value.shape[0], 128)

    gathered = spread(packet)
    cot = jnp.sum(gathered[:, CAP:, :].astype(F32), axis=0).astype(BF16)
    cot = jnp.concatenate([cot[:features], cot[features:]], axis=1)

    used = (half // 128) * (2 * tokens + features)
    padded = -(-used // 128) * 128
    vmem = pl.BlockSpec(memory_space=pltpu.VMEM)
    smem = pl.BlockSpec(memory_space=pltpu.SMEM)
    params = pltpu.CompilerParams(vmem_limit_bytes=VMEM_LIMIT)
    part = pl.pallas_call(
        functools.partial(forward_kernel, half),
        out_shape=jax.ShapeDtypeStruct((padded, 128), F32),
        in_specs=[smem] + [vmem] * 6,
        out_specs=vmem,
        compiler_params=params,
    )(core_arg, mlp_input, cot, gate_weight, up_weight, down_weight, rec)
    part = lax.all_to_all(part.reshape(16, padded // 16, 128), ("y", "l"), 0, 0, tiled=True)
    part = jnp.sum(part, axis=0)
    pre = lax.all_to_all(
        jnp.broadcast_to(part[None], (16,) + part.shape), ("y", "l"), 0, 0, tiled=True
    ).reshape(padded, 128)

    table = gathered.reshape(owners * packet.shape[0], 128)
    place = owner * packet.shape[0] + jnp.minimum(pos, CAP - 1)
    dec = jnp.take(table, place, axis=0, mode="clip")
    rounds = jnp.max(pos) // CAP + 1

    def more(carry):
        return carry[0] < rounds

    def another(carry):
        turn, have = carry
        _, rows_now = plan(ordered, rank, turn, owners, dec_rows)
        got = spread(jnp.take(up_decoder, rows_now, axis=0, mode="clip"))
        at = pos - turn * CAP
        here = jnp.logical_and(at >= 0, at < CAP)
        at = owner * CAP + jnp.clip(at, 0, CAP - 1)
        now = jnp.take(got.reshape(owners * CAP, 128), at, axis=0, mode="clip")
        return turn + 1, jnp.where(here[:, None], now, have)

    _, dec = lax.while_loop(more, another, (jnp.int32(1), dec))
    dec_far = swap(dec)

    steps = 4
    block = dec.shape[0] // steps
    whole = lambda *shape: pl.BlockSpec(shape, lambda i: (0, 0))
    out_rows = 512
    mine, theirs = pl.pallas_call(
        functools.partial(main_kernel, half, tokens, features),
        grid=(steps,),
        out_shape=(jax.ShapeDtypeStruct((out_rows, 128), F32),) * 2,
        in_specs=[
            smem,
            whole(*pre.shape),
            whole(*gate_weight.shape),
            whole(*up_weight.shape),
            whole(*rec.shape),
            pl.BlockSpec((block, 128), lambda i: (i, 0)),
            pl.BlockSpec((block, 128), lambda i: (i, 0)),
        ],
        out_specs=(whole(out_rows, 128),) * 2,
        scratch_shapes=[
            pltpu.VMEM((2 * dblk, 2 * half), BF16),
            pltpu.VMEM((features * tokens // steps, 2 * half), BF16),
        ],
        compiler_params=params,
    )(core_arg, pre, gate_weight, up_weight, rec, dec, dec_far)

    total = mine + swap(theirs)
    total = jnp.sum(lax.all_to_all(total.reshape(16, 32, 128), ("x", "y"), 0, 0, tiled=True), axis=0)
    total = jnp.sum(lax.all_to_all(total.reshape(16, 2, 128), ("l", "h"), 0, 0, tiled=True), axis=0)
    total = total.reshape(2, 2, features // 8, tokens // 4).transpose(2, 3, 0, 1)
    return total.reshape(features // 8, tokens // 4, slots // 16) * latent_acts[None, :, :]


def solution(mesh):
    fine = Mesh(mesh.devices.reshape(4, 4, 4, 2, 4), ("x", "h", "y", "c", "l"))
    width = ("y", "c", "l")
    tensor = ("x", "h")
    in_specs = (
        P(None, width),
        P(width, tensor),
        P(width, tensor),
        P(tensor, width),
        P(tensor, width),
        P(),
        P(tensor, width),
        P(),
        P("l", tensor),
    )
    out_specs = P(("y", "c"), "l", tensor)
    return jax.shard_map(
        on_device, mesh=fine, in_specs=in_specs, out_specs=out_specs, check_vma=False
    )
```

time: 1140 us -> 199 us (0.17)
  the two profiles are of different devices: /device:TPU:4 before, /device:TPU:8 now
where the time goes in v1:
time: 199 us; the launch traced here: 198 us
  blocking collectives  66.5 us (33%)
  waiting for transfers between devices  40.9 us (21%)
  local copies, waits for them, and re-layouts  33.2 us (17%)
  starting transfers between devices  23.2 us (12%)
  between operations  15.5 us (8%)
  Pallas kernels  14.4 us (7%)
  other arithmetic  4.36 us (2%)
    all_gather x1, blocking collectives, spread(): lax.all_gather(value, 'h')  31.6 us
    all_gather x1, waiting for transfers between devices, spread(): lax.all_gather(lax.all_gather(value, 'h'), 'x')  27.7 us
    all_to_all x1, blocking collectives, on_device(): lax.all_to_all(total.reshape(16, 2, 128), ('l', 'h'), 0, 0, tiled=True)  21.8 us
    gather x1, local copies, waits for them, and re-layouts, on_device(): dec = jnp.take(table, place, axis=0, mode='clip')  15.9 us
    all_to_all x1, blocking collectives, on_device(): lax.all_to_all(total.reshape(16, 32, 128), ('x', 'y'), 0, 0, tiled=True)  13.1 us
    pallas_call x1, Pallas kernels, on_device(): pl.pallas_call(functools.partial(main_kernel, half, tokens, features), gr...  10.3 us
    all_to_all x1, waiting for transfers between devices, on_device(): lax.all_to_all(jnp.broadcast_to(part[None], (16,) + part.shape), ('y', 'l...  9.03 us
    ppermute x4, starting transfers between devices, swap(): return lax.ppermute(value, 'c', [(0, 1), (1, 0)])  7.85 us
  transfers between devices with their start and end apart: 7, of which 4 were waited for; matrix products, arithmetic and copies ran while one was open for 16% of the time, Pallas kernels for 1%

profile of v1, /device:TPU:8, one launch (start us, length us, event | category | flops | bytes accessed | tf_op | source)
XLA Modules:
  0.0 198.3 jit_solution(14209421514484134782)
XLA Ops:
  6.5 0.0 copy-start
  6.5 0.0 all-gather.13.cloned.1.call-start
  6.5 0.7 broadcast_subtract_fusion
  7.3 0.5 copy-done
  7.8 0.3 convolution_convert_fusion
  8.1 1.9 collective-permute-start
  10.0 0.8 copy.40
  10.9 1.8 copy.41
  12.7 0.0 copy-start.1
  12.7 0.0 copy-start.2
  12.7 1.8 reshape_reshape.9.ids_ref
  14.4 0.1 pad_add_fusion.1.where_ref
  14.5 2.7 %shard_map.91 = (s32[32,128]{1,0:T(8,128)S(1)}, s32[352,1]{1,0:T(8,128)S(1)}) custom-call(s32[2]{0:T(128)S(1)} %pad_add_fusion.1.where_ref, s32[32,128]{1,0:T(8,128)S(1)} %reshape_reshape.9.ids_ref), custom_call_target="tpu_custom_call" | custom-call | tf_op jit(solution)/shard_map/pallas_call | solution.py:59
  17.2 0.1 reduce.3
  17.4 3.0 %gather_fusion.2 = bf16[352,128]{1,0:T(8,128)(2,1)S(1)} fusion(bf16[8192,128]{1,0:T(8,128)(2,1)} %param.17, s32[1024]{0:T(1024)S(1)} %pad_clamp_fusion.1), kind=kCustom, calls=%fused_computation.2 | custom fusion | bytes 181632 | tf_op jit(solution)/shard_map/jit(_take)/gather | solution.py:213
  20.4 0.0 collective-permute-done
  20.4 31.6 %all-gather.2 = bf16[1664,128]{1,0:T(8,128)(2,1)} all-gather(bf16[416,128]{1,0:T(8,128)(2,1)S(1)} %pad_maximum_fusion.1), channel_id=4, replica_groups=mesh['x'=4,'h'=4,'y'=4,'c'=2,'l'=4] {'h'}, dimensions={0}, use_global_device_ids=true | all-gather | bytes 532480 | tf_op jit(solution)/shard_map/all_gather | solution.py:217
  52.1 0.0 all-gather.13.cloned.1.call-update
  52.1 0.0 copy-start.5
  52.1 0.0 copy-done.1
  52.1 0.0 copy-done.2
  52.1 0.0 copy-start.6
  52.2 0.2 copy.53
  52.4 0.2 copy.45
  52.5 0.2 copy.52
  52.7 0.2 copy.43
  52.9 0.2 copy-done.5
  53.1 0.0 copy-done.6
  53.1 0.9 pad_maximum_fusion
  54.0 1.9 collective-permute-start.1
  55.9 27.7 %all-gather.13.cloned.1.call-done = bf16[16,416,128]{2,1,0:T(8,128)(2,1)} async-done(((bf16[4,416,128]{2,1,0:T(8,128)(2,1)}), bf16[16,416,128]{2,1,0:T(8,128)(2,1)}) %all-gather.13.cloned.1.call-update) | async-done | bytes 1703952 | tf_op jit(solution)/shard_map/all_gather | solution.py:217
  83.6 1.0 slice_reduce_fusion
  84.6 0.0 collective-permute-done.1.rec_ref
  84.6 1.4 shard_map.92
  86.1 7.8 %all-to-all-start = ((f32[16,72,128]{2,1,0:T(8,128)}), f32[16,72,128]{2,1,0:T(8,128)S(1)}, u32[]{:S(2)}, u32[]{:S(2)}) async-start(f32[16,72,128]{2,1,0:T(8,128)} %bitcast.15), calls=%async_computation | async-start | bytes 1179648 | tf_op jit(solution)/shard_map/all_to_all | solution.py:235
  93.9 1.8 reshape.181
  95.7 0.6 fusion.3
  98.2 1.7 reshape.183
  99.9 1.7 reshape_reshape.11
  101.6 0.1 multiply_add_fusion
  101.8 15.9 %gather_fusion.3 = bf16[4096,128]{1,0:T(8,128)(2,1)} fusion(bf16[6656,128]{1,0:T(8,128)(2,1)} %bitcast.52, s32[4096]{0:T(1024)S(1)} %broadcast_clamp_fusion), kind=kCustom, calls=%fused_computation.3 | custom fusion | bytes 2113536 | tf_op jit(solution)/shard_map/jit(_take)/gather | solution.py:243
  117.7 0.0 all-to-all-done
  117.7 0.9 broadcast_in_dim.18
  118.6 7.5 %all-to-all-start.1 = ((f32[16,72,128]{2,1,0:T(8,128)}), f32[16,72,128]{2,1,0:T(8,128)S(1)}, u32[]{:S(2)}, u32[]{:S(2)}) async-start(f32[16,72,128]{2,1,0:T(8,128)} %broadcast_in_dim.18), calls=%async_computation.1 | async-start | bytes 1179648 | tf_op jit(solution)/shard_map/all_to_all | solution.py:237
  126.1 2.1 %collective-permute-start.2 = (bf16[4096,128]{1,0:T(8,128)(2,1)}, bf16[4096,128]{1,0:T(8,128)(2,1)S(1)}, u32[]{:S(2)}, u32[]{:S(2)}) collective-permute-start(bf16[4096,128]{1,0:T(8,128)(2,1)} %get-tuple-element.55.own_ref), channel_id=1, source_target_pairs={{0,4},{4,0},{1,5},{5,1},{2,6},{6,2},{3,7},{7,3},{8,12},{12,8},{9,1... | collective-permute-start | bytes 3145736 | tf_op jit(solution)/shard_map/ppermute | solution.py:164
  128.2 2.7 %collective-permute-done.2.far_ref = bf16[4096,128]{1,0:T(8,128)(2,1)S(1)} collective-permute-done((bf16[4096,128]{1,0:T(8,128)(2,1)}, bf16[4096,128]{1,0:T(8,128)(2,1)S(1)}, u32[]{:S(2)}, u32[]{:S(2)}) %collective-permute-start.2) | collective-permute-done | bytes 1048608 | tf_op jit(solution)/shard_map/ppermute | solution.py:164
  130.9 0.0 copy-start.3
  130.9 1.0 copy-done.3
  131.8 9.0 %all-to-all-done.1 = f32[16,72,128]{2,1,0:T(8,128)S(1)} async-done(((f32[16,72,128]{2,1,0:T(8,128)}), f32[16,72,128]{2,1,0:T(8,128)S(1)}, u32[]{:S(2)}, u32[]{:S(2)}) %all-to-all-start.1) | async-done | bytes 589856 | tf_op jit(solution)/shard_map/all_to_all | solution.py:237
  140.9 0.0 copy-start.4
  140.9 1.2 copy-done.4
  142.1 10.3 %shard_map.93 = (f32[512,128]{1,0:T(8,128)S(1)}, f32[512,128]{1,0:T(8,128)S(1)}) custom-call(s32[1]{0:T(128)} %bitcast.4.core_ref, f32[1152,128]{1,0:T(8,128)S(1)} %bitcast.50, bf16[128,1792]{1,0:T(8,128)(2,1)S(1)} %copy-done.1, bf16[128,1792]{1,0:T(8,128)(2,1)S(1)} %copy-done.2, bf16[2752,128]{1,0:T(8,128)(2,1)S(1)} %collective-permute-done.1.rec_ref, ...), custom_call_target="tpu_custom_call" | custom-call | tf_op jit(solution)/shard_map/pallas_call | solution.py:266
  152.4 0.0 copy-start.7
  152.4 1.9 collective-permute-start.3
  154.3 1.5 collective-permute-done.3
  155.9 13.1 %all_to_all.20 = f32[16,32,128]{2,1,0:T(8,128)S(1)} all-to-all(f32[16,32,128]{2,1,0:T(8,128)S(1)} %bitcast.56), channel_id=1, replica_groups=mesh['x'=4,'h'=4,'y'=4,'c'=2,'l'=4] {'x','y'}, dimensions={0} | all-to-all | bytes 524288 | tf_op jit(solution)/shard_map/all_to_all | solution.py:288
  169.0 21.8 %all_to_all.21 = f32[16,2,128]{2,1,0:T(2,128)S(1)} all-to-all(f32[16,2,128]{2,1,0:T(2,128)S(1)} %bitcast.64), channel_id=1, replica_groups=mesh['x'=4,'h'=4,'y'=4,'c'=2,'l'=4] {'l','h'}, dimensions={0} | all-to-all | bytes 32768 | tf_op jit(solution)/shard_map/all_to_all | solution.py:289
  190.8 0.1 reshape.186
  190.9 0.0 copy-done.7
  190.9 0.6 copy_multiply_fusion
  (13 shorter events, 0.2 us)
Async XLA Ops:
  6.5 1.2 copy-start
  6.5 77.1 %all-gather.13.cloned.1.call-start = ((), (), s32[]{:S(2)}) async-start(), calls=%async_computation.4 | async-start | bytes 2129920 | tf_op jit(solution)/shard_map/all_gather | solution.py:217
  8.1 12.3 %collective-permute-start = (bf16[32,128]{1,0:T(8,128)(2,1)S(1)}, bf16[32,128]{1,0:T(8,128)(2,1)S(1)}, u32[]{:S(2)}, u32[]{:S(2)}) collective-permute-start(bf16[32,128]{1,0:T(8,128)(2,1)S(1)} %convolution_convert_fusion), channel_id=1, source_target_pairs={{0,4},{4,0},{1,5},{5,1},{2,6},{6,2},{3,7},{7,3},{8,12},{12,8},{9,1... | collective-permute-start | bytes 24584 | tf_op jit(solution)/shard_map/ppermute | solution.py:164
  12.7 39.4 %copy-start.1 = (bf16[128,1792]{1,0:T(8,128)(2,1)S(1)}, bf16[128,1792]{1,0:T(8,128)(2,1)}, u32[]{:S(2)}) copy-start(bf16[128,1792]{1,0:T(8,128)(2,1)} %gate_ref.3) | copy-start | bytes 1376260
  12.7 39.4 %copy-start.2 = (bf16[128,1792]{1,0:T(8,128)(2,1)S(1)}, bf16[128,1792]{1,0:T(8,128)(2,1)}, u32[]{:S(2)}) copy-start(bf16[128,1792]{1,0:T(8,128)(2,1)} %up_ref.3) | copy-start | bytes 1376260
  52.1 1.0 copy-start.5
  52.1 1.0 copy-start.6
  54.0 30.6 %collective-permute-start.1 = (bf16[2752,128]{1,0:T(8,128)(2,1)}, bf16[2752,128]{1,0:T(8,128)(2,1)S(1)}, u32[]{:S(2)}, u32[]{:S(2)}) collective-permute-start(bf16[2752,128]{1,0:T(8,128)(2,1)} %pad_maximum_fusion), channel_id=1, source_target_pairs={{0,4},{4,0},{1,5},{5,1},{2,6},{6,2},{3,7},{7,3},{8,12},{12,8},{9,1... | collective-permute-start | bytes 2113544 | tf_op jit(solution)/shard_map/ppermute | solution.py:164
  86.1 31.6 %all-to-all-start = ((f32[16,72,128]{2,1,0:T(8,128)}), f32[16,72,128]{2,1,0:T(8,128)S(1)}, u32[]{:S(2)}, u32[]{:S(2)}) async-start(f32[16,72,128]{2,1,0:T(8,128)} %bitcast.15), calls=%async_computation | async-start | bytes 1179648 | tf_op jit(solution)/shard_map/all_to_all | solution.py:235
  118.6 22.3 %all-to-all-start.1 = ((f32[16,72,128]{2,1,0:T(8,128)}), f32[16,72,128]{2,1,0:T(8,128)S(1)}, u32[]{:S(2)}, u32[]{:S(2)}) async-start(f32[16,72,128]{2,1,0:T(8,128)} %broadcast_in_dim.18), calls=%async_computation.1 | async-start | bytes 1179648 | tf_op jit(solution)/shard_map/all_to_all | solution.py:237
  126.1 4.8 %collective-permute-start.2 = (bf16[4096,128]{1,0:T(8,128)(2,1)}, bf16[4096,128]{1,0:T(8,128)(2,1)S(1)}, u32[]{:S(2)}, u32[]{:S(2)}) collective-permute-start(bf16[4096,128]{1,0:T(8,128)(2,1)} %get-tuple-element.55.own_ref), channel_id=1, source_target_pairs={{0,4},{4,0},{1,5},{5,1},{2,6},{6,2},{3,7},{7,3},{8,12},{12,8},{9,1... | collective-permute-start | bytes 3145736 | tf_op jit(solution)/shard_map/ppermute | solution.py:164
  130.9 1.0 copy-start.3
  140.9 1.2 copy-start.4
  152.4 38.5 %copy-start.7 = (f32[16,4]{0,1:T(4,128)S(1)}, f32[16,4]{0,1:T(4,128)}, u32[]{:S(2)}) copy-start(f32[16,4]{0,1:T(4,128)} %param.19) | copy-start | bytes 772
  152.4 3.4 %collective-permute-start.3 = (f32[512,128]{1,0:T(8,128)S(1)}, f32[512,128]{1,0:T(8,128)S(1)}, u32[]{:S(2)}, u32[]{:S(2)}) collective-permute-start(f32[512,128]{1,0:T(8,128)S(1)} %get-tuple-element.57), channel_id=1, source_target_pairs={{0,4},{4,0},{1,5},{5,1},{2,6},{6,2},{3,7},{7,3},{8,12},{12,8},{9,1... | collective-permute-start | bytes 786440 | tf_op jit(solution)/shard_map/ppermute | solution.py:164
Sparse Core Ops, SparseCore 0:
  52.2 31.3 all-gather.12

commit v2 on v1

--- a/solution.py
+++ b/solution.py
@@ -22,9 +22,11 @@
     return lax.dot_general(a, b, (((1,), (0,)), ((), ())), preferred_element_type=F32)
 
 
-def plan_kernel(owners, dec_rows, where_ref, ids_ref, pos_ref, list_ref):
-    rows, lanes = ids_ref.shape
+def plan_kernel(owners, dec_rows, where_ref, ids_ref, slot_ref, list_ref, rounds_ref):
+    tokens, slots = ids_ref.shape
     ids = ids_ref[...]
+    ids = jnp.concatenate([ids[: tokens // 2], ids[tokens // 2 :]], axis=1)
+    rows, lanes = ids.shape
     owner = lax.div(ids, dec_rows)
     upto = lax.broadcasted_iota(jnp.int32, (lanes, lanes), 0) <= lax.broadcasted_iota(
         jnp.int32, (lanes, lanes), 1
@@ -42,34 +44,89 @@
         total = nn(hit16, ones).astype(BF16)
         count = nn(hit16, upto) + nn(before, total)
         pos = pos + hit * (count - 1.0)
-    pos_ref[...] = pos.astype(jnp.int32)
     rank = where_ref[0]
     start = where_ref[1] * CAP
+    at = pos.astype(jnp.int32) - start
+    here = jnp.logical_and(at >= 0, at < CAP)
+    late = (at >= CAP // 2).astype(jnp.int32)
+    slot = late * (owners * CAP // 2) + owner * (CAP // 2) + at - late * (CAP // 2)
+    slot = jnp.where(here, slot, -1)
+    slot_ref[...] = jnp.concatenate([slot[:, :slots], slot[:, slots:]], axis=0)
+    rounds_ref[0] = lax.div(jnp.max(pos).astype(jnp.int32), CAP) + 1
     mine = jnp.where(owner == rank, pos - start.astype(F32), -1.0)
     local = (ids - rank * dec_rows).astype(F32)
-    slot = lax.broadcasted_iota(jnp.int32, (CAP, lanes), 0).astype(F32)
+    want = lax.broadcasted_iota(jnp.int32, (CAP, lanes), 0).astype(F32)
     acc = jnp.zeros((CAP, lanes), F32)
     for r in range(rows):
-        acc = acc + jnp.where(mine[r : r + 1, :] == slot, local[r : r + 1, :], 0.0)
+        acc = acc + jnp.where(mine[r : r + 1, :] == want, local[r : r + 1, :], 0.0)
     list_ref[...] = jnp.sum(acc, axis=1, keepdims=True).astype(jnp.int32)
 
 
 def plan(ids, rank, turn, owners, dec_rows):
-    flat = ids.reshape(-1, 128)
-    pos, rows = pl.pallas_call(
+    slot, rows, rounds = pl.pallas_call(
         functools.partial(plan_kernel, owners, dec_rows),
         out_shape=(
-            jax.ShapeDtypeStruct(flat.shape, jnp.int32),
+            jax.ShapeDtypeStruct(ids.shape, jnp.int32),
             jax.ShapeDtypeStruct((CAP, 1), jnp.int32),
+            jax.ShapeDtypeStruct((1,), jnp.int32),
         ),
         in_specs=[
             pl.BlockSpec(memory_space=pltpu.SMEM),
             pl.BlockSpec(memory_space=pltpu.VMEM),
         ],
-        out_specs=(pl.BlockSpec(memory_space=pltpu.VMEM), pl.BlockSpec(memory_space=pltpu.VMEM)),
+        out_specs=(
+            pl.BlockSpec(memory_space=pltpu.VMEM),
+            pl.BlockSpec(memory_space=pltpu.VMEM),
+            pl.BlockSpec(memory_space=pltpu.SMEM),
+        ),
         compiler_params=pltpu.CompilerParams(vmem_limit_bytes=VMEM_LIMIT),
-    )(jnp.stack([rank, turn]).astype(jnp.int32), flat)
-    return pos.reshape(-1), rows.reshape(-1)
+    )(jnp.stack([rank, turn]).astype(jnp.int32), ids)
+    return slot, rows.reshape(-1), rounds[0]
+
+
+def expand_kernel(slot_ref, early_ref, late_ref, out_ref, table, block):
+    size = early_ref.shape[0]
+    piece = 128
+
+    def widen(i, carry):
+        at = pl.ds(pl.multiple_of(i * piece, piece), piece)
+        table[at, :] = early_ref[at, :].astype(F32)
+        table[pl.ds(pl.multiple_of(size + i * piece, piece), piece), :] = late_ref[at, :].astype(F32)
+        return carry
+
+    lax.fori_loop(0, size // piece, widen, 0)
+    tokens, slots = slot_ref.shape
+
+    def token(t, carry):
+        for low in range(2):
+            for r in range(slots // 4):
+                for high in range(2):
+                    src = jnp.maximum(slot_ref[t, r * 4 + high * 2 + low], 0)
+                    to = low * (slots // 2) + r * 2 + high
+                    block[to : to + 1, :] = table[pl.ds(src, 1), :]
+        out_ref[pl.ds(pl.multiple_of(t * slots, slots), slots), :] = block[...].astype(BF16)
+        return carry
+
+    lax.fori_loop(0, tokens, token, 0)
+
+
+def expand(slot, early, late):
+    size = early.shape[0]
+    return pl.pallas_call(
+        expand_kernel,
+        out_shape=jax.ShapeDtypeStruct((slot.shape[0] * slot.shape[1], 128), BF16),
+        in_specs=[
+            pl.BlockSpec(memory_space=pltpu.SMEM),
+            pl.BlockSpec(memory_space=pltpu.VMEM),
+            pl.BlockSpec(memory_space=pltpu.VMEM),
+        ],
+        out_specs=pl.BlockSpec(memory_space=pltpu.VMEM),
+        scratch_shapes=[
+            pltpu.VMEM((2 * size, 128), F32),
+            pltpu.VMEM((slot.shape[1], 128), F32),
+        ],
+        compiler_params=pltpu.CompilerParams(vmem_limit_bytes=VMEM_LIMIT),
+    )(slot, early, late)
 
 
 def forward_kernel(half, core_ref, x_ref, cot_ref, gate_ref, up_ref, down_ref, rec_ref, out_ref):
@@ -207,17 +264,15 @@
     rec = swap(pack)
 
     dec_rows = up_decoder.shape[0]
-    ordered = latent_ids.reshape(tokens, slots // 4, 2, 2).transpose(0, 3, 1, 2).reshape(-1)
-    pos, rows = plan(ordered, rank, jnp.int32(0), owners, dec_rows)
-    owner = ordered // dec_rows
+    slot, rows, rounds = plan(latent_ids, rank, jnp.int32(0), owners, dec_rows)
     picked = jnp.take(up_decoder, rows, axis=0, mode="clip")
-    packet = jnp.concatenate([picked, chosen, chosen_far], axis=0)
+    packet = lax.all_gather(jnp.concatenate([picked, chosen, chosen_far], axis=0), "h")
 
     def spread(value):
-        return lax.all_gather(lax.all_gather(value, "h"), "x").reshape(owners, value.shape[0], 128)
-
-    gathered = spread(packet)
-    cot = jnp.sum(gathered[:, CAP:, :].astype(F32), axis=0).astype(BF16)
+        return lax.all_gather(value, "x").reshape(owners * value.shape[1], 128)
+
+    cot = lax.all_gather(packet[:, CAP:, :], "x").reshape(owners, 2 * features, 128)
+    cot = jnp.sum(cot.astype(F32), axis=0).astype(BF16)
     cot = jnp.concatenate([cot[:features], cot[features:]], axis=1)
 
     used = (half // 128) * (2 * tokens + features)
@@ -232,29 +287,27 @@
         out_specs=vmem,
         compiler_params=params,
     )(core_arg, mlp_input, cot, gate_weight, up_weight, down_weight, rec)
+    part, packet = lax.optimization_barrier((part, packet))
     part = lax.all_to_all(part.reshape(16, padded // 16, 128), ("y", "l"), 0, 0, tiled=True)
+    early, late = spread(packet[:, : CAP // 2, :]), spread(packet[:, CAP // 2 : CAP, :])
     part = jnp.sum(part, axis=0)
+    part, early, late = lax.optimization_barrier((part, early, late))
     pre = lax.all_to_all(
         jnp.broadcast_to(part[None], (16,) + part.shape), ("y", "l"), 0, 0, tiled=True
     ).reshape(padded, 128)
 
-    table = gathered.reshape(owners * packet.shape[0], 128)
-    place = owner * packet.shape[0] + jnp.minimum(pos, CAP - 1)
-    dec = jnp.take(table, place, axis=0, mode="clip")
-    rounds = jnp.max(pos) // CAP + 1
+    dec = expand(slot, early, late)
 
     def more(carry):
         return carry[0] < rounds
 
     def another(carry):
         turn, have = carry
-        _, rows_now = plan(ordered, rank, turn, owners, dec_rows)
-        got = spread(jnp.take(up_decoder, rows_now, axis=0, mode="clip"))
-        at = pos - turn * CAP
-        here = jnp.logical_and(at >= 0, at < CAP)
-        at = owner * CAP + jnp.clip(at, 0, CAP - 1)
-        now = jnp.take(got.reshape(owners * CAP, 128), at, axis=0, mode="clip")
-        return turn + 1, jnp.where(here[:, None], now, have)
+        slot_now, rows_now, _ = plan(latent_ids, rank, turn, owners, dec_rows)
+        got = lax.all_gather(jnp.take(up_decoder, rows_now, axis=0, mode="clip"), "h")
+        now = expand(slot_now, spread(got[:, : CAP // 2, :]), spread(got[:, CAP // 2 :, :]))
+        here = slot_now.reshape(tokens, slots // 4, 2, 2).transpose(0, 3, 1, 2).reshape(-1, 1)
+        return turn + 1, jnp.where(here >= 0, now, have)
 
     _, dec = lax.while_loop(more, another, (jnp.int32(1), dec))
     dec_far = swap(dec)

time: 199 us -> 173 us (0.87)
  blocking collectives: 66.5 us -> 106 us
  waiting for transfers between devices: 40.9 us -> 4.22 us
  local copies, waits for them, and re-layouts: 33.2 us -> 10.6 us
  between operations: 15.5 us -> 0.28 us
  Pallas kernels: 14.4 us -> 23.4 us
    all_gather x1 -> x4, blocking collectives: 31.6 us -> 72.1 us  [the longest x1 31.4 us: on_device(): lax.all_gather(jnp.concatenate([picked, chosen, chosen_far], axis=0), 'h')]
    all_gather x1 -> x0, waiting for transfers between devices: 27.7 us -> none  [spread(): lax.all_gather(lax.all_gather(value, 'h'), 'x')]
    gather x1 -> x0, local copies, waits for them, and re-layouts: 15.9 us -> none  [on_device(): dec = jnp.take(table, place, axis=0, mode='clip')]
    all_to_all x1, waiting for transfers between devices: 9.03 us -> 0.01 us  [on_device(): lax.all_to_all(jnp.broadcast_to(part[None], (16,) + part.shape), ('y', 'l...]
    pallas_call x0 -> x1, Pallas kernels: none -> 8.21 us  [expand(): pl.pallas_call(expand_kernel, out_shape=jax.ShapeDtypeStruct((slot.shape[...]
    reshape x2 -> x0, local copies, waits for them, and re-layouts: 3.53 us -> none  [on_device(): latent_ids.reshape(tokens, slots // 4, 2, 2).transpose(0, 3, 1, 2)]
    another operation x2 -> x0, local copies, waits for them, and re-layouts: 3.46 us -> none  [plan(): flat = ids.reshape(-1, 128)]
    unnamed x19 -> x30, local copies, waits for them, and re-layouts: 4.08 us -> 4.51 us
  transfers between devices with their start and end apart: 7 -> 6, of which waited for: 4 -> 2; matrix products, arithmetic and copies ran while one was open for 16% -> 3% of each run, Pallas kernels for 1% -> 7%
where the time goes in v2:
time: 173 us
  blocking collectives  106 us (61%)
  Pallas kernels  23.4 us (14%)
  starting transfers between devices  22.2 us (13%)
  local copies, waits for them, and re-layouts  10.6 us (6%)
  other arithmetic  4.82 us (3%)
  waiting for transfers between devices  4.22 us (2%)
    all_gather x1, blocking collectives, on_device(): lax.all_gather(jnp.concatenate([picked, chosen, chosen_far], axis=0), 'h')  31.4 us
    all_gather x2, blocking collectives, spread(): return lax.all_gather(value, 'x').reshape(owners * value.shape[1], 128)  27.3 us
    all_to_all x1, blocking collectives, on_device(): lax.all_to_all(total.reshape(16, 2, 128), ('l', 'h'), 0, 0, tiled=True)  21.2 us
    all_gather x1, blocking collectives, on_device(): lax.all_gather(packet[:, CAP:, :], 'x').reshape(owners, 2 * features, 128)  13.4 us
    all_to_all x1, blocking collectives, on_device(): lax.all_to_all(total.reshape(16, 32, 128), ('x', 'y'), 0, 0, tiled=True)  12.9 us
    pallas_call x1, Pallas kernels, on_device(): pl.pallas_call(functools.partial(main_kernel, half, tokens, features), gr...  10.5 us
    ppermute x4, starting transfers between devices, swap(): return lax.ppermute(value, 'c', [(0, 1), (1, 0)])  8.41 us
    pallas_call x1, Pallas kernels, expand(): pl.pallas_call(expand_kernel, out_shape=jax.ShapeDtypeStruct((slot.shape[...  8.21 us
  transfers between devices with their start and end apart: 6, of which 2 were waited for; matrix products, arithmetic and copies ran while one was open for 3% of the time, Pallas kernels for 7%

profile of v2, /device:TPU:8, one launch (start us, length us, event | category | flops | bytes accessed | tf_op | source)
XLA Modules:
  0.0 172.5 jit_solution(8779059229648872302)
XLA Ops:
  0.0 0.0 copy-start
  0.0 0.0 copy-start.7
  0.0 0.0 copy-start.8
  0.0 1.2 constant_dynamic-slice_fusion.1
  1.2 0.2 copy.40
  1.4 0.2 copy.34
  1.6 0.0 copy-start.13
  1.6 0.2 copy.41
  1.8 0.2 copy.36
  2.0 0.0 copy-done.7
  2.0 0.0 copy-start.11
  2.0 0.0 copy-done.8
  2.0 0.9 pad_maximum_fusion
  2.9 1.9 %collective-permute-start.1 = (bf16[2752,128]{1,0:T(8,128)(2,1)}, bf16[2752,128]{1,0:T(8,128)(2,1)S(1)}, u32[]{:S(2)}, u32[]{:S(2)}) collective-permute-start(bf16[2752,128]{1,0:T(8,128)(2,1)} %pad_maximum_fusion), channel_id=1, source_target_pairs={{0,4},{4,0},{1,5},{5,1},{2,6},{6,2},{3,7},{7,3},{8,12},{12,8},{9,1... | collective-permute-start | bytes 2113544 | tf_op jit(solution)/shard_map/ppermute | solution.py:221
  4.8 0.0 copy-done.13
  4.9 0.0 copy-done
  4.9 0.3 convolution_convert_fusion
  5.2 0.0 copy-start.1
  5.2 0.0 copy-start.2
  5.2 2.5 %collective-permute-start = (bf16[32,128]{1,0:T(8,128)(2,1)S(1)}, bf16[32,128]{1,0:T(8,128)(2,1)S(1)}, u32[]{:S(2)}, u32[]{:S(2)}) collective-permute-start(bf16[32,128]{1,0:T(8,128)(2,1)S(1)} %convolution_convert_fusion), channel_id=1, source_target_pairs={{0,4},{4,0},{1,5},{5,1},{2,6},{6,2},{3,7},{7,3},{8,12},{12,8},{9,1... | collective-permute-start | bytes 24584 | tf_op jit(solution)/shard_map/ppermute | solution.py:221
  7.8 0.1 pad_add_fusion.1.where_ref
  7.8 0.0 copy-done.11
  7.9 3.2 %shard_map.91 = (s32[64,64]{1,0:T(8,128)S(1)}, s32[352,1]{1,0:T(8,128)S(1)}, s32[1]{0:T(128)}) custom-call(s32[2]{0:T(128)S(1)} %pad_add_fusion.1.where_ref, s32[64,64]{1,0:T(8,128)S(1)} %copy-done.11), custom_call_target="tpu_custom_call" | custom-call | tf_op jit(solution)/shard_map/pallas_call | solution.py:66
  11.1 0.1 reduce.4
  11.2 3.5 %gather_fusion.1 = bf16[352,128]{1,0:T(8,128)(2,1)} fusion(bf16[8192,128]{1,0:T(8,128)(2,1)} %param.17, s32[1024]{0:T(1024)S(1)} %pad_clamp_fusion.1), kind=kCustom, calls=%fused_computation.1 | custom fusion | bytes 181632 | tf_op jit(solution)/shard_map/jit(_take)/gather | solution.py:268
  14.7 0.0 collective-permute-done
  14.7 0.9 pad_maximum_fusion.1
  15.6 31.4 %all-gather.3 = bf16[1664,128]{1,0:T(8,128)(2,1)S(1)} all-gather(bf16[416,128]{1,0:T(8,128)(2,1)S(1)} %pad_maximum_fusion.1), channel_id=5, replica_groups=mesh['x'=4,'h'=4,'y'=4,'c'=2,'l'=4] {'h'}, dimensions={0}, use_global_device_ids=true | all-gather | bytes 532480 | tf_op jit(solution)/shard_map/all_gather | solution.py:269
  47.0 0.0 copy-start.9
  47.0 0.8 copy-done.9
  47.8 13.4 %all-gather.4 = bf16[16,64,128]{2,1,0:T(8,128)(2,1)} all-gather(bf16[4,64,128]{2,1,0:T(8,128)(2,1)S(1)} %slice.32), channel_id=6, replica_groups=mesh['x'=4,'h'=4,'y'=4,'c'=2,'l'=4] {'x'}, dimensions={0}, use_global_device_ids=true | all-gather | bytes 327680 | tf_op jit(solution)/shard_map/all_gather | solution.py:274
  61.1 1.0 reduce_sum.39
  62.2 0.0 collective-permute-done.1.rec_ref
  62.2 0.0 copy-start.3
  62.2 0.0 copy-done.1
  62.2 0.0 copy-done.2
  62.2 1.4 shard_map.92
  63.6 0.0 copy-start.10
  63.6 0.0 copy-done.3
  63.6 6.3 %all-to-all-start = ((f32[16,72,128]{2,1,0:T(8,128)}), f32[16,72,128]{2,1,0:T(8,128)}, u32[]{:S(2)}, u32[]{:S(2)}) async-start(f32[16,72,128]{2,1,0:T(8,128)} %bitcast.15), calls=%async_computation | async-start | bytes 1179648 | tf_op jit(solution)/shard_map/all_to_all | solution.py:291
  70.0 0.0 copy-done.10
  70.0 14.2 %all-gather.5 = bf16[16,176,128]{2,1,0:T(8,128)(2,1)S(1)} all-gather(bf16[4,176,128]{2,1,0:T(8,128)(2,1)S(1)} %get-tuple-element.76), channel_id=7, replica_groups=mesh['x'=4,'h'=4,'y'=4,'c'=2,'l'=4] {'x'}, dimensions={0}, use_global_device_ids=true | all-gather | bytes 901120 | tf_op jit(solution)/shard_map/all_gather | solution.py:272
  84.2 13.2 %all-gather.6 = bf16[16,176,128]{2,1,0:T(8,128)(2,1)S(1)} all-gather(bf16[4,176,128]{2,1,0:T(8,128)(2,1)S(1)} %get-tuple-element.75), channel_id=8, replica_groups=mesh['x'=4,'h'=4,'y'=4,'c'=2,'l'=4] {'x'}, dimensions={0}, use_global_device_ids=true | all-gather | bytes 901120 | tf_op jit(solution)/shard_map/all_gather | solution.py:272
  97.4 0.0 all-to-all-done
  97.4 1.1 reduce_sum.40
  98.5 0.9 broadcast_in_dim.17
  99.4 7.4 %all-to-all-start.1 = ((f32[16,72,128]{2,1,0:T(8,128)}), f32[16,72,128]{2,1,0:T(8,128)}, u32[]{:S(2)}, u32[]{:S(2)}) async-start(f32[16,72,128]{2,1,0:T(8,128)} %broadcast_in_dim.17), calls=%async_computation.1 | async-start | bytes 1179648 | tf_op jit(solution)/shard_map/all_to_all | solution.py:295
  106.8 8.2 %shard_map.93 = bf16[4096,128]{1,0:T(8,128)(2,1)} custom-call(s32[64,64]{1,0:T(8,128)S(1)} %get-tuple-element.54.slot_ref, bf16[2816,128]{1,0:T(8,128)(2,1)S(1)} %bitcast.46, bf16[2816,128]{1,0:T(8,128)(2,1)S(1)} %bitcast.47), custom_call_target="tpu_custom_call" | custom-call | tf_op jit(solution)/shard_map/pallas_call | solution.py:115
  115.0 0.6 while.10
  115.6 1.9 %collective-permute-start.2 = (bf16[4096,128]{1,0:T(8,128)(2,1)}, bf16[4096,128]{1,0:T(8,128)(2,1)S(1)}, u32[]{:S(2)}, u32[]{:S(2)}) collective-permute-start(bf16[4096,128]{1,0:T(8,128)(2,1)} %get-tuple-element.58.own_ref), channel_id=1, source_target_pairs={{0,4},{4,0},{1,5},{5,1},{2,6},{6,2},{3,7},{7,3},{8,12},{12,8},{9,1... | collective-permute-start | bytes 3145736 | tf_op jit(solution)/shard_map/ppermute | solution.py:221
  117.5 2.8 %collective-permute-done.2.far_ref = bf16[4096,128]{1,0:T(8,128)(2,1)S(1)} collective-permute-done((bf16[4096,128]{1,0:T(8,128)(2,1)}, bf16[4096,128]{1,0:T(8,128)(2,1)S(1)}, u32[]{:S(2)}, u32[]{:S(2)}) %collective-permute-start.2) | collective-permute-done | bytes 1048608 | tf_op jit(solution)/shard_map/ppermute | solution.py:221
  120.3 1.0 copy-done.5
  121.3 0.0 all-to-all-done.1
  121.3 1.1 copy-done.4
  122.4 1.2 copy-done.6
  123.7 10.5 %shard_map.94 = (f32[512,128]{1,0:T(8,128)S(1)}, f32[512,128]{1,0:T(8,128)S(1)}) custom-call(s32[1]{0:T(128)} %bitcast.6.core_ref, f32[1152,128]{1,0:T(8,128)} %bitcast.18.pre_ref, bf16[128,1792]{1,0:T(8,128)(2,1)S(1)} %copy-done.1, bf16[128,1792]{1,0:T(8,128)(2,1)S(1)} %copy-done.2, bf16[2752,128]{1,0:T(8,128)(2,1)S(1)} %copy-done.4, ...), custom_call_target="tpu_custom_call" | custom-call | tf_op jit(solution)/shard_map/pallas_call | solution.py:319
  134.2 0.0 copy-start.12
  134.2 2.0 %collective-permute-start.3 = (f32[512,128]{1,0:T(8,128)S(1)}, f32[512,128]{1,0:T(8,128)S(1)}, u32[]{:S(2)}, u32[]{:S(2)}) collective-permute-start(f32[512,128]{1,0:T(8,128)S(1)} %get-tuple-element.60), channel_id=1, source_target_pairs={{0,4},{4,0},{1,5},{5,1},{2,6},{6,2},{3,7},{7,3},{8,12},{12,8},{9,1... | collective-permute-start | bytes 786440 | tf_op jit(solution)/shard_map/ppermute | solution.py:221
  136.2 1.4 collective-permute-done.3
  137.7 12.9 %all_to_all.20 = f32[16,32,128]{2,1,0:T(8,128)S(1)} all-to-all(f32[16,32,128]{2,1,0:T(8,128)S(1)} %bitcast.52), channel_id=1, replica_groups=mesh['x'=4,'h'=4,'y'=4,'c'=2,'l'=4] {'x','y'}, dimensions={0} | all-to-all | bytes 524288 | tf_op jit(solution)/shard_map/all_to_all | solution.py:341
  150.6 21.2 %all_to_all.21 = f32[16,2,128]{2,1,0:T(2,128)S(1)} all-to-all(f32[16,2,128]{2,1,0:T(2,128)S(1)} %bitcast.57), channel_id=1, replica_groups=mesh['x'=4,'h'=4,'y'=4,'c'=2,'l'=4] {'l','h'}, dimensions={0} | all-to-all | bytes 32768 | tf_op jit(solution)/shard_map/all_to_all | solution.py:342
  171.8 0.1 reshape.71
  171.9 0.0 copy-done.12
  171.9 0.6 copy_multiply_fusion
  (13 shorter events, 0.2 us)
Async XLA Ops:
  0.0 4.9 %copy-start = (bf16[4096,128]{1,0:T(8,128)(2,1)S(1)}, bf16[4096,128]{1,0:T(8,128)(2,1)}, u32[]{:S(2)}) copy-start(bf16[4096,128]{1,0:T(8,128)(2,1)} %param.15) | copy-start | bytes 3145732
  0.0 2.0 %copy-start.7 = (bf16[1792,128]{1,0:T(8,128)(2,1)S(1)}, bf16[1792,128]{1,0:T(8,128)(2,1)}, u32[]{:S(2)}) copy-start(bf16[1792,128]{1,0:T(8,128)(2,1)} %down_ref.1) | copy-start | bytes 1376260
  0.0 2.0 %copy-start.8 = (bf16[64,128]{1,0:T(8,128)(2,1)S(1)}, bf16[64,128]{1,0:T(8,128)(2,1)}, u32[]{:S(2)}) copy-start(bf16[64,128]{1,0:T(8,128)(2,1)} %x_ref.1) | copy-start | bytes 49156
  1.6 3.3 %copy-start.13 = (s32[32]{0:T(128)S(1)}, s32[32]{0:T(128)}, u32[]{:S(2)}) copy-start(s32[32]{0:T(128)} %param.16) | copy-start | bytes 388
  2.0 5.9 %copy-start.11 = (s32[64,64]{1,0:T(8,128)S(1)}, s32[64,64]{1,0:T(8,128)}, u32[]{:S(2)}) copy-start(s32[64,64]{1,0:T(8,128)} %ids_ref.1) | copy-start | bytes 49156
  2.9 59.2 %collective-permute-start.1 = (bf16[2752,128]{1,0:T(8,128)(2,1)}, bf16[2752,128]{1,0:T(8,128)(2,1)S(1)}, u32[]{:S(2)}, u32[]{:S(2)}) collective-permute-start(bf16[2752,128]{1,0:T(8,128)(2,1)} %pad_maximum_fusion), channel_id=1, source_target_pairs={{0,4},{4,0},{1,5},{5,1},{2,6},{6,2},{3,7},{7,3},{8,12},{12,8},{9,1... | collective-permute-start | bytes 2113544 | tf_op jit(solution)/shard_map/ppermute | solution.py:221
  5.2 57.0 %copy-start.1 = (bf16[128,1792]{1,0:T(8,128)(2,1)S(1)}, bf16[128,1792]{1,0:T(8,128)(2,1)}, u32[]{:S(2)}) copy-start(bf16[128,1792]{1,0:T(8,128)(2,1)} %gate_ref.3) | copy-start | bytes 1376260
  5.2 57.0 %copy-start.2 = (bf16[128,1792]{1,0:T(8,128)(2,1)S(1)}, bf16[128,1792]{1,0:T(8,128)(2,1)}, u32[]{:S(2)}) copy-start(bf16[128,1792]{1,0:T(8,128)(2,1)} %up_ref.3) | copy-start | bytes 1376260
  5.2 9.5 %collective-permute-start = (bf16[32,128]{1,0:T(8,128)(2,1)S(1)}, bf16[32,128]{1,0:T(8,128)(2,1)S(1)}, u32[]{:S(2)}, u32[]{:S(2)}) collective-permute-start(bf16[32,128]{1,0:T(8,128)(2,1)S(1)} %convolution_convert_fusion), channel_id=1, source_target_pairs={{0,4},{4,0},{1,5},{5,1},{2,6},{6,2},{3,7},{7,3},{8,12},{12,8},{9,1... | collective-permute-start | bytes 24584 | tf_op jit(solution)/shard_map/ppermute | solution.py:221
  47.0 0.8 copy-start.9
  62.2 1.5 copy-start.3
  63.6 6.3 %copy-start.10 = (bf16[1664,128]{1,0:T(8,128)(2,1)S(1)}, bf16[1664,128]{1,0:T(8,128)(2,1)}, u32[]{:S(2)}) copy-start(bf16[1664,128]{1,0:T(8,128)(2,1)} %copy-done.9) | copy-start | bytes 1277956
  63.6 33.7 %all-to-all-start = ((f32[16,72,128]{2,1,0:T(8,128)}), f32[16,72,128]{2,1,0:T(8,128)}, u32[]{:S(2)}, u32[]{:S(2)}) async-start(f32[16,72,128]{2,1,0:T(8,128)} %bitcast.15), calls=%async_computation | async-start | bytes 1179648 | tf_op jit(solution)/shard_map/all_to_all | solution.py:291
  99.4 22.0 %all-to-all-start.1 = ((f32[16,72,128]{2,1,0:T(8,128)}), f32[16,72,128]{2,1,0:T(8,128)}, u32[]{:S(2)}, u32[]{:S(2)}) async-start(f32[16,72,128]{2,1,0:T(8,128)} %broadcast_in_dim.17), calls=%async_computation.1 | async-start | bytes 1179648 | tf_op jit(solution)/shard_map/all_to_all | solution.py:295
  115.6 4.8 %collective-permute-start.2 = (bf16[4096,128]{1,0:T(8,128)(2,1)}, bf16[4096,128]{1,0:T(8,128)(2,1)S(1)}, u32[]{:S(2)}, u32[]{:S(2)}) collective-permute-start(bf16[4096,128]{1,0:T(8,128)(2,1)} %get-tuple-element.58.own_ref), channel_id=1, source_target_pairs={{0,4},{4,0},{1,5},{5,1},{2,6},{6,2},{3,7},{7,3},{8,12},{12,8},{9,1... | collective-permute-start | bytes 3145736 | tf_op jit(solution)/shard_map/ppermute | solution.py:221
  120.3 1.0 copy-start.5
  121.3 1.1 copy-start.4
  122.4 1.2 copy-start.6
  134.2 37.7 %copy-start.12 = (f32[16,4]{0,1:T(4,128)S(1)}, f32[16,4]{0,1:T(4,128)}, u32[]{:S(2)}) copy-start(f32[16,4]{0,1:T(4,128)} %param.19) | copy-start | bytes 772
  134.2 3.4 %collective-permute-start.3 = (f32[512,128]{1,0:T(8,128)S(1)}, f32[512,128]{1,0:T(8,128)S(1)}, u32[]{:S(2)}, u32[]{:S(2)}) collective-permute-start(f32[512,128]{1,0:T(8,128)S(1)} %get-tuple-element.60), channel_id=1, source_target_pairs={{0,4},{4,0},{1,5},{5,1},{2,6},{6,2},{3,7},{7,3},{8,12},{12,8},{9,1... | collective-permute-start | bytes 786440 | tf_op jit(solution)/shard_map/ppermute | solution.py:221

commit v3 on v2

--- a/solution.py
+++ b/solution.py
@@ -11,7 +11,7 @@
 F32 = jnp.float32
 BF16 = jnp.bfloat16
 CAP = 352
-VMEM_LIMIT = 48 * 1024 * 1024
+MIB = 1024 * 1024
 
 
 def nt(a, b):
@@ -48,9 +48,7 @@
     start = where_ref[1] * CAP
     at = pos.astype(jnp.int32) - start
     here = jnp.logical_and(at >= 0, at < CAP)
-    late = (at >= CAP // 2).astype(jnp.int32)
-    slot = late * (owners * CAP // 2) + owner * (CAP // 2) + at - late * (CAP // 2)
-    slot = jnp.where(here, slot, -1)
+    slot = jnp.where(here, lax.bitwise_xor(owner, rank) * CAP + at, -1)
     slot_ref[...] = jnp.concatenate([slot[:, :slots], slot[:, slots:]], axis=0)
     rounds_ref[0] = lax.div(jnp.max(pos).astype(jnp.int32), CAP) + 1
     mine = jnp.where(owner == rank, pos - start.astype(F32), -1.0)
@@ -79,19 +77,20 @@
             pl.BlockSpec(memory_space=pltpu.VMEM),
             pl.BlockSpec(memory_space=pltpu.SMEM),
         ),
-        compiler_params=pltpu.CompilerParams(vmem_limit_bytes=VMEM_LIMIT),
+        compiler_params=pltpu.CompilerParams(vmem_limit_bytes=4 * MIB),
     )(jnp.stack([rank, turn]).astype(jnp.int32), ids)
     return slot, rows.reshape(-1), rounds[0]
 
 
-def expand_kernel(slot_ref, early_ref, late_ref, out_ref, table, block):
-    size = early_ref.shape[0]
+def expand_kernel(slot_ref, *refs):
+    parts, (out_ref, table, block) = refs[:-3], refs[-3:]
+    size = parts[0].shape[0]
     piece = 128
 
     def widen(i, carry):
-        at = pl.ds(pl.multiple_of(i * piece, piece), piece)
-        table[at, :] = early_ref[at, :].astype(F32)
-        table[pl.ds(pl.multiple_of(size + i * piece, piece), piece), :] = late_ref[at, :].astype(F32)
+        for p, ref in enumerate(parts):
+            to = pl.ds(pl.multiple_of(p * size + i * piece, piece), piece)
+            table[to, :] = ref[pl.ds(pl.multiple_of(i * piece, piece), piece), :].astype(F32)
         return carry
 
     lax.fori_loop(0, size // piece, widen, 0)
@@ -110,23 +109,30 @@
     lax.fori_loop(0, tokens, token, 0)
 
 
-def expand(slot, early, late):
-    size = early.shape[0]
+def expand(slot, parts):
+    size = parts[0].shape[0]
+    vmem = pl.BlockSpec(memory_space=pltpu.VMEM)
     return pl.pallas_call(
         expand_kernel,
         out_shape=jax.ShapeDtypeStruct((slot.shape[0] * slot.shape[1], 128), BF16),
-        in_specs=[
-            pl.BlockSpec(memory_space=pltpu.SMEM),
-            pl.BlockSpec(memory_space=pltpu.VMEM),
-            pl.BlockSpec(memory_space=pltpu.VMEM),
-        ],
-        out_specs=pl.BlockSpec(memory_space=pltpu.VMEM),
+        in_specs=[pl.BlockSpec(memory_space=pltpu.SMEM)] + [vmem] * len(parts),
+        out_specs=vmem,
         scratch_shapes=[
-            pltpu.VMEM((2 * size, 128), F32),
+            pltpu.VMEM((len(parts) * size, 128), F32),
             pltpu.VMEM((slot.shape[1], 128), F32),
         ],
-        compiler_params=pltpu.CompilerParams(vmem_limit_bytes=VMEM_LIMIT),
-    )(slot, early, late)
+        compiler_params=pltpu.CompilerParams(vmem_limit_bytes=12 * MIB),
+    )(slot, *parts)
+
+
+def exchange(value, axis):
+    return [value] + [
+        lax.ppermute(value, axis, [(i, i ^ m) for i in range(4)]) for m in range(1, 4)
+    ]
+
+
+def column_blocks(value):
+    return jnp.concatenate(exchange(value, "h"), axis=0)
 
 
 def forward_kernel(half, core_ref, x_ref, cot_ref, gate_ref, up_ref, down_ref, rec_ref, out_ref):
@@ -246,7 +252,11 @@
     local = feature_ids - rank * enc_rows
     picker = (local[:, None] == jnp.arange(enc_rows, dtype=jnp.int32)[None, :]).astype(BF16)
     chosen = jnp.dot(picker, down_encoder, preferred_element_type=F32).astype(BF16)
-    chosen_far = swap(chosen)
+    chosen, other = lax.optimization_barrier((chosen, other))
+    chosen = jnp.concatenate([chosen, swap(chosen)], axis=0)
+    cot = lax.all_to_all(
+        jnp.broadcast_to(chosen[None], (owners,) + chosen.shape), ("x", "h"), 0, 0, tiled=True
+    )
 
     def columns(w):
         part = lax.dynamic_slice(w, (0, other * half), (dblk, half))
@@ -264,14 +274,11 @@
     rec = swap(pack)
 
     dec_rows = up_decoder.shape[0]
+    latent_ids, chosen = lax.optimization_barrier((latent_ids, chosen))
     slot, rows, rounds = plan(latent_ids, rank, jnp.int32(0), owners, dec_rows)
     picked = jnp.take(up_decoder, rows, axis=0, mode="clip")
-    packet = lax.all_gather(jnp.concatenate([picked, chosen, chosen_far], axis=0), "h")
-
-    def spread(value):
-        return lax.all_gather(value, "x").reshape(owners * value.shape[1], 128)
-
-    cot = lax.all_gather(packet[:, CAP:, :], "x").reshape(owners, 2 * features, 128)
+    column = column_blocks(picked)
+
     cot = jnp.sum(cot.astype(F32), axis=0).astype(BF16)
     cot = jnp.concatenate([cot[:features], cot[features:]], axis=1)
 
@@ -279,24 +286,23 @@
     padded = -(-used // 128) * 128
     vmem = pl.BlockSpec(memory_space=pltpu.VMEM)
     smem = pl.BlockSpec(memory_space=pltpu.SMEM)
-    params = pltpu.CompilerParams(vmem_limit_bytes=VMEM_LIMIT)
     part = pl.pallas_call(
         functools.partial(forward_kernel, half),
         out_shape=jax.ShapeDtypeStruct((padded, 128), F32),
         in_specs=[smem] + [vmem] * 6,
         out_specs=vmem,
-        compiler_params=params,
+        compiler_params=pltpu.CompilerParams(vmem_limit_bytes=8 * MIB),
     )(core_arg, mlp_input, cot, gate_weight, up_weight, down_weight, rec)
-    part, packet = lax.optimization_barrier((part, packet))
+    part, column = lax.optimization_barrier((part, column))
     part = lax.all_to_all(part.reshape(16, padded // 16, 128), ("y", "l"), 0, 0, tiled=True)
-    early, late = spread(packet[:, : CAP // 2, :]), spread(packet[:, CAP // 2 : CAP, :])
+    parts = exchange(column, "x")
     part = jnp.sum(part, axis=0)
-    part, early, late = lax.optimization_barrier((part, early, late))
+    part, slot = lax.optimization_barrier((part, slot))
     pre = lax.all_to_all(
         jnp.broadcast_to(part[None], (16,) + part.shape), ("y", "l"), 0, 0, tiled=True
     ).reshape(padded, 128)
 
-    dec = expand(slot, early, late)
+    dec = expand(slot, parts)
 
     def more(carry):
         return carry[0] < rounds
@@ -304,8 +310,8 @@
     def another(carry):
         turn, have = carry
         slot_now, rows_now, _ = plan(latent_ids, rank, turn, owners, dec_rows)
-        got = lax.all_gather(jnp.take(up_decoder, rows_now, axis=0, mode="clip"), "h")
-        now = expand(slot_now, spread(got[:, : CAP // 2, :]), spread(got[:, CAP // 2 :, :]))
+        taken = jnp.take(up_decoder, rows_now, axis=0, mode="clip")
+        now = expand(slot_now, exchange(column_blocks(taken), "x"))
         here = slot_now.reshape(tokens, slots // 4, 2, 2).transpose(0, 3, 1, 2).reshape(-1, 1)
         return turn + 1, jnp.where(here >= 0, now, have)
 
@@ -334,7 +340,7 @@
             pltpu.VMEM((2 * dblk, 2 * half), BF16),
             pltpu.VMEM((features * tokens // steps, 2 * half), BF16),
         ],
-        compiler_params=params,
+        compiler_params=pltpu.CompilerParams(vmem_limit_bytes=20 * MIB),
     )(core_arg, pre, gate_weight, up_weight, rec, dec, dec_far)
 
     total = mine + swap(theirs)

time: 173 us -> 169 us (0.977)
  blocking collectives: 106 us -> 30.5 us
  starting transfers between devices: 22.2 us -> 70.8 us
  waiting for transfers between devices: 4.22 us -> 26.5 us
    all_gather x4 -> x0, blocking collectives: 72.1 us -> none  [the longest x1 31.4 us: on_device(): lax.all_gather(jnp.concatenate([picked, chosen, chosen_far], axis=0), 'h')]
    ppermute x0 -> x6, starting transfers between devices: none -> 27.4 us  [exchange(): lax.ppermute(value, axis, [(i, i ^ m) for i in range(4)])]
    ppermute x0 -> x6, waiting for transfers between devices: none -> 18.6 us  [exchange(): lax.ppermute(value, axis, [(i, i ^ m) for i in range(4)])]
    all_to_all x0 -> x1, starting transfers between devices: none -> 17.7 us  [on_device(): lax.all_to_all(jnp.broadcast_to(chosen[None], (owners,) + chosen.shape),...]
    all_to_all x1, starting transfers between devices: 6.34 us -> 11 us  [on_device(): lax.all_to_all(part.reshape(16, padded // 16, 128), ('y', 'l'), 0, 0, til...]
    all_to_all x1, waiting for transfers between devices: 0.01 us -> 3.64 us  [on_device(): lax.all_to_all(part.reshape(16, padded // 16, 128), ('y', 'l'), 0, 0, til...]
    all_to_all x1, blocking collectives: 21.2 us -> 18.6 us  [on_device(): lax.all_to_all(total.reshape(16, 2, 128), ('l', 'h'), 0, 0, tiled=True)]
    unnamed x30 -> x27, local copies, waits for them, and re-layouts: 4.51 us -> 5.44 us
  transfers between devices with their start and end apart: 6 -> 13, of which waited for: 2 -> 6; matrix products, arithmetic and copies ran while one was open for 3% -> 5% of each run, Pallas kernels for 7% -> 7%
where the time goes in v3:
time: 169 us; the launch traced here: 168 us
  starting transfers between devices  70.8 us (42%)
  blocking collectives  30.5 us (18%)
  waiting for transfers between devices  26.5 us (16%)
  Pallas kernels  23.4 us (14%)
  local copies, waits for them, and re-layouts  11.6 us (7%)
  other arithmetic  3.75 us (2%)
    ppermute x6, starting transfers between devices, exchange(): lax.ppermute(value, axis, [(i, i ^ m) for i in range(4)])  27.4 us
    ppermute x6, waiting for transfers between devices, exchange(): lax.ppermute(value, axis, [(i, i ^ m) for i in range(4)])  18.6 us
    all_to_all x1, blocking collectives, on_device(): lax.all_to_all(total.reshape(16, 2, 128), ('l', 'h'), 0, 0, tiled=True)  18.6 us
    all_to_all x1, starting transfers between devices, on_device(): lax.all_to_all(jnp.broadcast_to(chosen[None], (owners,) + chosen.shape),...  17.7 us
    all_to_all x1, blocking collectives, on_device(): lax.all_to_all(total.reshape(16, 32, 128), ('x', 'y'), 0, 0, tiled=True)  11.9 us
    all_to_all x1, starting transfers between devices, on_device(): lax.all_to_all(part.reshape(16, padded // 16, 128), ('y', 'l'), 0, 0, til...  11 us
    pallas_call x1, Pallas kernels, on_device(): pl.pallas_call(functools.partial(main_kernel, half, tokens, features), gr...  10.5 us
    pallas_call x1, Pallas kernels, expand(): pl.pallas_call(expand_kernel, out_shape=jax.ShapeDtypeStruct((slot.shape[...  8.19 us
  transfers between devices with their start and end apart: 13, of which 6 were waited for; matrix products, arithmetic and copies ran while one was open for 5% of the time, Pallas kernels for 7%

profile of v3, /device:TPU:8, one launch (start us, length us, event | category | flops | bytes accessed | tf_op | source)
XLA Modules:
  0.0 167.9 jit_solution(13668309649557228100)
XLA Ops:
  0.0 0.7 broadcast_subtract_fusion
  0.8 0.5 copy-done
  1.2 0.3 convolution_convert_fusion
  1.6 1.9 %collective-permute-start.6 = (bf16[32,128]{1,0:T(8,128)(2,1)S(1)}, bf16[32,128]{1,0:T(8,128)(2,1)S(1)}, u32[]{:S(2)}, u32[]{:S(2)}) collective-permute-start(bf16[32,128]{1,0:T(8,128)(2,1)S(1)} %convolution_convert_fusion), channel_id=1, source_target_pairs={{0,4},{4,0},{1,5},{5,1},{2,6},{6,2},{3,7},{7,3},{8,12},{12,8},{9,1... | collective-permute-start | bytes 24584 | tf_op jit(solution)/shard_map/ppermute | solution.py:227
  3.5 1.1 constant_dynamic-slice_fusion.1
  4.6 0.0 copy-start.7
  4.6 0.2 copy.33
  4.8 0.0 copy-start.9
  4.8 0.2 copy.27
  5.0 0.2 copy.34
  5.2 0.2 copy.29
  5.3 0.0 copy-start.12
  5.4 0.0 collective-permute-done.6
  5.4 0.8 broadcast_in_dim.16
  6.1 17.7 %all-to-all-start = ((bf16[16,64,128]{2,1,0:T(8,128)(2,1)}), bf16[16,64,128]{2,1,0:T(8,128)(2,1)S(1)}, u32[]{:S(2)}, u32[]{:S(2)}) async-start(bf16[16,64,128]{2,1,0:T(8,128)(2,1)} %broadcast_in_dim.16), calls=%async_computation | async-start | bytes 524288 | tf_op jit(solution)/shard_map/all_to_all | solution.py:257
  23.8 0.0 copy-done.7
  23.9 0.0 copy-start.1
  23.9 0.0 copy-start.2
  23.9 0.9 pad_maximum_fusion
  24.8 2.1 %collective-permute-start.7 = (bf16[2752,128]{1,0:T(8,128)(2,1)}, bf16[2752,128]{1,0:T(8,128)(2,1)S(1)}, u32[]{:S(2)}, u32[]{:S(2)}) collective-permute-start(bf16[2752,128]{1,0:T(8,128)(2,1)} %pad_maximum_fusion), channel_id=1, source_target_pairs={{0,4},{4,0},{1,5},{5,1},{2,6},{6,2},{3,7},{7,3},{8,12},{12,8},{9,1... | collective-permute-start | bytes 2113544 | tf_op jit(solution)/shard_map/ppermute | solution.py:227
  26.9 0.1 pad_add_fusion.1.where_ref
  27.0 3.2 %shard_map.92 = (s32[64,64]{1,0:T(8,128)S(1)}, s32[352,1]{1,0:T(8,128)S(1)}, s32[1]{0:T(128)}) custom-call(s32[2]{0:T(128)S(1)} %pad_add_fusion.1.where_ref, s32[64,64]{1,0:T(8,128)S(1)} %copy-done.12), custom_call_target="tpu_custom_call" | custom-call | tf_op jit(solution)/shard_map/pallas_call | solution.py:64
  30.2 0.1 reduce.2
  30.4 3.0 %gather_fusion.1 = bf16[352,128]{1,0:T(8,128)(2,1)S(1)} fusion(bf16[8192,128]{1,0:T(8,128)(2,1)} %param.17, s32[1024]{0:T(1024)S(1)} %pad_clamp_fusion.1), kind=kCustom, calls=%fused_computation.1 | custom fusion | bytes 181632 | tf_op jit(solution)/shard_map/jit(_take)/gather | solution.py:279
  33.4 7.5 %collective-permute-start.10 = (bf16[352,128]{1,0:T(8,128)(2,1)S(1)}, bf16[352,128]{1,0:T(8,128)(2,1)S(1)}, u32[]{:S(2)}, u32[]{:S(2)}) collective-permute-start(bf16[352,128]{1,0:T(8,128)(2,1)S(1)} %gather_fusion.1), channel_id=1, source_target_pairs={{0,96},{32,64},{64,32},{96,0},{1,97},{33,65},{65,33},{97,1},{2,98}... | collective-permute-start | bytes 270344 | tf_op jit(solution)/shard_map/ppermute | solution.py:130
  40.9 7.3 %collective-permute-start.8 = (bf16[352,128]{1,0:T(8,128)(2,1)S(1)}, bf16[352,128]{1,0:T(8,128)(2,1)S(1)}, u32[]{:S(2)}, u32[]{:S(2)}) collective-permute-start(bf16[352,128]{1,0:T(8,128)(2,1)S(1)} %gather_fusion.1), channel_id=1, source_target_pairs={{0,32},{32,0},{64,96},{96,64},{1,33},{33,1},{65,97},{97,65},{2,34}... | collective-permute-start | bytes 270344 | tf_op jit(solution)/shard_map/ppermute | solution.py:130
  48.2 2.2 %collective-permute-start.9 = (bf16[352,128]{1,0:T(8,128)(2,1)S(1)}, bf16[352,128]{1,0:T(8,128)(2,1)S(1)}, u32[]{:S(2)}, u32[]{:S(2)}) collective-permute-start(bf16[352,128]{1,0:T(8,128)(2,1)S(1)} %gather_fusion.1), channel_id=1, source_target_pairs={{0,64},{32,96},{64,0},{96,32},{1,65},{33,97},{65,1},{97,33},{2,66}... | collective-permute-start | bytes 270344 | tf_op jit(solution)/shard_map/ppermute | solution.py:130
  50.4 0.0 collective-permute-done.10
  50.4 4.9 %collective-permute-done.8 = bf16[352,128]{1,0:T(8,128)(2,1)S(1)} collective-permute-done((bf16[352,128]{1,0:T(8,128)(2,1)S(1)}, bf16[352,128]{1,0:T(8,128)(2,1)S(1)}, u32[]{:S(2)}, u32[]{:S(2)}) %collective-permute-start.8) | collective-permute-done | bytes 90144 | tf_op jit(solution)/shard_map/ppermute | solution.py:130
  55.4 8.5 %collective-permute-done.9 = bf16[352,128]{1,0:T(8,128)(2,1)S(1)} collective-permute-done((bf16[352,128]{1,0:T(8,128)(2,1)S(1)}, bf16[352,128]{1,0:T(8,128)(2,1)S(1)}, u32[]{:S(2)}, u32[]{:S(2)}) %collective-permute-start.9) | collective-permute-done | bytes 90144 | tf_op jit(solution)/shard_map/ppermute | solution.py:130
  63.9 0.0 all-to-all-done
  64.0 0.0 collective-permute-done.7.rec_ref
  64.0 0.0 copy-start.8
  64.0 1.3 copy-done.8
  65.3 1.4 shard_map.91
  66.7 0.0 copy-done.3
  66.7 11.0 %all-to-all-start.1 = ((f32[16,72,128]{2,1,0:T(8,128)}), f32[16,72,128]{2,1,0:T(8,128)}, u32[]{:S(2)}, u32[]{:S(2)}) async-start(f32[16,72,128]{2,1,0:T(8,128)} %bitcast.11), calls=%async_computation.1 | async-start | bytes 1179648 | tf_op jit(solution)/shard_map/all_to_all | solution.py:297
  77.8 3.4 %collective-permute-start.11 = (bf16[1408,128]{1,0:T(8,128)(2,1)S(1)}, bf16[1408,128]{1,0:T(8,128)(2,1)S(1)}, u32[]{:S(2)}, u32[]{:S(2)}) collective-permute-start(bf16[1408,128]{1,0:T(8,128)(2,1)S(1)} %pad_maximum_fusion.1.refs_0_), channel_id=1, source_target_pairs={{0,128},{128,0},{256,384},{384,256},{1,129},{129,1},{257,385},{385... | collective-permute-start | bytes 1081352 | tf_op jit(solution)/shard_map/ppermute | solution.py:130
  81.1 4.6 %collective-permute-start.12 = (bf16[1408,128]{1,0:T(8,128)(2,1)S(1)}, bf16[1408,128]{1,0:T(8,128)(2,1)S(1)}, u32[]{:S(2)}, u32[]{:S(2)}) collective-permute-start(bf16[1408,128]{1,0:T(8,128)(2,1)S(1)} %pad_maximum_fusion.1.refs_0_), channel_id=1, source_target_pairs={{0,256},{128,384},{256,0},{384,128},{1,257},{129,385},{257,1},{385... | collective-permute-start | bytes 1081352 | tf_op jit(solution)/shard_map/ppermute | solution.py:130
  85.7 2.5 %collective-permute-start.13 = (bf16[1408,128]{1,0:T(8,128)(2,1)S(1)}, bf16[1408,128]{1,0:T(8,128)(2,1)}, u32[]{:S(2)}, u32[]{:S(2)}) collective-permute-start(bf16[1408,128]{1,0:T(8,128)(2,1)S(1)} %pad_maximum_fusion.1.refs_0_), channel_id=1, source_target_pairs={{0,384},{128,256},{256,128},{384,0},{1,385},{129,257},{257,129},{3... | collective-permute-start | bytes 1081352 | tf_op jit(solution)/shard_map/ppermute | solution.py:130
  88.2 3.6 %all-to-all-done.1 = f32[16,72,128]{2,1,0:T(8,128)} async-done(((f32[16,72,128]{2,1,0:T(8,128)}), f32[16,72,128]{2,1,0:T(8,128)}, u32[]{:S(2)}, u32[]{:S(2)}) %all-to-all-start.1) | async-done | bytes 589856 | tf_op jit(solution)/shard_map/all_to_all | solution.py:297
  91.9 1.1 reduce_sum.40
  93.0 0.9 broadcast_in_dim.17
  93.8 6.7 %all-to-all-start.2 = ((f32[16,72,128]{2,1,0:T(8,128)}), f32[16,72,128]{2,1,0:T(8,128)}, u32[]{:S(2)}, u32[]{:S(2)}) async-start(f32[16,72,128]{2,1,0:T(8,128)} %broadcast_in_dim.17), calls=%async_computation.2 | async-start | bytes 1179648 | tf_op jit(solution)/shard_map/all_to_all | solution.py:301
  100.5 0.0 collective-permute-done.11.refs_1_
  100.5 0.0 collective-permute-done.12.refs_2_
  100.5 5.2 %collective-permute-done.13.refs_3_ = bf16[1408,128]{1,0:T(8,128)(2,1)} collective-permute-done((bf16[1408,128]{1,0:T(8,128)(2,1)S(1)}, bf16[1408,128]{1,0:T(8,128)(2,1)}, u32[]{:S(2)}, u32[]{:S(2)}) %collective-permute-start.13) | collective-permute-done | bytes 360480 | tf_op jit(solution)/shard_map/ppermute | solution.py:130
  105.7 8.2 %shard_map.93 = bf16[4096,128]{1,0:T(8,128)(2,1)} custom-call(s32[64,64]{1,0:T(8,128)S(1)} %get-tuple-element.59.slot_ref, bf16[1408,128]{1,0:T(8,128)(2,1)S(1)} %pad_maximum_fusion.1.refs_0_, bf16[1408,128]{1,0:T(8,128)(2,1)S(1)} %collective-permute-done.11.refs_1_, bf16[1408,128]{1,0:T(8,128)(2,1)S(1)} %collective-permute-done.12.refs_2_, ...), custom_call_target="tpu_custom_call" | custom-call | tf_op jit(solution)/shard_map/pallas_call | solution.py:115
  113.9 0.6 while.10
  114.5 1.9 %collective-permute-start.14 = (bf16[4096,128]{1,0:T(8,128)(2,1)}, bf16[4096,128]{1,0:T(8,128)(2,1)S(1)}, u32[]{:S(2)}, u32[]{:S(2)}) collective-permute-start(bf16[4096,128]{1,0:T(8,128)(2,1)} %get-tuple-element.62.own_ref), channel_id=1, source_target_pairs={{0,4},{4,0},{1,5},{5,1},{2,6},{6,2},{3,7},{7,3},{8,12},{12,8},{9,1... | collective-permute-start | bytes 3145736 | tf_op jit(solution)/shard_map/ppermute | solution.py:227
  116.5 2.8 %collective-permute-done.14.far_ref = bf16[4096,128]{1,0:T(8,128)(2,1)S(1)} collective-permute-done((bf16[4096,128]{1,0:T(8,128)(2,1)}, bf16[4096,128]{1,0:T(8,128)(2,1)S(1)}, u32[]{:S(2)}, u32[]{:S(2)}) %collective-permute-start.14) | collective-permute-done | bytes 1048608 | tf_op jit(solution)/shard_map/ppermute | solution.py:227
  119.3 1.0 copy-done.5
  120.3 0.0 all-to-all-done.2
  120.3 1.1 copy-done.4
  121.4 1.2 copy-done.6
  122.6 10.5 %shard_map.94 = (f32[512,128]{1,0:T(8,128)S(1)}, f32[512,128]{1,0:T(8,128)S(1)}) custom-call(s32[1]{0:T(128)} %bitcast.3.core_ref, f32[1152,128]{1,0:T(8,128)} %bitcast.12.pre_ref, bf16[128,1792]{1,0:T(8,128)(2,1)S(1)} %copy-done.1, bf16[128,1792]{1,0:T(8,128)(2,1)S(1)} %copy-done.2, bf16[2752,128]{1,0:T(8,128)(2,1)S(1)} %copy-done.4, ...), custom_call_target="tpu_custom_call" | custom-call | tf_op jit(solution)/shard_map/pallas_call | solution.py:325
  133.1 0.0 copy-start.13
  133.1 2.0 %collective-permute-start.15 = (f32[512,128]{1,0:T(8,128)S(1)}, f32[512,128]{1,0:T(8,128)S(1)}, u32[]{:S(2)}, u32[]{:S(2)}) collective-permute-start(f32[512,128]{1,0:T(8,128)S(1)} %get-tuple-element.64), channel_id=1, source_target_pairs={{0,4},{4,0},{1,5},{5,1},{2,6},{6,2},{3,7},{7,3},{8,12},{12,8},{9,1... | collective-permute-start | bytes 786440 | tf_op jit(solution)/shard_map/ppermute | solution.py:227
  135.2 1.4 collective-permute-done.15
  136.6 11.9 %all_to_all.25 = f32[16,32,128]{2,1,0:T(8,128)S(1)} all-to-all(f32[16,32,128]{2,1,0:T(8,128)S(1)} %bitcast.33), channel_id=1, replica_groups=mesh['x'=4,'h'=4,'y'=4,'c'=2,'l'=4] {'x','y'}, dimensions={0} | all-to-all | bytes 524288 | tf_op jit(solution)/shard_map/all_to_all | solution.py:347
  148.6 18.6 %all_to_all.26 = f32[16,2,128]{2,1,0:T(2,128)S(1)} all-to-all(f32[16,2,128]{2,1,0:T(2,128)S(1)} %bitcast.38), channel_id=1, replica_groups=mesh['x'=4,'h'=4,'y'=4,'c'=2,'l'=4] {'l','h'}, dimensions={0} | all-to-all | bytes 32768 | tf_op jit(solution)/shard_map/all_to_all | solution.py:348
  167.2 0.1 reshape.57
  167.3 0.0 copy-done.13
  167.3 0.6 copy_multiply_fusion
  (20 shorter events, 0.2 us)
Async XLA Ops:
  0.0 1.2 copy-start
  1.6 3.8 %collective-permute-start.6 = (bf16[32,128]{1,0:T(8,128)(2,1)S(1)}, bf16[32,128]{1,0:T(8,128)(2,1)S(1)}, u32[]{:S(2)}, u32[]{:S(2)}) collective-permute-start(bf16[32,128]{1,0:T(8,128)(2,1)S(1)} %convolution_convert_fusion), channel_id=1, source_target_pairs={{0,4},{4,0},{1,5},{5,1},{2,6},{6,2},{3,7},{7,3},{8,12},{12,8},{9,1... | collective-permute-start | bytes 24584 | tf_op jit(solution)/shard_map/ppermute | solution.py:227
  4.6 19.2 %copy-start.7 = (bf16[1792,128]{1,0:T(8,128)(2,1)S(1)}, bf16[1792,128]{1,0:T(8,128)(2,1)}, u32[]{:S(2)}) copy-start(bf16[1792,128]{1,0:T(8,128)(2,1)} %down_ref.1) | copy-start | bytes 1376260
  4.8 19.0 %copy-start.9 = (bf16[64,128]{1,0:T(8,128)(2,1)S(1)}, bf16[64,128]{1,0:T(8,128)(2,1)}, u32[]{:S(2)}) copy-start(bf16[64,128]{1,0:T(8,128)(2,1)} %x_ref.1) | copy-start | bytes 49156
  5.3 21.6 %copy-start.12 = (s32[64,64]{1,0:T(8,128)S(1)}, s32[64,64]{1,0:T(8,128)}, u32[]{:S(2)}) copy-start(s32[64,64]{1,0:T(8,128)} %ids_ref) | copy-start | bytes 49156
  6.1 57.8 %all-to-all-start = ((bf16[16,64,128]{2,1,0:T(8,128)(2,1)}), bf16[16,64,128]{2,1,0:T(8,128)(2,1)S(1)}, u32[]{:S(2)}, u32[]{:S(2)}) async-start(bf16[16,64,128]{2,1,0:T(8,128)(2,1)} %broadcast_in_dim.16), calls=%async_computation | async-start | bytes 524288 | tf_op jit(solution)/shard_map/all_to_all | solution.py:257
  23.9 40.2 %copy-start.1 = (bf16[128,1792]{1,0:T(8,128)(2,1)S(1)}, bf16[128,1792]{1,0:T(8,128)(2,1)}, u32[]{:S(2)}) copy-start(bf16[128,1792]{1,0:T(8,128)(2,1)} %gate_ref.3) | copy-start | bytes 1376260
  23.9 40.2 %copy-start.2 = (bf16[128,1792]{1,0:T(8,128)(2,1)S(1)}, bf16[128,1792]{1,0:T(8,128)(2,1)}, u32[]{:S(2)}) copy-start(bf16[128,1792]{1,0:T(8,128)(2,1)} %up_ref.3) | copy-start | bytes 1376260
  24.8 39.2 %collective-permute-start.7 = (bf16[2752,128]{1,0:T(8,128)(2,1)}, bf16[2752,128]{1,0:T(8,128)(2,1)S(1)}, u32[]{:S(2)}, u32[]{:S(2)}) collective-permute-start(bf16[2752,128]{1,0:T(8,128)(2,1)} %pad_maximum_fusion), channel_id=1, source_target_pairs={{0,4},{4,0},{1,5},{5,1},{2,6},{6,2},{3,7},{7,3},{8,12},{12,8},{9,1... | collective-permute-start | bytes 2113544 | tf_op jit(solution)/shard_map/ppermute | solution.py:227
  33.4 17.1 %collective-permute-start.10 = (bf16[352,128]{1,0:T(8,128)(2,1)S(1)}, bf16[352,128]{1,0:T(8,128)(2,1)S(1)}, u32[]{:S(2)}, u32[]{:S(2)}) collective-permute-start(bf16[352,128]{1,0:T(8,128)(2,1)S(1)} %gather_fusion.1), channel_id=1, source_target_pairs={{0,96},{32,64},{64,32},{96,0},{1,97},{33,65},{65,33},{97,1},{2,98}... | collective-permute-start | bytes 270344 | tf_op jit(solution)/shard_map/ppermute | solution.py:130
  40.9 14.4 %collective-permute-start.8 = (bf16[352,128]{1,0:T(8,128)(2,1)S(1)}, bf16[352,128]{1,0:T(8,128)(2,1)S(1)}, u32[]{:S(2)}, u32[]{:S(2)}) collective-permute-start(bf16[352,128]{1,0:T(8,128)(2,1)S(1)} %gather_fusion.1), channel_id=1, source_target_pairs={{0,32},{32,0},{64,96},{96,64},{1,33},{33,1},{65,97},{97,65},{2,34}... | collective-permute-start | bytes 270344 | tf_op jit(solution)/shard_map/ppermute | solution.py:130
  48.2 15.7 %collective-permute-start.9 = (bf16[352,128]{1,0:T(8,128)(2,1)S(1)}, bf16[352,128]{1,0:T(8,128)(2,1)S(1)}, u32[]{:S(2)}, u32[]{:S(2)}) collective-permute-start(bf16[352,128]{1,0:T(8,128)(2,1)S(1)} %gather_fusion.1), channel_id=1, source_target_pairs={{0,64},{32,96},{64,0},{96,32},{1,65},{33,97},{65,1},{97,33},{2,66}... | collective-permute-start | bytes 270344 | tf_op jit(solution)/shard_map/ppermute | solution.py:130
  64.0 2.7 %copy-start.3 = (bf16[2752,128]{1,0:T(8,128)(2,1)}, bf16[2752,128]{1,0:T(8,128)(2,1)S(1)}, u32[]{:S(2)}) copy-start(bf16[2752,128]{1,0:T(8,128)(2,1)S(1)} %collective-permute-done.7.rec_ref) | copy-start | bytes 2113540
  64.0 1.3 copy-start.8
  66.7 25.1 %all-to-all-start.1 = ((f32[16,72,128]{2,1,0:T(8,128)}), f32[16,72,128]{2,1,0:T(8,128)}, u32[]{:S(2)}, u32[]{:S(2)}) async-start(f32[16,72,128]{2,1,0:T(8,128)} %bitcast.11), calls=%async_computation.1 | async-start | bytes 1179648 | tf_op jit(solution)/shard_map/all_to_all | solution.py:297
  77.8 22.7 %collective-permute-start.11 = (bf16[1408,128]{1,0:T(8,128)(2,1)S(1)}, bf16[1408,128]{1,0:T(8,128)(2,1)S(1)}, u32[]{:S(2)}, u32[]{:S(2)}) collective-permute-start(bf16[1408,128]{1,0:T(8,128)(2,1)S(1)} %pad_maximum_fusion.1.refs_0_), channel_id=1, source_target_pairs={{0,128},{128,0},{256,384},{384,256},{1,129},{129,1},{257,385},{385... | collective-permute-start | bytes 1081352 | tf_op jit(solution)/shard_map/ppermute | solution.py:130
  81.1 19.4 %collective-permute-start.12 = (bf16[1408,128]{1,0:T(8,128)(2,1)S(1)}, bf16[1408,128]{1,0:T(8,128)(2,1)S(1)}, u32[]{:S(2)}, u32[]{:S(2)}) collective-permute-start(bf16[1408,128]{1,0:T(8,128)(2,1)S(1)} %pad_maximum_fusion.1.refs_0_), channel_id=1, source_target_pairs={{0,256},{128,384},{256,0},{384,128},{1,257},{129,385},{257,1},{385... | collective-permute-start | bytes 1081352 | tf_op jit(solution)/shard_map/ppermute | solution.py:130
  85.7 20.0 %collective-permute-start.13 = (bf16[1408,128]{1,0:T(8,128)(2,1)S(1)}, bf16[1408,128]{1,0:T(8,128)(2,1)}, u32[]{:S(2)}, u32[]{:S(2)}) collective-permute-start(bf16[1408,128]{1,0:T(8,128)(2,1)S(1)} %pad_maximum_fusion.1.refs_0_), channel_id=1, source_target_pairs={{0,384},{128,256},{256,128},{384,0},{1,385},{129,257},{257,129},{3... | collective-permute-start | bytes 1081352 | tf_op jit(solution)/shard_map/ppermute | solution.py:130
  93.8 26.5 %all-to-all-start.2 = ((f32[16,72,128]{2,1,0:T(8,128)}), f32[16,72,128]{2,1,0:T(8,128)}, u32[]{:S(2)}, u32[]{:S(2)}) async-start(f32[16,72,128]{2,1,0:T(8,128)} %broadcast_in_dim.17), calls=%async_computation.2 | async-start | bytes 1179648 | tf_op jit(solution)/shard_map/all_to_all | solution.py:301
  114.5 4.8 %collective-permute-start.14 = (bf16[4096,128]{1,0:T(8,128)(2,1)}, bf16[4096,128]{1,0:T(8,128)(2,1)S(1)}, u32[]{:S(2)}, u32[]{:S(2)}) collective-permute-start(bf16[4096,128]{1,0:T(8,128)(2,1)} %get-tuple-element.62.own_ref), channel_id=1, source_target_pairs={{0,4},{4,0},{1,5},{5,1},{2,6},{6,2},{3,7},{7,3},{8,12},{12,8},{9,1... | collective-permute-start | bytes 3145736 | tf_op jit(solution)/shard_map/ppermute | solution.py:227
  119.3 1.0 copy-start.5
  120.3 1.1 copy-start.4
  121.4 1.2 copy-start.6
  133.1 34.2 %copy-start.13 = (f32[16,4]{0,1:T(4,128)S(1)}, f32[16,4]{0,1:T(4,128)}, u32[]{:S(2)}) copy-start(f32[16,4]{0,1:T(4,128)} %param.19) | copy-start | bytes 772
  133.1 3.4 %collective-permute-start.15 = (f32[512,128]{1,0:T(8,128)S(1)}, f32[512,128]{1,0:T(8,128)S(1)}, u32[]{:S(2)}, u32[]{:S(2)}) collective-permute-start(f32[512,128]{1,0:T(8,128)S(1)} %get-tuple-element.64), channel_id=1, source_target_pairs={{0,4},{4,0},{1,5},{5,1},{2,6},{6,2},{3,7},{7,3},{8,12},{12,8},{9,1... | collective-permute-start | bytes 786440 | tf_op jit(solution)/shard_map/ppermute | solution.py:227

commit v4 on v3

--- a/solution.py
+++ b/solution.py
@@ -131,8 +131,8 @@
     ]
 
 
-def column_blocks(value):
-    return jnp.concatenate(exchange(value, "h"), axis=0)
+def after(value, other):
+    return lax.optimization_barrier((value, other))[0]
 
 
 def forward_kernel(half, core_ref, x_ref, cot_ref, gate_ref, up_ref, down_ref, rec_ref, out_ref):
@@ -252,7 +252,7 @@
     local = feature_ids - rank * enc_rows
     picker = (local[:, None] == jnp.arange(enc_rows, dtype=jnp.int32)[None, :]).astype(BF16)
     chosen = jnp.dot(picker, down_encoder, preferred_element_type=F32).astype(BF16)
-    chosen, other = lax.optimization_barrier((chosen, other))
+    other = after(other, chosen)
     chosen = jnp.concatenate([chosen, swap(chosen)], axis=0)
     cot = lax.all_to_all(
         jnp.broadcast_to(chosen[None], (owners,) + chosen.shape), ("x", "h"), 0, 0, tiled=True
@@ -274,12 +274,12 @@
     rec = swap(pack)
 
     dec_rows = up_decoder.shape[0]
-    latent_ids, chosen = lax.optimization_barrier((latent_ids, chosen))
+    latent_ids = after(latent_ids, chosen)
     slot, rows, rounds = plan(latent_ids, rank, jnp.int32(0), owners, dec_rows)
     picked = jnp.take(up_decoder, rows, axis=0, mode="clip")
-    column = column_blocks(picked)
-
-    cot = jnp.sum(cot.astype(F32), axis=0).astype(BF16)
+    column = exchange(picked, "h")
+
+    cot = jnp.sum(after(cot, column[1]).astype(F32), axis=0).astype(BF16)
     cot = jnp.concatenate([cot[:features], cot[features:]], axis=1)
 
     used = (half // 128) * (2 * tokens + features)
@@ -293,11 +293,11 @@
         out_specs=vmem,
         compiler_params=pltpu.CompilerParams(vmem_limit_bytes=8 * MIB),
     )(core_arg, mlp_input, cot, gate_weight, up_weight, down_weight, rec)
-    part, column = lax.optimization_barrier((part, column))
+    column = after(jnp.concatenate(column, axis=0), part)
     part = lax.all_to_all(part.reshape(16, padded // 16, 128), ("y", "l"), 0, 0, tiled=True)
     parts = exchange(column, "x")
     part = jnp.sum(part, axis=0)
-    part, slot = lax.optimization_barrier((part, slot))
+    slot = after(slot, part)
     pre = lax.all_to_all(
         jnp.broadcast_to(part[None], (16,) + part.shape), ("y", "l"), 0, 0, tiled=True
     ).reshape(padded, 128)
@@ -311,7 +311,7 @@
         turn, have = carry
         slot_now, rows_now, _ = plan(latent_ids, rank, turn, owners, dec_rows)
         taken = jnp.take(up_decoder, rows_now, axis=0, mode="clip")
-        now = expand(slot_now, exchange(column_blocks(taken), "x"))
+        now = expand(slot_now, exchange(jnp.concatenate(exchange(taken, "h")), "x"))
         here = slot_now.reshape(tokens, slots // 4, 2, 2).transpose(0, 3, 1, 2).reshape(-1, 1)
         return turn + 1, jnp.where(here >= 0, now, have)
 

time: 169 us -> 180 us (1.065)
  blocking collectives: 30.5 us -> 39.4 us
  waiting for transfers between devices: 26.5 us -> 29.7 us
  local copies, waits for them, and re-layouts: 11.6 us -> 9.43 us
    all_to_all x1, blocking collectives: 18.6 us -> 27.2 us  [on_device(): lax.all_to_all(total.reshape(16, 2, 128), ('l', 'h'), 0, 0, tiled=True)]
    ppermute x6, starting transfers between devices: 27.4 us -> 33.7 us  [exchange(): lax.ppermute(value, axis, [(i, i ^ m) for i in range(4)])]
    all_to_all x1, starting transfers between devices: 11 us -> 4.94 us  [on_device(): lax.all_to_all(part.reshape(16, padded // 16, 128), ('y', 'l'), 0, 0, til...]
    ppermute x6, waiting for transfers between devices: 18.6 us -> 24.4 us  [exchange(): lax.ppermute(value, axis, [(i, i ^ m) for i in range(4)])]
    all_to_all x1, waiting for transfers between devices: 3.64 us -> 0.01 us  [on_device(): lax.all_to_all(part.reshape(16, padded // 16, 128), ('y', 'l'), 0, 0, til...]
    unnamed x27 -> x26, local copies, waits for them, and re-layouts: 5.44 us -> 4.28 us
  transfers between devices with their start and end apart: 13 -> 13, of which waited for: 6 -> 7; matrix products, arithmetic and copies ran while one was open for 5% -> 4% of each run, Pallas kernels for 7% -> 6%
where the time goes in v4:
time: 180 us; the launch traced here: 179 us
  starting transfers between devices  71.6 us (40%)
  blocking collectives  39.4 us (22%)
  waiting for transfers between devices  29.7 us (16%)
  Pallas kernels  23.4 us (13%)
  local copies, waits for them, and re-layouts  9.43 us (5%)
  other arithmetic  4.75 us (3%)
    ppermute x6, starting transfers between devices, exchange(): lax.ppermute(value, axis, [(i, i ^ m) for i in range(4)])  33.7 us
    all_to_all x1, blocking collectives, on_device(): lax.all_to_all(total.reshape(16, 2, 128), ('l', 'h'), 0, 0, tiled=True)  27.2 us
    ppermute x6, waiting for transfers between devices, exchange(): lax.ppermute(value, axis, [(i, i ^ m) for i in range(4)])  24.4 us
    all_to_all x1, starting transfers between devices, on_device(): lax.all_to_all(jnp.broadcast_to(chosen[None], (owners,) + chosen.shape),...  17.7 us
    all_to_all x1, blocking collectives, on_device(): lax.all_to_all(total.reshape(16, 32, 128), ('x', 'y'), 0, 0, tiled=True)  12.2 us
    pallas_call x1, Pallas kernels, on_device(): pl.pallas_call(functools.partial(main_kernel, half, tokens, features), gr...  10.5 us
    pallas_call x1, Pallas kernels, expand(): pl.pallas_call(expand_kernel, out_shape=jax.ShapeDtypeStruct((slot.shape[...  8.2 us
    ppermute x4, starting transfers between devices, swap(): return lax.ppermute(value, 'c', [(0, 1), (1, 0)])  7.79 us
  transfers between devices with their start and end apart: 13, of which 7 were waited for; matrix products, arithmetic and copies ran while one was open for 4% of the time, Pallas kernels for 6%

profile of v4, /device:TPU:8, one launch (start us, length us, event | category | flops | bytes accessed | tf_op | source)
XLA Modules:
  0.0 179.5 jit_solution(4364130102314859435)
XLA Ops:
  0.0 0.0 copy-start
  0.0 0.8 broadcast_subtract_fusion
  0.8 0.4 copy-done
  1.2 0.3 convolution_convert_fusion
  1.6 1.9 %collective-permute-start.6 = (bf16[32,128]{1,0:T(8,128)(2,1)S(1)}, bf16[32,128]{1,0:T(8,128)(2,1)S(1)}, u32[]{:S(2)}, u32[]{:S(2)}) collective-permute-start(bf16[32,128]{1,0:T(8,128)(2,1)S(1)} %convolution_convert_fusion), channel_id=1, source_target_pairs={{0,4},{4,0},{1,5},{5,1},{2,6},{6,2},{3,7},{7,3},{8,12},{12,8},{9,1... | collective-permute-start | bytes 24584 | tf_op jit(solution)/shard_map/ppermute | solution.py:227
  3.5 1.1 collective-permute-done.6
  4.6 0.8 broadcast_in_dim.16
  5.4 17.7 %all-to-all-start = ((bf16[16,64,128]{2,1,0:T(8,128)(2,1)}), bf16[16,64,128]{2,1,0:T(8,128)(2,1)}, u32[]{:S(2)}, u32[]{:S(2)}) async-start(bf16[16,64,128]{2,1,0:T(8,128)(2,1)} %broadcast_in_dim.16), calls=%async_computation | async-start | bytes 524288 | tf_op jit(solution)/shard_map/all_to_all | solution.py:257
  23.1 0.0 copy-start.7
  23.1 0.0 copy-done.1
  23.2 0.0 copy-done.2
  23.2 0.0 copy-start.8
  23.2 0.2 copy.34
  23.4 0.2 copy.29
  23.6 0.0 copy-start.11
  23.6 0.2 copy.33
  23.8 0.2 copy.27
  24.0 0.2 copy-done.7
  24.2 0.0 copy-done.8
  24.2 0.9 pad_maximum_fusion
  25.1 1.9 %collective-permute-start.8 = (bf16[2752,128]{1,0:T(8,128)(2,1)}, bf16[2752,128]{1,0:T(8,128)(2,1)S(1)}, u32[]{:S(2)}, u32[]{:S(2)}) collective-permute-start(bf16[2752,128]{1,0:T(8,128)(2,1)} %pad_maximum_fusion), channel_id=1, source_target_pairs={{0,4},{4,0},{1,5},{5,1},{2,6},{6,2},{3,7},{7,3},{8,12},{12,8},{9,1... | collective-permute-start | bytes 2113544 | tf_op jit(solution)/shard_map/ppermute | solution.py:227
  27.0 0.1 pad_add_fusion.1.where_ref
  27.1 0.0 copy-done.11
  27.1 3.2 %shard_map.91 = (s32[64,64]{1,0:T(8,128)S(1)}, s32[352,1]{1,0:T(8,128)S(1)}, s32[1]{0:T(128)}) custom-call(s32[2]{0:T(128)S(1)} %pad_add_fusion.1.where_ref, s32[64,64]{1,0:T(8,128)S(1)} %copy-done.11), custom_call_target="tpu_custom_call" | custom-call | tf_op jit(solution)/shard_map/pallas_call | solution.py:64
  30.3 0.1 reduce.2
  30.4 3.0 %gather_fusion.1 = bf16[352,128]{1,0:T(8,128)(2,1)S(1)} fusion(bf16[8192,128]{1,0:T(8,128)(2,1)} %param.17, s32[1024]{0:T(1024)S(1)} %pad_clamp_fusion.1), kind=kCustom, calls=%fused_computation.1 | custom fusion | bytes 181632 | tf_op jit(solution)/shard_map/jit(_take)/gather | solution.py:279
  33.5 7.7 %collective-permute-start.7 = (bf16[352,128]{1,0:T(8,128)(2,1)S(1)}, bf16[352,128]{1,0:T(8,128)(2,1)S(1)}, u32[]{:S(2)}, u32[]{:S(2)}) collective-permute-start(bf16[352,128]{1,0:T(8,128)(2,1)S(1)} %gather_fusion.1), channel_id=1, source_target_pairs={{0,32},{32,0},{64,96},{96,64},{1,33},{33,1},{65,97},{97,65},{2,34}... | collective-permute-start | bytes 270344 | tf_op jit(solution)/shard_map/ppermute | solution.py:130
  41.2 9.7 %collective-permute-done.7 = bf16[352,128]{1,0:T(8,128)(2,1)S(1)} collective-permute-done((bf16[352,128]{1,0:T(8,128)(2,1)S(1)}, bf16[352,128]{1,0:T(8,128)(2,1)S(1)}, u32[]{:S(2)}, u32[]{:S(2)}) %collective-permute-start.7) | collective-permute-done | bytes 90144 | tf_op jit(solution)/shard_map/ppermute | solution.py:130
  50.8 0.0 all-to-all-done
  50.8 1.0 reduce_sum.39
  51.9 0.0 collective-permute-done.8.rec_ref
  51.9 1.5 shard_map.92
  53.3 4.9 %all-to-all-start.1 = ((f32[16,72,128]{2,1,0:T(8,128)}), f32[16,72,128]{2,1,0:T(8,128)}, u32[]{:S(2)}, u32[]{:S(2)}) async-start(f32[16,72,128]{2,1,0:T(8,128)} %bitcast.11), calls=%async_computation.1 | async-start | bytes 1179648 | tf_op jit(solution)/shard_map/all_to_all | solution.py:297
  58.3 8.3 %collective-permute-start.10 = (bf16[352,128]{1,0:T(8,128)(2,1)S(1)}, bf16[352,128]{1,0:T(8,128)(2,1)S(1)}, u32[]{:S(2)}, u32[]{:S(2)}) collective-permute-start(bf16[352,128]{1,0:T(8,128)(2,1)S(1)} %gather_fusion.1), channel_id=1, source_target_pairs={{0,96},{32,64},{64,32},{96,0},{1,97},{33,65},{65,33},{97,1},{2,98}... | collective-permute-start | bytes 270344 | tf_op jit(solution)/shard_map/ppermute | solution.py:130
  66.6 7.3 %collective-permute-start.9 = (bf16[352,128]{1,0:T(8,128)(2,1)S(1)}, bf16[352,128]{1,0:T(8,128)(2,1)S(1)}, u32[]{:S(2)}, u32[]{:S(2)}) collective-permute-start(bf16[352,128]{1,0:T(8,128)(2,1)S(1)} %gather_fusion.1), channel_id=1, source_target_pairs={{0,64},{32,96},{64,0},{96,32},{1,65},{33,97},{65,1},{97,33},{2,66}... | collective-permute-start | bytes 270344 | tf_op jit(solution)/shard_map/ppermute | solution.py:130
  73.8 2.4 %collective-permute-done.10 = bf16[352,128]{1,0:T(8,128)(2,1)S(1)} collective-permute-done((bf16[352,128]{1,0:T(8,128)(2,1)S(1)}, bf16[352,128]{1,0:T(8,128)(2,1)S(1)}, u32[]{:S(2)}, u32[]{:S(2)}) %collective-permute-start.10) | collective-permute-done | bytes 90144 | tf_op jit(solution)/shard_map/ppermute | solution.py:130
  76.3 9.7 %collective-permute-done.9 = bf16[352,128]{1,0:T(8,128)(2,1)S(1)} collective-permute-done((bf16[352,128]{1,0:T(8,128)(2,1)S(1)}, bf16[352,128]{1,0:T(8,128)(2,1)S(1)}, u32[]{:S(2)}, u32[]{:S(2)}) %collective-permute-start.9) | collective-permute-done | bytes 90144 | tf_op jit(solution)/shard_map/ppermute | solution.py:130
  86.1 3.4 %collective-permute-start.11 = (bf16[1408,128]{1,0:T(8,128)(2,1)S(1)}, bf16[1408,128]{1,0:T(8,128)(2,1)S(1)}, u32[]{:S(2)}, u32[]{:S(2)}) collective-permute-start(bf16[1408,128]{1,0:T(8,128)(2,1)S(1)} %pad_maximum_fusion.1.refs_0_), channel_id=1, source_target_pairs={{0,128},{128,0},{256,384},{384,256},{1,129},{129,1},{257,385},{385... | collective-permute-start | bytes 1081352 | tf_op jit(solution)/shard_map/ppermute | solution.py:130
  89.4 4.6 %collective-permute-start.12 = (bf16[1408,128]{1,0:T(8,128)(2,1)S(1)}, bf16[1408,128]{1,0:T(8,128)(2,1)S(1)}, u32[]{:S(2)}, u32[]{:S(2)}) collective-permute-start(bf16[1408,128]{1,0:T(8,128)(2,1)S(1)} %pad_maximum_fusion.1.refs_0_), channel_id=1, source_target_pairs={{0,256},{128,384},{256,0},{384,128},{1,257},{129,385},{257,1},{385... | collective-permute-start | bytes 1081352 | tf_op jit(solution)/shard_map/ppermute | solution.py:130
  94.0 2.5 %collective-permute-start.13 = (bf16[1408,128]{1,0:T(8,128)(2,1)S(1)}, bf16[1408,128]{1,0:T(8,128)(2,1)S(1)}, u32[]{:S(2)}, u32[]{:S(2)}) collective-permute-start(bf16[1408,128]{1,0:T(8,128)(2,1)S(1)} %pad_maximum_fusion.1.refs_0_), channel_id=1, source_target_pairs={{0,384},{128,256},{256,128},{384,0},{1,385},{129,257},{257,129},{3... | collective-permute-start | bytes 1081352 | tf_op jit(solution)/shard_map/ppermute | solution.py:130
  96.5 0.0 all-to-all-done.1
  96.5 1.1 reduce_sum.40
  97.6 0.8 broadcast_in_dim.17
  98.5 7.5 %all-to-all-start.2 = ((f32[16,72,128]{2,1,0:T(8,128)}), f32[16,72,128]{2,1,0:T(8,128)}, u32[]{:S(2)}, u32[]{:S(2)}) async-start(f32[16,72,128]{2,1,0:T(8,128)} %broadcast_in_dim.17), calls=%async_computation.2 | async-start | bytes 1179648 | tf_op jit(solution)/shard_map/all_to_all | solution.py:301
  106.0 0.0 collective-permute-done.11.refs_1_
  106.0 0.0 collective-permute-done.12.refs_2_
  106.0 2.5 %collective-permute-done.13.refs_3_ = bf16[1408,128]{1,0:T(8,128)(2,1)S(1)} collective-permute-done((bf16[1408,128]{1,0:T(8,128)(2,1)S(1)}, bf16[1408,128]{1,0:T(8,128)(2,1)S(1)}, u32[]{:S(2)}, u32[]{:S(2)}) %collective-permute-start.13) | collective-permute-done | bytes 360480 | tf_op jit(solution)/shard_map/ppermute | solution.py:130
  108.5 8.2 %shard_map.93 = bf16[4096,128]{1,0:T(8,128)(2,1)} custom-call(s32[64,64]{1,0:T(8,128)S(1)} %get-tuple-element.55.slot_ref, bf16[1408,128]{1,0:T(8,128)(2,1)S(1)} %pad_maximum_fusion.1.refs_0_, bf16[1408,128]{1,0:T(8,128)(2,1)S(1)} %collective-permute-done.11.refs_1_, bf16[1408,128]{1,0:T(8,128)(2,1)S(1)} %collective-permute-done.12.refs_2_, ...), custom_call_target="tpu_custom_call" | custom-call | tf_op jit(solution)/shard_map/pallas_call | solution.py:115
  116.7 0.6 while.10
  117.2 1.9 %collective-permute-start.14 = (bf16[4096,128]{1,0:T(8,128)(2,1)}, bf16[4096,128]{1,0:T(8,128)(2,1)S(1)}, u32[]{:S(2)}, u32[]{:S(2)}) collective-permute-start(bf16[4096,128]{1,0:T(8,128)(2,1)} %get-tuple-element.168), channel_id=1, source_target_pairs={{0,4},{4,0},{1,5},{5,1},{2,6},{6,2},{3,7},{7,3},{8,12},{12,8},{9,1... | collective-permute-start | bytes 3145736 | tf_op jit(solution)/shard_map/ppermute | solution.py:227
  119.2 2.8 %collective-permute-done.14.far_ref = bf16[4096,128]{1,0:T(8,128)(2,1)S(1)} collective-permute-done((bf16[4096,128]{1,0:T(8,128)(2,1)}, bf16[4096,128]{1,0:T(8,128)(2,1)S(1)}, u32[]{:S(2)}, u32[]{:S(2)}) %collective-permute-start.14) | collective-permute-done | bytes 1048608 | tf_op jit(solution)/shard_map/ppermute | solution.py:227
  122.0 1.0 copy-done.5
  123.0 0.0 all-to-all-done.2
  123.0 1.1 copy-done.4
  124.1 1.2 copy-done.6
  125.3 10.5 %shard_map.94 = (f32[512,128]{1,0:T(8,128)S(1)}, f32[512,128]{1,0:T(8,128)S(1)}) custom-call(s32[1]{0:T(128)} %bitcast.3.core_ref, f32[1152,128]{1,0:T(8,128)} %bitcast.12.pre_ref, bf16[128,1792]{1,0:T(8,128)(2,1)S(1)} %copy-done.1, bf16[128,1792]{1,0:T(8,128)(2,1)S(1)} %copy-done.2, bf16[2752,128]{1,0:T(8,128)(2,1)S(1)} %copy-done.4, ...), custom_call_target="tpu_custom_call" | custom-call | tf_op jit(solution)/shard_map/pallas_call | solution.py:325
  135.8 0.0 copy-start.14
  135.9 2.0 %collective-permute-start.15 = (f32[512,128]{1,0:T(8,128)S(1)}, f32[512,128]{1,0:T(8,128)S(1)}, u32[]{:S(2)}, u32[]{:S(2)}) collective-permute-start(f32[512,128]{1,0:T(8,128)S(1)} %get-tuple-element.60), channel_id=1, source_target_pairs={{0,4},{4,0},{1,5},{5,1},{2,6},{6,2},{3,7},{7,3},{8,12},{12,8},{9,1... | collective-permute-start | bytes 786440 | tf_op jit(solution)/shard_map/ppermute | solution.py:227
  137.9 1.4 collective-permute-done.15
  139.3 12.2 %all_to_all.25 = f32[16,32,128]{2,1,0:T(8,128)S(1)} all-to-all(f32[16,32,128]{2,1,0:T(8,128)S(1)} %bitcast.33), channel_id=1, replica_groups=mesh['x'=4,'h'=4,'y'=4,'c'=2,'l'=4] {'x','y'}, dimensions={0} | all-to-all | bytes 524288 | tf_op jit(solution)/shard_map/all_to_all | solution.py:347
  151.6 27.2 %all_to_all.26 = f32[16,2,128]{2,1,0:T(2,128)S(1)} all-to-all(f32[16,2,128]{2,1,0:T(2,128)S(1)} %bitcast.38), channel_id=1, replica_groups=mesh['x'=4,'h'=4,'y'=4,'c'=2,'l'=4] {'l','h'}, dimensions={0} | all-to-all | bytes 32768 | tf_op jit(solution)/shard_map/all_to_all | solution.py:348
  178.8 0.1 reshape.57
  178.9 0.0 copy-done.14
  178.9 0.6 copy_multiply_fusion
  (19 shorter events, 0.2 us)
Async XLA Ops:
  0.0 1.2 copy-start
  0.0 23.1 %copy-start.1 = (bf16[128,1792]{1,0:T(8,128)(2,1)S(1)}, bf16[128,1792]{1,0:T(8,128)(2,1)}, u32[]{:S(2)}) copy-start(bf16[128,1792]{1,0:T(8,128)(2,1)} %gate_ref.3) | copy-start | bytes 1376260
  0.0 23.1 %copy-start.2 = (bf16[128,1792]{1,0:T(8,128)(2,1)S(1)}, bf16[128,1792]{1,0:T(8,128)(2,1)}, u32[]{:S(2)}) copy-start(bf16[128,1792]{1,0:T(8,128)(2,1)} %up_ref.3) | copy-start | bytes 1376260
  1.6 3.1 %collective-permute-start.6 = (bf16[32,128]{1,0:T(8,128)(2,1)S(1)}, bf16[32,128]{1,0:T(8,128)(2,1)S(1)}, u32[]{:S(2)}, u32[]{:S(2)}) collective-permute-start(bf16[32,128]{1,0:T(8,128)(2,1)S(1)} %convolution_convert_fusion), channel_id=1, source_target_pairs={{0,4},{4,0},{1,5},{5,1},{2,6},{6,2},{3,7},{7,3},{8,12},{12,8},{9,1... | collective-permute-start | bytes 24584 | tf_op jit(solution)/shard_map/ppermute | solution.py:227
  5.4 45.4 %all-to-all-start = ((bf16[16,64,128]{2,1,0:T(8,128)(2,1)}), bf16[16,64,128]{2,1,0:T(8,128)(2,1)}, u32[]{:S(2)}, u32[]{:S(2)}) async-start(bf16[16,64,128]{2,1,0:T(8,128)(2,1)} %broadcast_in_dim.16), calls=%async_computation | async-start | bytes 524288 | tf_op jit(solution)/shard_map/all_to_all | solution.py:257
  23.1 1.0 copy-start.7
  23.2 1.0 copy-start.8
  23.6 3.5 %copy-start.11 = (s32[64,64]{1,0:T(8,128)S(1)}, s32[64,64]{1,0:T(8,128)}, u32[]{:S(2)}) copy-start(s32[64,64]{1,0:T(8,128)} %ids_ref) | copy-start | bytes 49156
  25.1 26.8 %collective-permute-start.8 = (bf16[2752,128]{1,0:T(8,128)(2,1)}, bf16[2752,128]{1,0:T(8,128)(2,1)S(1)}, u32[]{:S(2)}, u32[]{:S(2)}) collective-permute-start(bf16[2752,128]{1,0:T(8,128)(2,1)} %pad_maximum_fusion), channel_id=1, source_target_pairs={{0,4},{4,0},{1,5},{5,1},{2,6},{6,2},{3,7},{7,3},{8,12},{12,8},{9,1... | collective-permute-start | bytes 2113544 | tf_op jit(solution)/shard_map/ppermute | solution.py:227
  33.5 17.4 %collective-permute-start.7 = (bf16[352,128]{1,0:T(8,128)(2,1)S(1)}, bf16[352,128]{1,0:T(8,128)(2,1)S(1)}, u32[]{:S(2)}, u32[]{:S(2)}) collective-permute-start(bf16[352,128]{1,0:T(8,128)(2,1)S(1)} %gather_fusion.1), channel_id=1, source_target_pairs={{0,32},{32,0},{64,96},{96,64},{1,33},{33,1},{65,97},{97,65},{2,34}... | collective-permute-start | bytes 270344 | tf_op jit(solution)/shard_map/ppermute | solution.py:130
  51.9 1.5 copy-start.3
  53.3 43.2 %all-to-all-start.1 = ((f32[16,72,128]{2,1,0:T(8,128)}), f32[16,72,128]{2,1,0:T(8,128)}, u32[]{:S(2)}, u32[]{:S(2)}) async-start(f32[16,72,128]{2,1,0:T(8,128)} %bitcast.11), calls=%async_computation.1 | async-start | bytes 1179648 | tf_op jit(solution)/shard_map/all_to_all | solution.py:297
  58.3 18.0 %collective-permute-start.10 = (bf16[352,128]{1,0:T(8,128)(2,1)S(1)}, bf16[352,128]{1,0:T(8,128)(2,1)S(1)}, u32[]{:S(2)}, u32[]{:S(2)}) collective-permute-start(bf16[352,128]{1,0:T(8,128)(2,1)S(1)} %gather_fusion.1), channel_id=1, source_target_pairs={{0,96},{32,64},{64,32},{96,0},{1,97},{33,65},{65,33},{97,1},{2,98}... | collective-permute-start | bytes 270344 | tf_op jit(solution)/shard_map/ppermute | solution.py:130
  66.6 19.5 %collective-permute-start.9 = (bf16[352,128]{1,0:T(8,128)(2,1)S(1)}, bf16[352,128]{1,0:T(8,128)(2,1)S(1)}, u32[]{:S(2)}, u32[]{:S(2)}) collective-permute-start(bf16[352,128]{1,0:T(8,128)(2,1)S(1)} %gather_fusion.1), channel_id=1, source_target_pairs={{0,64},{32,96},{64,0},{96,32},{1,65},{33,97},{65,1},{97,33},{2,66}... | collective-permute-start | bytes 270344 | tf_op jit(solution)/shard_map/ppermute | solution.py:130
  86.1 19.9 %collective-permute-start.11 = (bf16[1408,128]{1,0:T(8,128)(2,1)S(1)}, bf16[1408,128]{1,0:T(8,128)(2,1)S(1)}, u32[]{:S(2)}, u32[]{:S(2)}) collective-permute-start(bf16[1408,128]{1,0:T(8,128)(2,1)S(1)} %pad_maximum_fusion.1.refs_0_), channel_id=1, source_target_pairs={{0,128},{128,0},{256,384},{384,256},{1,129},{129,1},{257,385},{385... | collective-permute-start | bytes 1081352 | tf_op jit(solution)/shard_map/ppermute | solution.py:130
  89.4 16.5 %collective-permute-start.12 = (bf16[1408,128]{1,0:T(8,128)(2,1)S(1)}, bf16[1408,128]{1,0:T(8,128)(2,1)S(1)}, u32[]{:S(2)}, u32[]{:S(2)}) collective-permute-start(bf16[1408,128]{1,0:T(8,128)(2,1)S(1)} %pad_maximum_fusion.1.refs_0_), channel_id=1, source_target_pairs={{0,256},{128,384},{256,0},{384,128},{1,257},{129,385},{257,1},{385... | collective-permute-start | bytes 1081352 | tf_op jit(solution)/shard_map/ppermute | solution.py:130
  94.0 14.4 %collective-permute-start.13 = (bf16[1408,128]{1,0:T(8,128)(2,1)S(1)}, bf16[1408,128]{1,0:T(8,128)(2,1)S(1)}, u32[]{:S(2)}, u32[]{:S(2)}) collective-permute-start(bf16[1408,128]{1,0:T(8,128)(2,1)S(1)} %pad_maximum_fusion.1.refs_0_), channel_id=1, source_target_pairs={{0,384},{128,256},{256,128},{384,0},{1,385},{129,257},{257,129},{3... | collective-permute-start | bytes 1081352 | tf_op jit(solution)/shard_map/ppermute | solution.py:130
  98.5 24.5 %all-to-all-start.2 = ((f32[16,72,128]{2,1,0:T(8,128)}), f32[16,72,128]{2,1,0:T(8,128)}, u32[]{:S(2)}, u32[]{:S(2)}) async-start(f32[16,72,128]{2,1,0:T(8,128)} %broadcast_in_dim.17), calls=%async_computation.2 | async-start | bytes 1179648 | tf_op jit(solution)/shard_map/all_to_all | solution.py:301
  105.9 10.7 %copy-start.12 = (s32[64,64]{1,0:T(8,128)S(1)}, s32[64,64]{1,0:T(8,128)}, u32[]{:S(2)}) copy-start(s32[64,64]{1,0:T(8,128)} %ids_ref) | copy-start | bytes 49156
  117.2 4.8 %collective-permute-start.14 = (bf16[4096,128]{1,0:T(8,128)(2,1)}, bf16[4096,128]{1,0:T(8,128)(2,1)S(1)}, u32[]{:S(2)}, u32[]{:S(2)}) collective-permute-start(bf16[4096,128]{1,0:T(8,128)(2,1)} %get-tuple-element.168), channel_id=1, source_target_pairs={{0,4},{4,0},{1,5},{5,1},{2,6},{6,2},{3,7},{7,3},{8,12},{12,8},{9,1... | collective-permute-start | bytes 3145736 | tf_op jit(solution)/shard_map/ppermute | solution.py:227
  122.0 1.0 copy-start.5
  123.0 1.1 copy-start.4
  124.1 1.2 copy-start.6
  135.8 43.0 %copy-start.14 = (f32[16,4]{0,1:T(4,128)S(1)}, f32[16,4]{0,1:T(4,128)}, u32[]{:S(2)}) copy-start(f32[16,4]{0,1:T(4,128)} %param.19) | copy-start | bytes 772
  135.9 3.4 %collective-permute-start.15 = (f32[512,128]{1,0:T(8,128)S(1)}, f32[512,128]{1,0:T(8,128)S(1)}, u32[]{:S(2)}, u32[]{:S(2)}) collective-permute-start(f32[512,128]{1,0:T(8,128)S(1)} %get-tuple-element.60), channel_id=1, source_target_pairs={{0,4},{4,0},{1,5},{5,1},{2,6},{6,2},{3,7},{7,3},{8,12},{12,8},{9,1... | collective-permute-start | bytes 786440 | tf_op jit(solution)/shard_map/ppermute | solution.py:227

commit v5 on v4

v5 whole, which is shorter than its diff:
```python
import functools

import jax
import jax.numpy as jnp
from jax import lax
from jax.experimental import pallas as pl
from jax.experimental.pallas import tpu as pltpu
from jax.sharding import Mesh
from jax.sharding import PartitionSpec as P

F32 = jnp.float32
BF16 = jnp.bfloat16
CAP = 352
MIB = 1024 * 1024


def nt(a, b):
    return lax.dot_general(a, b, (((1,), (1,)), ((), ())), preferred_element_type=F32)


def nn(a, b):
    return lax.dot_general(a, b, (((1,), (0,)), ((), ())), preferred_element_type=F32)


def plan_kernel(owners, dec_rows, where_ref, ids_ref, slot_ref, list_ref, rounds_ref):
    tokens, slots = ids_ref.shape
    ids = ids_ref[...]
    ids = jnp.concatenate([ids[: tokens // 2], ids[tokens // 2 :]], axis=1)
    rows, lanes = ids.shape
    owner = lax.div(ids, dec_rows)
    upto = lax.broadcasted_iota(jnp.int32, (lanes, lanes), 0) <= lax.broadcasted_iota(
        jnp.int32, (lanes, lanes), 1
    )
    upto = upto.astype(F32).astype(BF16)
    before = lax.broadcasted_iota(jnp.int32, (rows, rows), 1) < lax.broadcasted_iota(
        jnp.int32, (rows, rows), 0
    )
    before = before.astype(F32).astype(BF16)
    ones = jnp.ones((lanes, lanes), BF16)
    pos = jnp.zeros((rows, lanes), F32)
    for o in range(owners):
        hit = (owner == o).astype(F32)
        hit16 = hit.astype(BF16)
        total = nn(hit16, ones).astype(BF16)
        count = nn(hit16, upto) + nn(before, total)
        pos = pos + hit * (count - 1.0)
    rank = where_ref[0]
    start = where_ref[1] * CAP
    at = pos.astype(jnp.int32) - start
    here = jnp.logical_and(at >= 0, at < CAP)
    slot = jnp.where(here, owner * CAP + at, -1)
    slot_ref[...] = jnp.concatenate([slot[:, :slots], slot[:, slots:]], axis=0)
    rounds_ref[0] = lax.div(jnp.max(pos).astype(jnp.int32), CAP) + 1
    mine = jnp.where(owner == rank, pos - start.astype(F32), -1.0)
    local = (ids - rank * dec_rows).astype(F32)
    want = lax.broadcasted_iota(jnp.int32, (CAP, lanes), 0).astype(F32)
    acc = jnp.zeros((CAP, lanes), F32)
    for r in range(rows):
        acc = acc + jnp.where(mine[r : r + 1, :] == want, local[r : r + 1, :], 0.0)
    list_ref[...] = jnp.sum(acc, axis=1, keepdims=True).astype(jnp.int32)


def plan(ids, rank, turn, owners, dec_rows):
    slot, rows, rounds = pl.pallas_call(
        functools.partial(plan_kernel, owners, dec_rows),
        out_shape=(
            jax.ShapeDtypeStruct(ids.shape, jnp.int32),
            jax.ShapeDtypeStruct((CAP, 1), jnp.int32),
            jax.ShapeDtypeStruct((1,), jnp.int32),
        ),
        in_specs=[
            pl.BlockSpec(memory_space=pltpu.SMEM),
            pl.BlockSpec(memory_space=pltpu.VMEM),
        ],
        out_specs=(
            pl.BlockSpec(memory_space=pltpu.VMEM),
            pl.BlockSpec(memory_space=pltpu.VMEM),
            pl.BlockSpec(memory_space=pltpu.SMEM),
        ),
        compiler_params=pltpu.CompilerParams(vmem_limit_bytes=4 * MIB),
    )(jnp.stack([rank, turn]).astype(jnp.int32), ids)
    return slot, rows.reshape(-1), rounds


def expand_kernel(rounds_ref, slot_ref, have_ref, *refs):
    parts, (out_ref, table, block, old, sem) = refs[:-5], refs[-5:]
    size = parts[0].shape[0]
    piece = 128

    def widen(i, carry):
        for p, ref in enumerate(parts):
            to = pl.ds(pl.multiple_of(p * size + i * piece, piece), piece)
            table[to, :] = ref[pl.ds(pl.multiple_of(i * piece, piece), piece), :].astype(F32)
        return carry

    lax.fori_loop(0, size // piece, widen, 0)
    tokens, slots = slot_ref.shape

    def place(low, r, high):
        return low * (slots // 2) + r * 2 + high, r * 4 + high * 2 + low

    order = [place(low, r, high) for low in range(2) for r in range(slots // 4) for high in range(2)]

    def token(t, carry):
        for to, k in order:
            block[to : to + 1, :] = table[pl.ds(slot_ref[t, k], 1), :]
        out_ref[pl.ds(pl.multiple_of(t * slots, slots), slots), :] = block[...].astype(BF16)
        return carry

    def merged(t, carry):
        rows = pl.ds(pl.multiple_of(t * slots, slots), slots)
        copy = pltpu.make_async_copy(have_ref.at[rows], old, sem)
        copy.start()
        copy.wait()
        block[...] = old[...].astype(F32)
        for to, k in order:
            src = slot_ref[t, k]

            @pl.when(src >= 0)
            def _():
                block[to : to + 1, :] = table[pl.ds(src, 1), :]

        out_ref[rows, :] = block[...].astype(BF16)
        return carry

    @pl.when(rounds_ref[0] == 1)
    def _():
        lax.fori_loop(0, tokens, token, 0)

    @pl.when(rounds_ref[0] > 1)
    def _():
        lax.fori_loop(0, tokens, merged, 0)


def expand(rounds, slot, have, parts):
    size = parts[0].shape[0]
    smem = pl.BlockSpec(memory_space=pltpu.SMEM)
    vmem = pl.BlockSpec(memory_space=pltpu.VMEM)
    return pl.pallas_call(
        expand_kernel,
        out_shape=jax.ShapeDtypeStruct(have.shape, BF16),
        in_specs=[smem, smem, pl.BlockSpec(memory_space=pl.ANY)] + [vmem] * len(parts),
        out_specs=vmem,
        scratch_shapes=[
            pltpu.VMEM((len(parts) * size, 128), F32),
            pltpu.VMEM((slot.shape[1], 128), F32),
            pltpu.VMEM((slot.shape[1], 128), BF16),
            pltpu.SemaphoreType.DMA,
        ],
        compiler_params=pltpu.CompilerParams(vmem_limit_bytes=12 * MIB),
    )(rounds, slot, have, *parts)


def tell(value, axis, count):
    return lax.all_to_all(
        jnp.broadcast_to(value[None], (count,) + value.shape), axis, 0, 0, tiled=True
    )


def after(value, other):
    return lax.optimization_barrier((value, other))[0]


def weight_kernel(half, core_ref, gate_ref, up_ref, rec_ref, out_ref):
    dblk = gate_ref.shape[0]
    cols = pl.ds(pl.multiple_of(core_ref[0] * half, 128), half)
    out_ref[:dblk, :half] = gate_ref[:, cols]
    out_ref[:dblk, half:] = up_ref[:, cols]
    for i in range(2 * half // 128):
        out_ref[dblk:, i * 128 : (i + 1) * 128] = rec_ref[i * 128 : (i + 1) * 128, :]


def forward_kernel(half, core_ref, x_ref, cot_ref, weight_ref, down_ref, rec_ref, out_ref):
    core = core_ref[0]
    tokens, dblk = x_ref.shape
    features = cot_ref.shape[0]
    group = 2 * tokens + features
    x = jnp.concatenate([x_ref[...], rec_ref[3 * half : 3 * half + tokens, :]], axis=1)
    pre = nn(x, weight_ref[...])
    down = jnp.concatenate(
        [
            down_ref[pl.ds(pl.multiple_of(core * half, 128), half), :],
            rec_ref[2 * half : 3 * half, :],
        ],
        axis=1,
    )
    neuron = nt(cot_ref[...], down)
    for i in range(half // 128):
        base = i * group
        cols = slice(i * 128, (i + 1) * 128)
        out_ref[base : base + tokens, :] = pre[:, cols]
        out_ref[base + tokens : base + 2 * tokens, :] = pre[:, half + i * 128 : half + (i + 1) * 128]
        out_ref[base + 2 * tokens : base + group, :] = neuron[:, cols]
    used = (half // 128) * group
    if out_ref.shape[0] > used:
        out_ref[used:, :] = jnp.zeros((out_ref.shape[0] - used, 128), F32)


def main_kernel(
    half, tokens, features, steps, core_ref, pre_ref, weight_ref, own_ref, far_ref, mine_ref, theirs_ref,
    dec_ref, grads, sems,
):
    core = core_ref[0]
    tile = tokens // steps
    block = dec_ref.shape[0] // steps
    group = 2 * tokens + features

    def copies(step):
        rows = pl.ds(pl.multiple_of(step * block, block), block)
        return (
            pltpu.make_async_copy(own_ref.at[rows], dec_ref.at[rows, pl.ds(0, 128)], sems.at[step, 0]),
            pltpu.make_async_copy(
                far_ref.at[rows], dec_ref.at[rows, pl.ds(128, 128)], sems.at[step, 1]
            ),
        )

    for step in range(steps):
        for copy in copies(step):
            copy.start()
    lane = lax.broadcasted_iota(jnp.int32, (64, 128), 1)
    first = lax.broadcasted_iota(jnp.int32, (32, 128), 1) < 64
    which = lax.rem(lane, tile)

    def one_step(step, carry):
        for i in range(half // 128):
            base = i * group
            gate_pre = pre_ref[pl.ds(pl.multiple_of(base + step * tile, 8), tile), :]
            up_pre = pre_ref[pl.ds(pl.multiple_of(base + tokens + step * tile, 8), tile), :]
            neuron = pre_ref[base + 2 * tokens : base + group, :]
            s = jax.nn.sigmoid(gate_pre)
            gate_factor = up_pre * s * (1.0 + gate_pre * (1.0 - s))
            up_factor = gate_pre * s
            for j in range(features):
                row = neuron[j : j + 1, :]
                to = slice(j * tile, (j + 1) * tile)
                grads[to, i * 128 : (i + 1) * 128] = (row * gate_factor).astype(BF16)
                grads[to, half + i * 128 : half + (i + 1) * 128] = (row * up_factor).astype(BF16)
        width = nt(grads[...], weight_ref[...])
        high = width.astype(BF16)
        low = (width - high.astype(F32)).astype(BF16)
        for copy in copies(step):
            copy.wait()
        dec = dec_ref[pl.ds(pl.multiple_of(step * block, block), block), :]
        for y in range(features // 8):
            part = slice(y * 128, (y + 1) * 128)
            both = jnp.concatenate([high[part, :], low[part, :]], axis=0)
            full = nt(dec, both)
            full = full[:, :128] + full[:, 128:]
            sel = full[:64, :]
            for t in range(1, tile):
                sel = jnp.where(which == t, full[t * 64 : (t + 1) * 64, :], sel)
            a, b = sel[:32, :], sel[32:, :]
            zero = jnp.where(first, a, pltpu.roll(b, 64, 1))
            one = jnp.where(first, pltpu.roll(a, 64, 1), b)
            keep = jnp.where(core == 0, zero, one)
            send = jnp.where(core == 0, one, zero)
            for x in range(4):
                to = pl.ds(pl.multiple_of(((x * 4 + y) * 4 + step) * 8, 8), 8)
                mine_ref[to, :] = keep[x * 8 : (x + 1) * 8, :]
                theirs_ref[to, :] = send[x * 8 : (x + 1) * 8, :]
        return carry

    lax.fori_loop(0, steps, one_step, 0)


def contract(core_arg, pre, weight, dec, dec_far, half, tokens, features):
    steps = 4
    vmem = pl.BlockSpec(memory_space=pltpu.VMEM)
    hbm = pl.BlockSpec(memory_space=pl.ANY)
    return pl.pallas_call(
        functools.partial(main_kernel, half, tokens, features, steps),
        out_shape=(jax.ShapeDtypeStruct((512, 128), F32),) * 2,
        in_specs=[pl.BlockSpec(memory_space=pltpu.SMEM), vmem, vmem, hbm, hbm],
        out_specs=(vmem,) * 2,
        scratch_shapes=[
            pltpu.VMEM((dec.shape[0], 256), BF16),
            pltpu.VMEM((features * tokens // steps, 2 * half), BF16),
            pltpu.SemaphoreType.DMA((steps, 2)),
        ],
        compiler_params=pltpu.CompilerParams(vmem_limit_bytes=20 * MIB),
    )(core_arg, pre, weight, dec, dec_far)


def swap(value):
    return lax.ppermute(value, "c", [(0, 1), (1, 0)])


def on_device(
    mlp_input,
    gate_weight,
    up_weight,
    down_weight,
    down_encoder,
    feature_ids,
    up_decoder,
    latent_ids,
    latent_acts,
):
    tokens, dblk = mlp_input.shape
    half = gate_weight.shape[1] // 2
    features = feature_ids.shape[0]
    slots = latent_ids.shape[1]
    owners = 16
    core = lax.axis_index("c").astype(jnp.int32)
    rank = (lax.axis_index("x") * 4 + lax.axis_index("h")).astype(jnp.int32)
    core_arg = core[None]
    other = 1 - core

    enc_rows = down_encoder.shape[0]
    local = feature_ids - rank * enc_rows
    picker = (local[:, None] == jnp.arange(enc_rows, dtype=jnp.int32)[None, :]).astype(BF16)
    chosen = jnp.dot(picker, down_encoder, preferred_element_type=F32).astype(BF16)
    other = after(other, chosen)
    chosen = jnp.concatenate([chosen, swap(chosen)], axis=0)

    dec_rows = up_decoder.shape[0]
    slot, rows, rounds = plan(latent_ids, rank, jnp.int32(0), owners, dec_rows)

    def more(carry):
        return carry[0] < rounds[0]

    def another(carry):
        turn, have = carry
        slot_now, rows_now, _ = plan(latent_ids, rank, turn, owners, dec_rows)
        taken = jnp.take(up_decoder, rows_now, axis=0, mode="clip")
        spread = tell(tell(taken, "h", 4).reshape(4 * CAP, 128), "x", 4)
        return turn + 1, expand(rounds, slot_now, have, [spread.reshape(owners * CAP, 128)])

    nothing = jnp.zeros((tokens * slots, 128), BF16)
    _, have = lax.while_loop(more, another, (jnp.int32(1), nothing))
    cot = tell(after(chosen, have), ("x", "h"), owners)

    def columns(w):
        part = lax.dynamic_slice(w, (0, other * half), (dblk, half))
        return part.reshape(dblk, half // 128, 128).transpose(1, 0, 2).reshape(half, 128)

    pack = jnp.concatenate(
        [
            columns(gate_weight),
            columns(up_weight),
            lax.dynamic_slice(down_weight, (other * half, 0), (half, dblk)),
            mlp_input,
        ],
        axis=0,
    )
    rec = swap(pack)

    picked = jnp.take(up_decoder, rows, axis=0, mode="clip")

    table = lax.all_gather(picked, ("x", "h")).reshape(owners * CAP, 128)

    cot = jnp.sum(after(cot, picked).astype(F32), axis=0).astype(BF16)
    cot = jnp.concatenate([cot[:features], cot[features:]], axis=1)

    vmem = pl.BlockSpec(memory_space=pltpu.VMEM)
    smem = pl.BlockSpec(memory_space=pltpu.SMEM)
    weight = pl.pallas_call(
        functools.partial(weight_kernel, half),
        out_shape=jax.ShapeDtypeStruct((2 * dblk, 2 * half), BF16),
        in_specs=[smem] + [vmem] * 3,
        out_specs=vmem,
        compiler_params=pltpu.CompilerParams(vmem_limit_bytes=6 * MIB),
    )(core_arg, gate_weight, up_weight, rec)

    used = (half // 128) * (2 * tokens + features)
    padded = -(-used // 128) * 128
    part = pl.pallas_call(
        functools.partial(forward_kernel, half),
        out_shape=jax.ShapeDtypeStruct((padded, 128), F32),
        in_specs=[smem] + [vmem] * 5,
        out_specs=vmem,
        compiler_params=pltpu.CompilerParams(vmem_limit_bytes=8 * MIB),
    )(core_arg, mlp_input, cot, weight, down_weight, rec)
    part = lax.all_to_all(part.reshape(16, padded // 16, 128), ("y", "l"), 0, 0, tiled=True)
    part = jnp.sum(after(part, table), axis=0)
    slot = after(slot, part)
    pre = lax.all_to_all(
        jnp.broadcast_to(part[None], (16,) + part.shape), ("y", "l"), 0, 0, tiled=True
    ).reshape(padded, 128)

    dec = expand(rounds, slot, have, [table])
    dec_far = swap(dec)

    mine, theirs = contract(core_arg, pre, weight, dec, dec_far, half, tokens, features)

    total = mine + swap(theirs)
    total = jnp.sum(lax.all_to_all(total.reshape(16, 32, 128), ("x", "y"), 0, 0, tiled=True), axis=0)
    total = jnp.sum(lax.all_to_all(total.reshape(16, 2, 128), ("l", "h"), 0, 0, tiled=True), axis=0)
    total = total.reshape(2, 2, features // 8, tokens // 4).transpose(2, 3, 0, 1)
    return total.reshape(features // 8, tokens // 4, slots // 16) * latent_acts[None, :, :]


def solution(mesh):
    fine = Mesh(mesh.devices.reshape(4, 4, 4, 2, 4), ("x", "h", "y", "c", "l"))
    width = ("y", "c", "l")
    tensor = ("x", "h")
    in_specs = (
        P(None, width),
        P(width, tensor),
        P(width, tensor),
        P(tensor, width),
        P(tensor, width),
        P(),
        P(tensor, width),
        P(),
        P("l", tensor),
    )
    out_specs = P(("y", "c"), "l", tensor)
    return jax.shard_map(
        on_device, mesh=fine, in_specs=in_specs, out_specs=out_specs, check_vma=False
    )
```

time: 180 us -> 213 us (1.18)
  waiting for transfers between devices: 29.7 us -> 81.2 us
  starting transfers between devices: 71.6 us -> 39.8 us
  between operations: 0.33 us -> 13.6 us
  local copies, waits for them, and re-layouts: 9.43 us -> 18.2 us
  blocking collectives: 39.4 us -> 32.3 us
    all_gather x0 -> x1, waiting for transfers between devices: none -> 63.2 us  [on_device(): table = lax.all_gather(picked, ('x', 'h')).reshape(owners * CAP, 128)]
    ppermute x6 -> x0, starting transfers between devices: 33.7 us -> none  [exchange(): lax.ppermute(value, axis, [(i, i ^ m) for i in range(4)])]
    ppermute x6 -> x0, waiting for transfers between devices: 24.4 us -> none  [exchange(): lax.ppermute(value, axis, [(i, i ^ m) for i in range(4)])]
    all_to_all x1, waiting for transfers between devices: 0.01 us -> 12.5 us  [tell(): lax.all_to_all(jnp.broadcast_to(value[None], (count,) + value.shape), axi...]
    all_to_all x1, blocking collectives: 27.2 us -> 18 us  [on_device(): lax.all_to_all(total.reshape(16, 2, 128), ('l', 'h'), 0, 0, tiled=True)]
    all_to_all x1, starting transfers between devices: 4.94 us -> 9.3 us  [on_device(): lax.all_to_all(part.reshape(16, padded // 16, 128), ('y', 'l'), 0, 0, til...]
    unnamed x26 -> x32, local copies, waits for them, and re-layouts: 4.28 us -> 7.69 us
    all_to_all x1, starting transfers between devices: 7.47 us -> 4.75 us  [on_device(): lax.all_to_all(jnp.broadcast_to(part[None], (16,) + part.shape), ('y', 'l...]
  transfers between devices with their start and end apart: 13 -> 8, of which waited for: 7 -> 5; matrix products, arithmetic and copies ran while one was open for 4% -> 4% of each run, Pallas kernels for 6% -> 5%
where the time goes in v5:
time: 213 us; the launch traced here: 212 us
  waiting for transfers between devices  81.2 us (38%)
  starting transfers between devices  39.8 us (19%)
  blocking collectives  32.3 us (15%)
  Pallas kernels  22.4 us (11%)
  local copies, waits for them, and re-layouts  18.2 us (9%)
  between operations  13.6 us (6%)
  other arithmetic  3.61 us (2%)
    all_gather x1, waiting for transfers between devices, on_device(): table = lax.all_gather(picked, ('x', 'h')).reshape(owners * CAP, 128)  63.2 us
    all_to_all x1, blocking collectives, on_device(): lax.all_to_all(total.reshape(16, 2, 128), ('l', 'h'), 0, 0, tiled=True)  18 us
    all_to_all x1, starting transfers between devices, tell(): lax.all_to_all(jnp.broadcast_to(value[None], (count,) + value.shape), axi...  17.8 us
    all_to_all x1, blocking collectives, on_device(): lax.all_to_all(total.reshape(16, 32, 128), ('x', 'y'), 0, 0, tiled=True)  14.3 us
    all_to_all x1, waiting for transfers between devices, tell(): lax.all_to_all(jnp.broadcast_to(value[None], (count,) + value.shape), axi...  12.5 us
    pallas_call x1, Pallas kernels, contract(): pl.pallas_call(functools.partial(main_kernel, half, tokens, features, ste...  11.2 us
    all_to_all x1, starting transfers between devices, on_device(): lax.all_to_all(part.reshape(16, padded // 16, 128), ('y', 'l'), 0, 0, til...  9.3 us
    ppermute x4, starting transfers between devices, swap(): return lax.ppermute(value, 'c', [(0, 1), (1, 0)])  7.89 us
  transfers between devices with their start and end apart: 8, of which 5 were waited for; matrix products, arithmetic and copies ran while one was open for 4% of the time, Pallas kernels for 5%

profile of v5, /device:TPU:8, one launch (start us, length us, event | category | flops | bytes accessed | tf_op | source)
XLA Modules:
  0.0 212.1 jit_solution(7753864056679105775)
XLA Ops:
  6.5 0.0 copy-start
  6.5 0.8 broadcast_subtract_fusion
  7.3 0.4 copy-done
  7.8 0.3 convolution_convert_fusion
  8.1 1.9 collective-permute-start
  10.0 1.7 constant_dynamic-slice_fusion
  11.7 0.0 copy-done.4
  11.7 0.0 copy-done.6
  11.7 0.1 pad_add_fusion.1.where_ref
  11.8 0.2 copy.28
  12.0 0.9 copy.23
  12.9 0.2 copy.27
  13.0 0.8 copy.21
  13.9 3.4 %shard_map.91 = (s32[64,64]{1,0:T(8,128)S(1)}, s32[352,1]{1,0:T(8,128)S(1)}, s32[1]{0:T(128)}) custom-call(s32[2]{0:T(128)S(1)} %pad_add_fusion.1.where_ref, s32[64,64]{1,0:T(8,128)} %ids_ref.1), custom_call_target="tpu_custom_call" | custom-call | tf_op jit(solution)/shard_map/pallas_call | solution.py:64
  17.3 0.0 copy-start.11
  17.3 0.7 copy-done.11
  18.0 0.6 copy-done.14
  18.6 0.0 collective-permute-done
  18.6 0.6 pad_maximum_fusion.1
  19.2 1.1 broadcast_in_dim.26
  20.3 0.6 while.10
  21.0 0.0 copy-start.12
  21.0 1.5 broadcast_in_dim.27
  22.5 17.8 %all-to-all-start.2 = ((bf16[16,64,128]{2,1,0:T(8,128)(2,1)}), bf16[16,64,128]{2,1,0:T(8,128)(2,1)S(1)}, u32[]{:S(2)}, u32[]{:S(2)}) async-start(bf16[16,64,128]{2,1,0:T(8,128)(2,1)} %broadcast_in_dim.27), calls=%async_computation.2 | async-start | bytes 524288 | tf_op jit(solution)/shard_map/all_to_all | solution.py:155
  40.3 0.0 all-gather.3.cloned.1.call-start
  40.3 0.0 copy-done.13
  40.4 1.2 pad_maximum_fusion
  41.6 2.1 %collective-permute-start.1 = (bf16[2752,128]{1,0:T(8,128)(2,1)S(1)}, bf16[2752,128]{1,0:T(8,128)(2,1)S(1)}, u32[]{:S(2)}, u32[]{:S(2)}) collective-permute-start(bf16[2752,128]{1,0:T(8,128)(2,1)S(1)} %pad_maximum_fusion), channel_id=1, source_target_pairs={{0,4},{4,0},{1,5},{5,1},{2,6},{6,2},{3,7},{7,3},{8,12},{12,8},{9,1... | collective-permute-start | bytes 2113544 | tf_op jit(solution)/shard_map/ppermute | solution.py:285
  43.7 0.0 copy-done.12
  43.7 0.1 reduce.2
  43.9 3.5 %gather_fusion.1 = bf16[352,128]{1,0:T(8,128)(2,1)} fusion(bf16[8192,128]{1,0:T(8,128)(2,1)} %param.17, s32[1024]{0:T(1024)S(1)} %pad_clamp_fusion.1), kind=kCustom, calls=%fused_computation.1 | custom fusion | bytes 181632 | tf_op jit(solution)/shard_map/jit(_take)/gather | solution.py:348
  47.4 0.0 all-gather.3.cloned.1.call-update
  47.4 0.0 collective-permute-done.1.rec_ref
  47.4 0.0 copy-done.5
  47.4 0.0 copy-start.7
  47.4 1.0 copy-done.7
  48.4 0.1 shard_map.92.weight_ref
  48.6 12.5 %all-to-all-done.2 = bf16[16,64,128]{2,1,0:T(8,128)(2,1)S(1)} async-done(((bf16[16,64,128]{2,1,0:T(8,128)(2,1)}), bf16[16,64,128]{2,1,0:T(8,128)(2,1)S(1)}, u32[]{:S(2)}, u32[]{:S(2)}) %all-to-all-start.2) | async-done | bytes 262176 | tf_op jit(solution)/shard_map/all_to_all | solution.py:155
  61.2 0.0 copy-start.8
  61.2 1.0 copy-done.8
  62.2 1.2 shard_map.93
  63.4 9.3 %all-to-all-start.3 = ((f32[16,72,128]{2,1,0:T(8,128)}), f32[16,72,128]{2,1,0:T(8,128)S(1)}, u32[]{:S(2)}, u32[]{:S(2)}) async-start(f32[16,72,128]{2,1,0:T(8,128)} %bitcast.13), calls=%async_computation.3 | async-start | bytes 1179648 | tf_op jit(solution)/shard_map/all_to_all | solution.py:374
  72.7 63.2 %all-gather.3.cloned.1.call-done.refs_0_ = bf16[5632,128]{1,0:T(8,128)(2,1)} async-done(((bf16[352,128]{1,0:T(8,128)(2,1)}), bf16[5632,128]{1,0:T(8,128)(2,1)}) %all-gather.3.cloned.1.call-update) | async-done | bytes 1441808 | tf_op jit(solution)/shard_map/all_gather | solution.py:350
  135.9 0.0 all-to-all-done.3
  135.9 0.9 broadcast_in_dim.28
  136.8 4.8 %all-to-all-start.4 = ((f32[16,72,128]{2,1,0:T(8,128)}), f32[16,72,128]{2,1,0:T(8,128)}, u32[]{:S(2)}, u32[]{:S(2)}) async-start(f32[16,72,128]{2,1,0:T(8,128)} %broadcast_in_dim.28), calls=%async_computation.4 | async-start | bytes 1179648 | tf_op jit(solution)/shard_map/all_to_all | solution.py:377
  141.5 0.0 copy-done.15
  141.5 0.0 copy-start.1
  141.6 1.4 copy-done.1
  142.9 6.4 %shard_map.94.own_ref = bf16[4096,128]{1,0:T(8,128)(2,1)S(1)} custom-call(s32[1]{0:T(128)} %get-tuple-element.121.rounds_ref, s32[64,64]{1,0:T(8,128)S(1)} %copy-done.15, bf16[4096,128]{1,0:T(8,128)(2,1)} %get-tuple-element.51.have_ref, bf16[5632,128]{1,0:T(8,128)(2,1)S(1)} %copy-done.1), custom_call_target="tpu_custom_call" | custom-call | tf_op jit(solution)/shard_map/pallas_call | solution.py:139
  149.3 1.9 collective-permute-start.2
  151.2 2.6 %collective-permute-done.2.far_ref = bf16[4096,128]{1,0:T(8,128)(2,1)S(1)} collective-permute-done((bf16[4096,128]{1,0:T(8,128)(2,1)S(1)}, bf16[4096,128]{1,0:T(8,128)(2,1)S(1)}, u32[]{:S(2)}, u32[]{:S(2)}) %collective-permute-start.2) | collective-permute-done | bytes 1048608 | tf_op jit(solution)/shard_map/ppermute | solution.py:285
  153.8 1.0 copy-done.2
  154.8 1.3 all-to-all-done.4
  156.2 1.2 copy-done.3
  157.4 11.2 %shard_map.95 = (f32[512,128]{1,0:T(8,128)S(1)}, f32[512,128]{1,0:T(8,128)S(1)}) custom-call(s32[1]{0:T(128)} %bitcast.5.core_ref, f32[1152,128]{1,0:T(8,128)} %bitcast.14.pre_ref, bf16[256,1792]{1,0:T(8,128)(2,1)S(1)} %shard_map.92.weight_ref, bf16[4096,128]{1,0:T(8,128)(2,1)S(1)} %shard_map.94.own_ref, bf16[4096,128]{1,0:T(8,128)(2,1)S(1)} %copy-done.3), custom_call_target="tpu_custom_call" | custom-call | tf_op jit(solution)/shard_map/pallas_call | solution.py:270
  168.6 0.0 copy-start.16
  168.7 1.9 collective-permute-start.3
  170.6 1.5 collective-permute-done.3
  172.1 14.3 %all_to_all.37 = f32[16,32,128]{2,1,0:T(8,128)S(1)} all-to-all(f32[16,32,128]{2,1,0:T(8,128)S(1)} %bitcast.34), channel_id=1, replica_groups=mesh['x'=4,'h'=4,'y'=4,'c'=2,'l'=4] {'x','y'}, dimensions={0} | all-to-all | bytes 524288 | tf_op jit(solution)/shard_map/all_to_all | solution.py:387
  186.5 18.0 %all_to_all.38 = f32[16,2,128]{2,1,0:T(2,128)S(1)} all-to-all(f32[16,2,128]{2,1,0:T(2,128)S(1)} %bitcast.39), channel_id=1, replica_groups=mesh['x'=4,'h'=4,'y'=4,'c'=2,'l'=4] {'l','h'}, dimensions={0} | all-to-all | bytes 32768 | tf_op jit(solution)/shard_map/all_to_all | solution.py:388
  204.5 0.1 reshape.54
  204.6 0.0 copy-done.16
  204.6 0.6 copy_multiply_fusion
  (17 shorter events, 0.2 us)
Async XLA Ops:
  6.5 1.2 copy-start
  6.5 5.2 %copy-start.4 = (bf16[128,1792]{1,0:T(8,128)(2,1)S(1)}, bf16[128,1792]{1,0:T(8,128)(2,1)}, u32[]{:S(2)}) copy-start(bf16[128,1792]{1,0:T(8,128)(2,1)} %gate_ref.1) | copy-start | bytes 1376260
  6.5 5.2 %copy-start.6 = (bf16[128,1792]{1,0:T(8,128)(2,1)S(1)}, bf16[128,1792]{1,0:T(8,128)(2,1)}, u32[]{:S(2)}) copy-start(bf16[128,1792]{1,0:T(8,128)(2,1)} %up_ref.1) | copy-start | bytes 1376260
  8.1 10.5 %collective-permute-start = (bf16[32,128]{1,0:T(8,128)(2,1)S(1)}, bf16[32,128]{1,0:T(8,128)(2,1)S(1)}, u32[]{:S(2)}, u32[]{:S(2)}) collective-permute-start(bf16[32,128]{1,0:T(8,128)(2,1)S(1)} %convolution_convert_fusion), channel_id=1, source_target_pairs={{0,4},{4,0},{1,5},{5,1},{2,6},{6,2},{3,7},{7,3},{8,12},{12,8},{9,1... | collective-permute-start | bytes 24584 | tf_op jit(solution)/shard_map/ppermute | solution.py:285
  17.3 0.7 copy-start.11
  18.0 0.6 copy-start.14
  20.3 20.0 %copy-start.13 = (bf16[64,128]{1,0:T(8,128)(2,1)S(1)}, bf16[64,128]{1,0:T(8,128)(2,1)}, u32[]{:S(2)}) copy-start(bf16[64,128]{1,0:T(8,128)(2,1)} %x_ref.1) | copy-start | bytes 49156
  21.0 22.7 %copy-start.12 = (s32[352,1]{1,0:T(8,128)S(1)}, s32[352,1]{1,0:T(8,128)}, u32[]{:S(2)}) copy-start(s32[352,1]{1,0:T(8,128)} %copy-done.11) | copy-start | bytes 4228
  22.5 24.9 %copy-start.5 = (bf16[128,1792]{1,0:T(8,128)(2,1)S(1)}, bf16[128,1792]{1,0:T(8,128)(2,1)}, u32[]{:S(2)}) copy-start(bf16[128,1792]{1,0:T(8,128)(2,1)} %gate_ref.1) | copy-start | bytes 1376260
  22.5 38.6 %all-to-all-start.2 = ((bf16[16,64,128]{2,1,0:T(8,128)(2,1)}), bf16[16,64,128]{2,1,0:T(8,128)(2,1)S(1)}, u32[]{:S(2)}, u32[]{:S(2)}) async-start(bf16[16,64,128]{2,1,0:T(8,128)(2,1)} %broadcast_in_dim.27), calls=%async_computation.2 | async-start | bytes 524288 | tf_op jit(solution)/shard_map/all_to_all | solution.py:155
  40.3 95.6 %all-gather.3.cloned.1.call-start = ((), (), s32[]{:S(2)}) async-start(), calls=%async_computation.7 | async-start | bytes 1531904 | tf_op jit(solution)/shard_map/all_gather | solution.py:350
  41.6 5.8 %collective-permute-start.1 = (bf16[2752,128]{1,0:T(8,128)(2,1)S(1)}, bf16[2752,128]{1,0:T(8,128)(2,1)S(1)}, u32[]{:S(2)}, u32[]{:S(2)}) collective-permute-start(bf16[2752,128]{1,0:T(8,128)(2,1)S(1)} %pad_maximum_fusion), channel_id=1, source_target_pairs={{0,4},{4,0},{1,5},{5,1},{2,6},{6,2},{3,7},{7,3},{8,12},{12,8},{9,1... | collective-permute-start | bytes 2113544 | tf_op jit(solution)/shard_map/ppermute | solution.py:285
  47.4 1.0 copy-start.7
  61.2 1.0 copy-start.8
  63.4 72.5 %all-to-all-start.3 = ((f32[16,72,128]{2,1,0:T(8,128)}), f32[16,72,128]{2,1,0:T(8,128)S(1)}, u32[]{:S(2)}, u32[]{:S(2)}) async-start(f32[16,72,128]{2,1,0:T(8,128)} %bitcast.13), calls=%async_computation.3 | async-start | bytes 1179648 | tf_op jit(solution)/shard_map/all_to_all | solution.py:374
  72.7 68.8 %copy-start.15 = (s32[64,64]{1,0:T(8,128)S(1)}, s32[64,64]{1,0:T(8,128)}, u32[]{:S(2)}) copy-start(s32[64,64]{1,0:T(8,128)} %copy-done.14) | copy-start | bytes 49156
  136.8 19.4 %all-to-all-start.4 = ((f32[16,72,128]{2,1,0:T(8,128)}), f32[16,72,128]{2,1,0:T(8,128)}, u32[]{:S(2)}, u32[]{:S(2)}) async-start(f32[16,72,128]{2,1,0:T(8,128)} %broadcast_in_dim.28), calls=%async_computation.4 | async-start | bytes 1179648 | tf_op jit(solution)/shard_map/all_to_all | solution.py:377
  141.5 1.4 copy-start.1
  149.3 4.6 %collective-permute-start.2 = (bf16[4096,128]{1,0:T(8,128)(2,1)S(1)}, bf16[4096,128]{1,0:T(8,128)(2,1)S(1)}, u32[]{:S(2)}, u32[]{:S(2)}) collective-permute-start(bf16[4096,128]{1,0:T(8,128)(2,1)S(1)} %shard_map.94.own_ref), channel_id=1, source_target_pairs={{0,4},{4,0},{1,5},{5,1},{2,6},{6,2},{3,7},{7,3},{8,12},{12,8},{9,1... | collective-permute-start | bytes 3145736 | tf_op jit(solution)/shard_map/ppermute | solution.py:285
  153.8 1.0 copy-start.2
  156.2 1.2 copy-start.3
  168.6 36.0 %copy-start.16 = (f32[16,4]{0,1:T(4,128)S(1)}, f32[16,4]{0,1:T(4,128)}, u32[]{:S(2)}) copy-start(f32[16,4]{0,1:T(4,128)} %param.19) | copy-start | bytes 772
  168.7 3.4 %collective-permute-start.3 = (f32[512,128]{1,0:T(8,128)S(1)}, f32[512,128]{1,0:T(8,128)S(1)}, u32[]{:S(2)}, u32[]{:S(2)}) collective-permute-start(f32[512,128]{1,0:T(8,128)S(1)} %get-tuple-element.60), channel_id=1, source_target_pairs={{0,4},{4,0},{1,5},{5,1},{2,6},{6,2},{3,7},{7,3},{8,12},{12,8},{9,1... | collective-permute-start | bytes 786440 | tf_op jit(solution)/shard_map/ppermute | solution.py:285
Sparse Core Ops, SparseCore 0:
  47.5 88.3 all-gather.2

commit v6 on v5

--- a/solution.py
+++ b/solution.py
@@ -48,7 +48,8 @@
     start = where_ref[1] * CAP
     at = pos.astype(jnp.int32) - start
     here = jnp.logical_and(at >= 0, at < CAP)
-    slot = jnp.where(here, owner * CAP + at, -1)
+    column = lax.bitwise_and(rank, owners - 4)
+    slot = jnp.where(here, lax.bitwise_xor(owner, column) * CAP + at, -1)
     slot_ref[...] = jnp.concatenate([slot[:, :slots], slot[:, slots:]], axis=0)
     rounds_ref[0] = lax.div(jnp.max(pos).astype(jnp.int32), CAP) + 1
     mine = jnp.where(owner == rank, pos - start.astype(F32), -1.0)
@@ -151,10 +152,14 @@
     )(rounds, slot, have, *parts)
 
 
-def tell(value, axis, count):
-    return lax.all_to_all(
-        jnp.broadcast_to(value[None], (count,) + value.shape), axis, 0, 0, tiled=True
-    )
+def exchange(value, axis):
+    return [value] + [
+        lax.ppermute(value, axis, [(i, i ^ m) for i in range(4)]) for m in range(1, 4)
+    ]
+
+
+def tell(value, axis):
+    return lax.all_to_all(jnp.broadcast_to(value[None], (4,) + value.shape), axis, 0, 0, tiled=True)
 
 
 def after(value, other):
@@ -237,15 +242,13 @@
                 grads[to, half + i * 128 : half + (i + 1) * 128] = (row * up_factor).astype(BF16)
         width = nt(grads[...], weight_ref[...])
         high = width.astype(BF16)
-        low = (width - high.astype(F32)).astype(BF16)
         for copy in copies(step):
             copy.wait()
         dec = dec_ref[pl.ds(pl.multiple_of(step * block, block), block), :]
         for y in range(features // 8):
-            part = slice(y * 128, (y + 1) * 128)
-            both = jnp.concatenate([high[part, :], low[part, :]], axis=0)
-            full = nt(dec, both)
-            full = full[:, :128] + full[:, 128:]
+            if y % 2 == 0:
+                pair = nt(dec, high[y * 128 : (y + 2) * 128, :])
+            full = pair[:, (y % 2) * 128 : (y % 2 + 1) * 128]
             sel = full[:64, :]
             for t in range(1, tile):
                 sel = jnp.where(which == t, full[t * 64 : (t + 1) * 64, :], sel)
@@ -323,12 +326,12 @@
         turn, have = carry
         slot_now, rows_now, _ = plan(latent_ids, rank, turn, owners, dec_rows)
         taken = jnp.take(up_decoder, rows_now, axis=0, mode="clip")
-        spread = tell(tell(taken, "h", 4).reshape(4 * CAP, 128), "x", 4)
-        return turn + 1, expand(rounds, slot_now, have, [spread.reshape(owners * CAP, 128)])
+        spread = exchange(tell(taken, "h").reshape(4 * CAP, 128), "x")
+        return turn + 1, expand(rounds, slot_now, have, spread)
 
     nothing = jnp.zeros((tokens * slots, 128), BF16)
     _, have = lax.while_loop(more, another, (jnp.int32(1), nothing))
-    cot = tell(after(chosen, have), ("x", "h"), owners)
+    chosen = tell(after(chosen, have), "x")
 
     def columns(w):
         part = lax.dynamic_slice(w, (0, other * half), (dblk, half))
@@ -347,9 +350,9 @@
 
     picked = jnp.take(up_decoder, rows, axis=0, mode="clip")
 
-    table = lax.all_gather(picked, ("x", "h")).reshape(owners * CAP, 128)
-
-    cot = jnp.sum(after(cot, picked).astype(F32), axis=0).astype(BF16)
+    chosen = jnp.sum(after(chosen, picked).astype(F32), axis=0).astype(BF16)
+    packet = tell(jnp.concatenate([picked, chosen], axis=0), "h")
+    cot = jnp.sum(packet[:, CAP:, :].astype(F32), axis=0).astype(BF16)
     cot = jnp.concatenate([cot[:features], cot[features:]], axis=1)
 
     vmem = pl.BlockSpec(memory_space=pltpu.VMEM)
@@ -371,14 +374,16 @@
         out_specs=vmem,
         compiler_params=pltpu.CompilerParams(vmem_limit_bytes=8 * MIB),
     )(core_arg, mlp_input, cot, weight, down_weight, rec)
+    part, column = lax.optimization_barrier((part, packet[:, :CAP, :].reshape(4 * CAP, 128)))
     part = lax.all_to_all(part.reshape(16, padded // 16, 128), ("y", "l"), 0, 0, tiled=True)
-    part = jnp.sum(after(part, table), axis=0)
-    slot = after(slot, part)
+    parts = exchange(column, "x")
+    part = jnp.sum(part, axis=0)
+    part, slot, parts[1], parts[2] = lax.optimization_barrier((part, slot, parts[1], parts[2]))
     pre = lax.all_to_all(
         jnp.broadcast_to(part[None], (16,) + part.shape), ("y", "l"), 0, 0, tiled=True
     ).reshape(padded, 128)
 
-    dec = expand(rounds, slot, have, [table])
+    dec = expand(rounds, slot, have, parts)
     dec_far = swap(dec)
 
     mine, theirs = contract(core_arg, pre, weight, dec, dec_far, half, tokens, features)

time: 213 us -> 171 us (0.80)
  waiting for transfers between devices: 81.2 us -> 40.3 us
  starting transfers between devices: 39.8 us -> 57.2 us
  between operations: 13.6 us -> 0.32 us
  local copies, waits for them, and re-layouts: 18.2 us -> 15.3 us
  Pallas kernels: 22.4 us -> 19.6 us
    all_gather x1 -> x0, waiting for transfers between devices: 63.2 us -> none  [on_device(): table = lax.all_gather(picked, ('x', 'h')).reshape(owners * CAP, 128)]
    ppermute x0 -> x3, waiting for transfers between devices: none -> 10.5 us  [exchange(): lax.ppermute(value, axis, [(i, i ^ m) for i in range(4)])]
    ppermute x0 -> x3, starting transfers between devices: none -> 10.4 us  [exchange(): lax.ppermute(value, axis, [(i, i ^ m) for i in range(4)])]
    all_to_all x1, waiting for transfers between devices: 0.01 us -> 5.75 us  [on_device(): lax.all_to_all(part.reshape(16, padded // 16, 128), ('y', 'l'), 0, 0, til...]
    all_to_all x1 -> x2, waiting for transfers between devices: 12.5 us -> 17.9 us  [tell(): lax.all_to_all(jnp.broadcast_to(value[None], (4,) + value.shape), axis, 0...]
    all_to_all x1, starting transfers between devices: 9.3 us -> 12.1 us  [on_device(): lax.all_to_all(part.reshape(16, padded // 16, 128), ('y', 'l'), 0, 0, til...]
    all_to_all x1, starting transfers between devices: 4.75 us -> 7.52 us  [on_device(): lax.all_to_all(jnp.broadcast_to(part[None], (16,) + part.shape), ('y', 'l...]
    pallas_call x1, Pallas kernels: 11.2 us -> 8.7 us  [contract(): pl.pallas_call(functools.partial(main_kernel, half, tokens, features, ste...]
  transfers between devices with their start and end apart: 8 -> 11, of which waited for: 5 -> 8; matrix products, arithmetic and copies ran while one was open for 4% -> 3% of each run, Pallas kernels for 5% -> 6%
where the time goes in v6:
time: 171 us; the launch traced here: 170 us
  starting transfers between devices  57.2 us (33%)
  waiting for transfers between devices  40.3 us (24%)
  blocking collectives  32.6 us (19%)
  Pallas kernels  19.6 us (11%)
  local copies, waits for them, and re-layouts  15.3 us (9%)
  other arithmetic  3.7 us (2%)
    all_to_all x1, blocking collectives, on_device(): lax.all_to_all(total.reshape(16, 2, 128), ('l', 'h'), 0, 0, tiled=True)  19.6 us
    all_to_all x2, starting transfers between devices, tell(): lax.all_to_all(jnp.broadcast_to(value[None], (4,) + value.shape), axis, 0...  19.4 us
    all_to_all x2, waiting for transfers between devices, tell(): lax.all_to_all(jnp.broadcast_to(value[None], (4,) + value.shape), axis, 0...  17.9 us
    all_to_all x1, blocking collectives, on_device(): lax.all_to_all(total.reshape(16, 32, 128), ('x', 'y'), 0, 0, tiled=True)  13.1 us
    all_to_all x1, starting transfers between devices, on_device(): lax.all_to_all(part.reshape(16, padded // 16, 128), ('y', 'l'), 0, 0, til...  12.1 us
    ppermute x3, waiting for transfers between devices, exchange(): lax.ppermute(value, axis, [(i, i ^ m) for i in range(4)])  10.5 us
    ppermute x3, starting transfers between devices, exchange(): lax.ppermute(value, axis, [(i, i ^ m) for i in range(4)])  10.4 us
    pallas_call x1, Pallas kernels, contract(): pl.pallas_call(functools.partial(main_kernel, half, tokens, features, ste...  8.7 us
  transfers between devices with their start and end apart: 11, of which 8 were waited for; matrix products, arithmetic and copies ran while one was open for 3% of the time, Pallas kernels for 6%

profile of v6, /device:TPU:8, one launch (start us, length us, event | category | flops | bytes accessed | tf_op | source)
XLA Modules:
  0.0 169.9 jit_solution(7500206556298180474)
XLA Ops:
  0.0 0.0 copy-start
  0.0 0.7 broadcast_subtract_fusion
  0.8 0.5 copy-done
  1.2 0.3 convolution_convert_fusion
  1.6 1.9 %collective-permute-start.3 = (bf16[32,128]{1,0:T(8,128)(2,1)S(1)}, bf16[32,128]{1,0:T(8,128)(2,1)S(1)}, u32[]{:S(2)}, u32[]{:S(2)}) collective-permute-start(bf16[32,128]{1,0:T(8,128)(2,1)S(1)} %convolution_convert_fusion), channel_id=1, source_target_pairs={{0,4},{4,0},{1,5},{5,1},{2,6},{6,2},{3,7},{7,3},{8,12},{12,8},{9,1... | collective-permute-start | bytes 24584 | tf_op jit(solution)/shard_map/ppermute | solution.py:288
  3.5 0.1 pad_add_fusion.1.where_ref
  3.6 3.4 %shard_map.91 = (s32[64,64]{1,0:T(8,128)S(1)}, s32[352,1]{1,0:T(8,128)S(1)}, s32[1]{0:T(128)}) custom-call(s32[2]{0:T(128)S(1)} %pad_add_fusion.1.where_ref, s32[64,64]{1,0:T(8,128)} %ids_ref.1), custom_call_target="tpu_custom_call" | custom-call | tf_op jit(solution)/shard_map/pallas_call | solution.py:65
  7.0 0.1 reduce.3
  7.1 0.0 collective-permute-done.3
  7.2 1.1 broadcast_in_dim.21
  8.3 0.0 copy-done.13
  8.3 0.6 while.10
  8.9 0.0 copy-start.3
  8.9 0.0 copy-start.4
  8.9 0.6 broadcast_in_dim.22
  9.5 4.3 %all-to-all-start.1 = ((bf16[4,64,128]{2,1,0:T(8,128)(2,1)}), bf16[4,64,128]{2,1,0:T(8,128)(2,1)S(1)}, u32[]{:S(2)}, u32[]{:S(2)}) async-start(bf16[4,64,128]{2,1,0:T(8,128)(2,1)} %broadcast_in_dim.22), calls=%async_computation.1 | async-start | bytes 131072 | tf_op jit(solution)/shard_map/all_to_all | solution.py:162
  13.8 3.0 %gather_fusion.1 = bf16[352,128]{1,0:T(8,128)(2,1)S(1)} fusion(bf16[8192,128]{1,0:T(8,128)(2,1)} %param.17, s32[1024]{0:T(1024)S(1)} %pad_clamp_fusion.1), kind=kCustom, calls=%fused_computation.1 | custom fusion | bytes 181632 | tf_op jit(solution)/shard_map/jit(_take)/gather | solution.py:351
  16.9 2.6 %all-to-all-done.1 = bf16[4,64,128]{2,1,0:T(8,128)(2,1)S(1)} async-done(((bf16[4,64,128]{2,1,0:T(8,128)(2,1)}), bf16[4,64,128]{2,1,0:T(8,128)(2,1)S(1)}, u32[]{:S(2)}, u32[]{:S(2)}) %all-to-all-start.1) | async-done | bytes 65568 | tf_op jit(solution)/shard_map/all_to_all | solution.py:162
  19.5 0.8 broadcast_in_dim.23
  20.3 15.1 %all-to-all-start.2 = ((bf16[4,416,128]{2,1,0:T(8,128)(2,1)}), bf16[4,416,128]{2,1,0:T(8,128)(2,1)}, u32[]{:S(2)}, u32[]{:S(2)}) async-start(bf16[4,416,128]{2,1,0:T(8,128)(2,1)} %broadcast_in_dim.23), calls=%async_computation.2 | async-start | bytes 851968 | tf_op jit(solution)/shard_map/all_to_all | solution.py:162
  35.4 0.0 copy-done.4
  35.4 0.0 copy-start.12
  35.5 0.2 copy.28
  35.6 0.2 copy.23
  35.8 0.2 copy.27
  36.0 0.2 copy.21
  36.2 0.2 copy-done.6
  36.5 1.9 %collective-permute-start.4 = (bf16[2752,128]{1,0:T(8,128)(2,1)S(1)}, bf16[2752,128]{1,0:T(8,128)(2,1)S(1)}, u32[]{:S(2)}, u32[]{:S(2)}) collective-permute-start(bf16[2752,128]{1,0:T(8,128)(2,1)S(1)} %pad_maximum_fusion), channel_id=1, source_target_pairs={{0,4},{4,0},{1,5},{5,1},{2,6},{6,2},{3,7},{7,3},{8,12},{12,8},{9,1... | collective-permute-start | bytes 2113544 | tf_op jit(solution)/shard_map/ppermute | solution.py:288
  38.4 2.1 %collective-permute-done.4.rec_ref = bf16[2752,128]{1,0:T(8,128)(2,1)S(1)} collective-permute-done((bf16[2752,128]{1,0:T(8,128)(2,1)S(1)}, bf16[2752,128]{1,0:T(8,128)(2,1)S(1)}, u32[]{:S(2)}, u32[]{:S(2)}) %collective-permute-start.4) | collective-permute-done | bytes 704544 | tf_op jit(solution)/shard_map/ppermute | solution.py:288
  40.6 1.0 copy-done.5
  41.6 0.1 shard_map.92.weight_ref
  41.7 15.3 %all-to-all-done.2 = bf16[4,416,128]{2,1,0:T(8,128)(2,1)} async-done(((bf16[4,416,128]{2,1,0:T(8,128)(2,1)}), bf16[4,416,128]{2,1,0:T(8,128)(2,1)}, u32[]{:S(2)}, u32[]{:S(2)}) %all-to-all-start.2) | async-done | bytes 426016 | tf_op jit(solution)/shard_map/all_to_all | solution.py:162
  57.0 0.9 slice_reduce_fusion
  57.8 1.0 slice.23
  58.9 0.0 copy-start.7
  58.9 1.0 copy-done.7
  59.9 1.2 shard_map.93
  61.1 12.1 %all-to-all-start.3 = ((f32[16,72,128]{2,1,0:T(8,128)}), f32[16,72,128]{2,1,0:T(8,128)}, u32[]{:S(2)}, u32[]{:S(2)}) async-start(f32[16,72,128]{2,1,0:T(8,128)} %bitcast.13), calls=%async_computation.3 | async-start | bytes 1179648 | tf_op jit(solution)/shard_map/all_to_all | solution.py:378
  73.2 2.6 %collective-permute-start.5 = (bf16[1408,128]{1,0:T(8,128)(2,1)S(1)}, bf16[1408,128]{1,0:T(8,128)(2,1)S(1)}, u32[]{:S(2)}, u32[]{:S(2)}) collective-permute-start(bf16[1408,128]{1,0:T(8,128)(2,1)S(1)} %bitcast.34), channel_id=1, source_target_pairs={{0,128},{128,0},{256,384},{384,256},{1,129},{129,1},{257,385},{385... | collective-permute-start | bytes 1081352 | tf_op jit(solution)/shard_map/ppermute | solution.py:157
  75.8 4.2 %collective-permute-start.6 = (bf16[1408,128]{1,0:T(8,128)(2,1)S(1)}, bf16[1408,128]{1,0:T(8,128)(2,1)S(1)}, u32[]{:S(2)}, u32[]{:S(2)}) collective-permute-start(bf16[1408,128]{1,0:T(8,128)(2,1)S(1)} %bitcast.35), channel_id=1, source_target_pairs={{0,256},{128,384},{256,0},{384,128},{1,257},{129,385},{257,1},{385... | collective-permute-start | bytes 1081352 | tf_op jit(solution)/shard_map/ppermute | solution.py:157
  80.0 5.8 %all-to-all-done.3 = f32[16,72,128]{2,1,0:T(8,128)} async-done(((f32[16,72,128]{2,1,0:T(8,128)}), f32[16,72,128]{2,1,0:T(8,128)}, u32[]{:S(2)}, u32[]{:S(2)}) %all-to-all-start.3) | async-done | bytes 589856 | tf_op jit(solution)/shard_map/all_to_all | solution.py:378
  85.8 1.1 reduce_sum.53
  86.9 0.0 collective-permute-done.5.refs_1_
  86.9 3.6 %collective-permute-done.6.refs_2_ = bf16[1408,128]{1,0:T(8,128)(2,1)S(1)} collective-permute-done((bf16[1408,128]{1,0:T(8,128)(2,1)S(1)}, bf16[1408,128]{1,0:T(8,128)(2,1)S(1)}, u32[]{:S(2)}, u32[]{:S(2)}) %collective-permute-start.6) | collective-permute-done | bytes 360480 | tf_op jit(solution)/shard_map/ppermute | solution.py:157
  90.5 0.9 broadcast_in_dim.24
  91.4 7.5 %all-to-all-start.4 = ((f32[16,72,128]{2,1,0:T(8,128)}), f32[16,72,128]{2,1,0:T(8,128)}, u32[]{:S(2)}, u32[]{:S(2)}) async-start(f32[16,72,128]{2,1,0:T(8,128)} %broadcast_in_dim.24), calls=%async_computation.4 | async-start | bytes 1179648 | tf_op jit(solution)/shard_map/all_to_all | solution.py:382
  98.9 3.6 %collective-permute-start.7 = (bf16[1408,128]{1,0:T(8,128)(2,1)S(1)}, bf16[1408,128]{1,0:T(8,128)(2,1)S(1)}, u32[]{:S(2)}, u32[]{:S(2)}) collective-permute-start(bf16[1408,128]{1,0:T(8,128)(2,1)S(1)} %bitcast.36), channel_id=1, source_target_pairs={{0,384},{128,256},{256,128},{384,0},{1,385},{129,257},{257,129},{3... | collective-permute-start | bytes 1081352 | tf_op jit(solution)/shard_map/ppermute | solution.py:157
  102.6 6.9 %collective-permute-done.7.refs_3_ = bf16[1408,128]{1,0:T(8,128)(2,1)S(1)} collective-permute-done((bf16[1408,128]{1,0:T(8,128)(2,1)S(1)}, bf16[1408,128]{1,0:T(8,128)(2,1)S(1)}, u32[]{:S(2)}, u32[]{:S(2)}) %collective-permute-start.7) | collective-permute-done | bytes 360480 | tf_op jit(solution)/shard_map/ppermute | solution.py:157
  109.5 1.0 copy-done.9
  110.5 1.0 copy-done.11
  111.4 6.1 %shard_map.94.own_ref = bf16[4096,128]{1,0:T(8,128)(2,1)S(1)} custom-call(s32[1]{0:T(128)} %get-tuple-element.129.rounds_ref, s32[64,64]{1,0:T(8,128)S(1)} %get-tuple-element.64.slot_ref, bf16[4096,128]{1,0:T(8,128)(2,1)} %get-tuple-element.56.have_ref, bf16[1408,128]{1,0:T(8,128)(2,1)S(1)} %bitcast.37, bf16[1408,128]{1,0:T(8,128)(2,1)S(1)} %copy-done.9, ...), custom_call_target="tpu_custom_call" | custom-call | tf_op jit(solution)/shard_map/pallas_call | solution.py:140
  117.6 1.9 %collective-permute-start.8 = (bf16[4096,128]{1,0:T(8,128)(2,1)S(1)}, bf16[4096,128]{1,0:T(8,128)(2,1)S(1)}, u32[]{:S(2)}, u32[]{:S(2)}) collective-permute-start(bf16[4096,128]{1,0:T(8,128)(2,1)S(1)} %shard_map.94.own_ref), channel_id=1, source_target_pairs={{0,4},{4,0},{1,5},{5,1},{2,6},{6,2},{3,7},{7,3},{8,12},{12,8},{9,1... | collective-permute-start | bytes 3145736 | tf_op jit(solution)/shard_map/ppermute | solution.py:288
  119.5 2.6 %collective-permute-done.8.far_ref = bf16[4096,128]{1,0:T(8,128)(2,1)S(1)} collective-permute-done((bf16[4096,128]{1,0:T(8,128)(2,1)S(1)}, bf16[4096,128]{1,0:T(8,128)(2,1)S(1)}, u32[]{:S(2)}, u32[]{:S(2)}) %collective-permute-start.8) | collective-permute-done | bytes 1048608 | tf_op jit(solution)/shard_map/ppermute | solution.py:288
  122.1 1.0 copy-done.1
  123.1 0.0 all-to-all-done.4
  123.1 1.2 copy-done.2
  124.4 8.7 %shard_map.95 = (f32[512,128]{1,0:T(8,128)S(1)}, f32[512,128]{1,0:T(8,128)S(1)}) custom-call(s32[1]{0:T(128)} %bitcast.4.core_ref, f32[1152,128]{1,0:T(8,128)} %bitcast.14.pre_ref, bf16[256,1792]{1,0:T(8,128)(2,1)S(1)} %shard_map.92.weight_ref, bf16[4096,128]{1,0:T(8,128)(2,1)S(1)} %shard_map.94.own_ref, bf16[4096,128]{1,0:T(8,128)(2,1)S(1)} %copy-done.2), custom_call_target="tpu_custom_call" | custom-call | tf_op jit(solution)/shard_map/pallas_call | solution.py:273
  133.1 0.0 copy-start.14
  133.1 2.0 %collective-permute-start.9 = (f32[512,128]{1,0:T(8,128)S(1)}, f32[512,128]{1,0:T(8,128)S(1)}, u32[]{:S(2)}, u32[]{:S(2)}) collective-permute-start(f32[512,128]{1,0:T(8,128)S(1)} %get-tuple-element.68), channel_id=1, source_target_pairs={{0,4},{4,0},{1,5},{5,1},{2,6},{6,2},{3,7},{7,3},{8,12},{12,8},{9,1... | collective-permute-start | bytes 786440 | tf_op jit(solution)/shard_map/ppermute | solution.py:288
  135.1 1.4 collective-permute-done.9
  136.5 13.1 %all_to_all.36 = f32[16,32,128]{2,1,0:T(8,128)S(1)} all-to-all(f32[16,32,128]{2,1,0:T(8,128)S(1)} %bitcast.38), channel_id=1, replica_groups=mesh['x'=4,'h'=4,'y'=4,'c'=2,'l'=4] {'x','y'}, dimensions={0} | all-to-all | bytes 524288 | tf_op jit(solution)/shard_map/all_to_all | solution.py:392
  149.7 19.6 %all_to_all.37 = f32[16,2,128]{2,1,0:T(2,128)S(1)} all-to-all(f32[16,2,128]{2,1,0:T(2,128)S(1)} %bitcast.43), channel_id=1, replica_groups=mesh['x'=4,'h'=4,'y'=4,'c'=2,'l'=4] {'l','h'}, dimensions={0} | all-to-all | bytes 32768 | tf_op jit(solution)/shard_map/all_to_all | solution.py:393
  169.2 0.1 reshape.53
  169.3 0.6 copy_multiply_fusion
  (26 shorter events, 0.3 us)
Async XLA Ops:
  0.0 1.2 copy-start
  0.0 8.3 %copy-start.13 = (s32[64,64]{1,0:T(8,128)S(1)}, s32[64,64]{1,0:T(8,128)}, u32[]{:S(2)}) copy-start(s32[64,64]{1,0:T(8,128)} %ids_ref.1) | copy-start | bytes 49156
  1.6 5.6 %collective-permute-start.3 = (bf16[32,128]{1,0:T(8,128)(2,1)S(1)}, bf16[32,128]{1,0:T(8,128)(2,1)S(1)}, u32[]{:S(2)}, u32[]{:S(2)}) collective-permute-start(bf16[32,128]{1,0:T(8,128)(2,1)S(1)} %convolution_convert_fusion), channel_id=1, source_target_pairs={{0,4},{4,0},{1,5},{5,1},{2,6},{6,2},{3,7},{7,3},{8,12},{12,8},{9,1... | collective-permute-start | bytes 24584 | tf_op jit(solution)/shard_map/ppermute | solution.py:288
  8.9 26.5 %copy-start.3 = (bf16[128,1792]{1,0:T(8,128)(2,1)S(1)}, bf16[128,1792]{1,0:T(8,128)(2,1)}, u32[]{:S(2)}) copy-start(bf16[128,1792]{1,0:T(8,128)(2,1)} %gate_ref.1) | copy-start | bytes 1376260
  8.9 26.5 %copy-start.4 = (bf16[128,1792]{1,0:T(8,128)(2,1)S(1)}, bf16[128,1792]{1,0:T(8,128)(2,1)}, u32[]{:S(2)}) copy-start(bf16[128,1792]{1,0:T(8,128)(2,1)} %up_ref.1) | copy-start | bytes 1376260
  9.5 9.9 %all-to-all-start.1 = ((bf16[4,64,128]{2,1,0:T(8,128)(2,1)}), bf16[4,64,128]{2,1,0:T(8,128)(2,1)S(1)}, u32[]{:S(2)}, u32[]{:S(2)}) async-start(bf16[4,64,128]{2,1,0:T(8,128)(2,1)} %broadcast_in_dim.22), calls=%async_computation.1 | async-start | bytes 131072 | tf_op jit(solution)/shard_map/all_to_all | solution.py:162
  20.3 36.7 %all-to-all-start.2 = ((bf16[4,416,128]{2,1,0:T(8,128)(2,1)}), bf16[4,416,128]{2,1,0:T(8,128)(2,1)}, u32[]{:S(2)}, u32[]{:S(2)}) async-start(bf16[4,416,128]{2,1,0:T(8,128)(2,1)} %broadcast_in_dim.23), calls=%async_computation.2 | async-start | bytes 851968 | tf_op jit(solution)/shard_map/all_to_all | solution.py:162
  35.4 1.0 copy-start.6
  35.4 1.0 copy-start.12
  36.5 4.1 %collective-permute-start.4 = (bf16[2752,128]{1,0:T(8,128)(2,1)S(1)}, bf16[2752,128]{1,0:T(8,128)(2,1)S(1)}, u32[]{:S(2)}, u32[]{:S(2)}) collective-permute-start(bf16[2752,128]{1,0:T(8,128)(2,1)S(1)} %pad_maximum_fusion), channel_id=1, source_target_pairs={{0,4},{4,0},{1,5},{5,1},{2,6},{6,2},{3,7},{7,3},{8,12},{12,8},{9,1... | collective-permute-start | bytes 2113544 | tf_op jit(solution)/shard_map/ppermute | solution.py:288
  40.6 1.0 copy-start.5
  58.9 1.0 copy-start.7
  61.1 24.7 %all-to-all-start.3 = ((f32[16,72,128]{2,1,0:T(8,128)}), f32[16,72,128]{2,1,0:T(8,128)}, u32[]{:S(2)}, u32[]{:S(2)}) async-start(f32[16,72,128]{2,1,0:T(8,128)} %bitcast.13), calls=%async_computation.3 | async-start | bytes 1179648 | tf_op jit(solution)/shard_map/all_to_all | solution.py:378
  73.2 13.7 %collective-permute-start.5 = (bf16[1408,128]{1,0:T(8,128)(2,1)S(1)}, bf16[1408,128]{1,0:T(8,128)(2,1)S(1)}, u32[]{:S(2)}, u32[]{:S(2)}) collective-permute-start(bf16[1408,128]{1,0:T(8,128)(2,1)S(1)} %bitcast.34), channel_id=1, source_target_pairs={{0,128},{128,0},{256,384},{384,256},{1,129},{129,1},{257,385},{385... | collective-permute-start | bytes 1081352 | tf_op jit(solution)/shard_map/ppermute | solution.py:157
  75.8 14.7 %collective-permute-start.6 = (bf16[1408,128]{1,0:T(8,128)(2,1)S(1)}, bf16[1408,128]{1,0:T(8,128)(2,1)S(1)}, u32[]{:S(2)}, u32[]{:S(2)}) collective-permute-start(bf16[1408,128]{1,0:T(8,128)(2,1)S(1)} %bitcast.35), channel_id=1, source_target_pairs={{0,256},{128,384},{256,0},{384,128},{1,257},{129,385},{257,1},{385... | collective-permute-start | bytes 1081352 | tf_op jit(solution)/shard_map/ppermute | solution.py:157
  86.9 15.7 %copy-start.8 = (bf16[1408,128]{1,0:T(8,128)(2,1)}, bf16[1408,128]{1,0:T(8,128)(2,1)S(1)}, u32[]{:S(2)}) copy-start(bf16[1408,128]{1,0:T(8,128)(2,1)S(1)} %collective-permute-done.5.refs_1_) | copy-start | bytes 1081348
  90.5 12.1 %copy-start.10 = (bf16[1408,128]{1,0:T(8,128)(2,1)}, bf16[1408,128]{1,0:T(8,128)(2,1)S(1)}, u32[]{:S(2)}) copy-start(bf16[1408,128]{1,0:T(8,128)(2,1)S(1)} %collective-permute-done.6.refs_2_) | copy-start | bytes 1081348
  91.4 31.7 %all-to-all-start.4 = ((f32[16,72,128]{2,1,0:T(8,128)}), f32[16,72,128]{2,1,0:T(8,128)}, u32[]{:S(2)}, u32[]{:S(2)}) async-start(f32[16,72,128]{2,1,0:T(8,128)} %broadcast_in_dim.24), calls=%async_computation.4 | async-start | bytes 1179648 | tf_op jit(solution)/shard_map/all_to_all | solution.py:382
  98.9 10.5 %collective-permute-start.7 = (bf16[1408,128]{1,0:T(8,128)(2,1)S(1)}, bf16[1408,128]{1,0:T(8,128)(2,1)S(1)}, u32[]{:S(2)}, u32[]{:S(2)}) collective-permute-start(bf16[1408,128]{1,0:T(8,128)(2,1)S(1)} %bitcast.36), channel_id=1, source_target_pairs={{0,384},{128,256},{256,128},{384,0},{1,385},{129,257},{257,129},{3... | collective-permute-start | bytes 1081352 | tf_op jit(solution)/shard_map/ppermute | solution.py:157
  109.5 1.0 copy-start.9
  110.5 1.0 copy-start.11
  117.6 4.6 %collective-permute-start.8 = (bf16[4096,128]{1,0:T(8,128)(2,1)S(1)}, bf16[4096,128]{1,0:T(8,128)(2,1)S(1)}, u32[]{:S(2)}, u32[]{:S(2)}) collective-permute-start(bf16[4096,128]{1,0:T(8,128)(2,1)S(1)} %shard_map.94.own_ref), channel_id=1, source_target_pairs={{0,4},{4,0},{1,5},{5,1},{2,6},{6,2},{3,7},{7,3},{8,12},{12,8},{9,1... | collective-permute-start | bytes 3145736 | tf_op jit(solution)/shard_map/ppermute | solution.py:288
  122.1 1.0 copy-start.1
  123.1 1.2 copy-start.2
  133.1 36.3 %copy-start.14 = (f32[16,4]{0,1:T(4,128)S(1)}, f32[16,4]{0,1:T(4,128)}, u32[]{:S(2)}) copy-start(f32[16,4]{0,1:T(4,128)} %param.19) | copy-start | bytes 772
  133.1 3.4 %collective-permute-start.9 = (f32[512,128]{1,0:T(8,128)S(1)}, f32[512,128]{1,0:T(8,128)S(1)}, u32[]{:S(2)}, u32[]{:S(2)}) collective-permute-start(f32[512,128]{1,0:T(8,128)S(1)} %get-tuple-element.68), channel_id=1, source_target_pairs={{0,4},{4,0},{1,5},{5,1},{2,6},{6,2},{3,7},{7,3},{8,12},{12,8},{9,1... | collective-permute-start | bytes 786440 | tf_op jit(solution)/shard_map/ppermute | solution.py:288

commit v7 on v6

--- a/solution.py
+++ b/solution.py
@@ -22,7 +22,7 @@
     return lax.dot_general(a, b, (((1,), (0,)), ((), ())), preferred_element_type=F32)
 
 
-def plan_kernel(owners, dec_rows, where_ref, ids_ref, slot_ref, list_ref, rounds_ref):
+def plan_kernel(owners, dec_rows, where_ref, ids_ref, slot_ref, here_ref, list_ref, rounds_ref):
     tokens, slots = ids_ref.shape
     ids = ids_ref[...]
     ids = jnp.concatenate([ids[: tokens // 2], ids[tokens // 2 :]], axis=1)
@@ -48,9 +48,10 @@
     start = where_ref[1] * CAP
     at = pos.astype(jnp.int32) - start
     here = jnp.logical_and(at >= 0, at < CAP)
-    column = lax.bitwise_and(rank, owners - 4)
-    slot = jnp.where(here, lax.bitwise_xor(owner, column) * CAP + at, -1)
+    slot = jnp.where(here, lax.bitwise_xor(owner, where_ref[2]) * CAP + at, 0)
     slot_ref[...] = jnp.concatenate([slot[:, :slots], slot[:, slots:]], axis=0)
+    here = here.astype(jnp.int32)
+    here_ref[...] = jnp.concatenate([here[:, :slots], here[:, slots:]], axis=0)
     rounds_ref[0] = lax.div(jnp.max(pos).astype(jnp.int32), CAP) + 1
     mine = jnp.where(owner == rank, pos - start.astype(F32), -1.0)
     local = (ids - rank * dec_rows).astype(F32)
@@ -61,10 +62,11 @@
     list_ref[...] = jnp.sum(acc, axis=1, keepdims=True).astype(jnp.int32)
 
 
-def plan(ids, rank, turn, owners, dec_rows):
-    slot, rows, rounds = pl.pallas_call(
+def plan(ids, rank, turn, flip, owners, dec_rows):
+    slot, here, rows, rounds = pl.pallas_call(
         functools.partial(plan_kernel, owners, dec_rows),
         out_shape=(
+            jax.ShapeDtypeStruct(ids.shape, jnp.int32),
             jax.ShapeDtypeStruct(ids.shape, jnp.int32),
             jax.ShapeDtypeStruct((CAP, 1), jnp.int32),
             jax.ShapeDtypeStruct((1,), jnp.int32),
@@ -76,15 +78,16 @@
         out_specs=(
             pl.BlockSpec(memory_space=pltpu.VMEM),
             pl.BlockSpec(memory_space=pltpu.VMEM),
+            pl.BlockSpec(memory_space=pltpu.VMEM),
             pl.BlockSpec(memory_space=pltpu.SMEM),
         ),
         compiler_params=pltpu.CompilerParams(vmem_limit_bytes=4 * MIB),
-    )(jnp.stack([rank, turn]).astype(jnp.int32), ids)
-    return slot, rows.reshape(-1), rounds
-
-
-def expand_kernel(rounds_ref, slot_ref, have_ref, *refs):
-    parts, (out_ref, table, block, old, sem) = refs[:-5], refs[-5:]
+    )(jnp.stack([rank, turn, flip]).astype(jnp.int32), ids)
+    return slot, here, rows.reshape(-1), rounds[0]
+
+
+def expand_kernel(slot_ref, *refs):
+    parts, (out_ref, table, block) = refs[:-3], refs[-3:]
     size = parts[0].shape[0]
     piece = 128
 
@@ -97,59 +100,33 @@
     lax.fori_loop(0, size // piece, widen, 0)
     tokens, slots = slot_ref.shape
 
-    def place(low, r, high):
-        return low * (slots // 2) + r * 2 + high, r * 4 + high * 2 + low
-
-    order = [place(low, r, high) for low in range(2) for r in range(slots // 4) for high in range(2)]
-
     def token(t, carry):
-        for to, k in order:
-            block[to : to + 1, :] = table[pl.ds(slot_ref[t, k], 1), :]
+        for low in range(2):
+            for r in range(slots // 4):
+                for high in range(2):
+                    src = slot_ref[t, r * 4 + high * 2 + low]
+                    to = low * (slots // 2) + r * 2 + high
+                    block[to : to + 1, :] = table[pl.ds(src, 1), :]
         out_ref[pl.ds(pl.multiple_of(t * slots, slots), slots), :] = block[...].astype(BF16)
         return carry
 
-    def merged(t, carry):
-        rows = pl.ds(pl.multiple_of(t * slots, slots), slots)
-        copy = pltpu.make_async_copy(have_ref.at[rows], old, sem)
-        copy.start()
-        copy.wait()
-        block[...] = old[...].astype(F32)
-        for to, k in order:
-            src = slot_ref[t, k]
-
-            @pl.when(src >= 0)
-            def _():
-                block[to : to + 1, :] = table[pl.ds(src, 1), :]
-
-        out_ref[rows, :] = block[...].astype(BF16)
-        return carry
-
-    @pl.when(rounds_ref[0] == 1)
-    def _():
-        lax.fori_loop(0, tokens, token, 0)
-
-    @pl.when(rounds_ref[0] > 1)
-    def _():
-        lax.fori_loop(0, tokens, merged, 0)
-
-
-def expand(rounds, slot, have, parts):
+    lax.fori_loop(0, tokens, token, 0)
+
+
+def expand(slot, parts):
     size = parts[0].shape[0]
-    smem = pl.BlockSpec(memory_space=pltpu.SMEM)
     vmem = pl.BlockSpec(memory_space=pltpu.VMEM)
     return pl.pallas_call(
         expand_kernel,
-        out_shape=jax.ShapeDtypeStruct(have.shape, BF16),
-        in_specs=[smem, smem, pl.BlockSpec(memory_space=pl.ANY)] + [vmem] * len(parts),
+        out_shape=jax.ShapeDtypeStruct((slot.shape[0] * slot.shape[1], 128), BF16),
+        in_specs=[pl.BlockSpec(memory_space=pltpu.SMEM)] + [vmem] * len(parts),
         out_specs=vmem,
         scratch_shapes=[
             pltpu.VMEM((len(parts) * size, 128), F32),
             pltpu.VMEM((slot.shape[1], 128), F32),
-            pltpu.VMEM((slot.shape[1], 128), BF16),
-            pltpu.SemaphoreType.DMA,
         ],
         compiler_params=pltpu.CompilerParams(vmem_limit_bytes=12 * MIB),
-    )(rounds, slot, have, *parts)
+    )(slot, *parts)
 
 
 def exchange(value, axis):
@@ -160,10 +137,6 @@
 
 def tell(value, axis):
     return lax.all_to_all(jnp.broadcast_to(value[None], (4,) + value.shape), axis, 0, 0, tiled=True)
-
-
-def after(value, other):
-    return lax.optimization_barrier((value, other))[0]
 
 
 def weight_kernel(half, core_ref, gate_ref, up_ref, rec_ref, out_ref):
@@ -313,25 +286,9 @@
     local = feature_ids - rank * enc_rows
     picker = (local[:, None] == jnp.arange(enc_rows, dtype=jnp.int32)[None, :]).astype(BF16)
     chosen = jnp.dot(picker, down_encoder, preferred_element_type=F32).astype(BF16)
-    other = after(other, chosen)
+    chosen, other = lax.optimization_barrier((chosen, other))
     chosen = jnp.concatenate([chosen, swap(chosen)], axis=0)
-
-    dec_rows = up_decoder.shape[0]
-    slot, rows, rounds = plan(latent_ids, rank, jnp.int32(0), owners, dec_rows)
-
-    def more(carry):
-        return carry[0] < rounds[0]
-
-    def another(carry):
-        turn, have = carry
-        slot_now, rows_now, _ = plan(latent_ids, rank, turn, owners, dec_rows)
-        taken = jnp.take(up_decoder, rows_now, axis=0, mode="clip")
-        spread = exchange(tell(taken, "h").reshape(4 * CAP, 128), "x")
-        return turn + 1, expand(rounds, slot_now, have, spread)
-
-    nothing = jnp.zeros((tokens * slots, 128), BF16)
-    _, have = lax.while_loop(more, another, (jnp.int32(1), nothing))
-    chosen = tell(after(chosen, have), "x")
+    chosen = tell(chosen, "x")
 
     def columns(w):
         part = lax.dynamic_slice(w, (0, other * half), (dblk, half))
@@ -348,10 +305,13 @@
     )
     rec = swap(pack)
 
+    dec_rows = up_decoder.shape[0]
+    slot, _, rows, rounds = plan(latent_ids, rank, jnp.int32(0), rank // 4 * 4, owners, dec_rows)
     picked = jnp.take(up_decoder, rows, axis=0, mode="clip")
-
-    chosen = jnp.sum(after(chosen, picked).astype(F32), axis=0).astype(BF16)
+    picked, chosen = lax.optimization_barrier((picked, chosen))
+    chosen = jnp.sum(chosen.astype(F32), axis=0).astype(BF16)
     packet = tell(jnp.concatenate([picked, chosen], axis=0), "h")
+    column = packet[:, :CAP, :].reshape(4 * CAP, 128)
     cot = jnp.sum(packet[:, CAP:, :].astype(F32), axis=0).astype(BF16)
     cot = jnp.concatenate([cot[:features], cot[features:]], axis=1)
 
@@ -374,16 +334,29 @@
         out_specs=vmem,
         compiler_params=pltpu.CompilerParams(vmem_limit_bytes=8 * MIB),
     )(core_arg, mlp_input, cot, weight, down_weight, rec)
-    part, column = lax.optimization_barrier((part, packet[:, :CAP, :].reshape(4 * CAP, 128)))
+    part, column = lax.optimization_barrier((part, column))
     part = lax.all_to_all(part.reshape(16, padded // 16, 128), ("y", "l"), 0, 0, tiled=True)
     parts = exchange(column, "x")
     part = jnp.sum(part, axis=0)
-    part, slot, parts[1], parts[2] = lax.optimization_barrier((part, slot, parts[1], parts[2]))
+    part, slot = lax.optimization_barrier((part, slot))
     pre = lax.all_to_all(
         jnp.broadcast_to(part[None], (16,) + part.shape), ("y", "l"), 0, 0, tiled=True
     ).reshape(padded, 128)
 
-    dec = expand(rounds, slot, have, parts)
+    dec = expand(slot, parts)
+
+    def more(carry):
+        return carry[0] < rounds
+
+    def another(carry):
+        turn, have = carry
+        slot_now, here, rows_now, _ = plan(latent_ids, rank, turn, rank, owners, dec_rows)
+        taken = jnp.take(up_decoder, rows_now, axis=0, mode="clip")
+        now = expand(slot_now, exchange(jnp.concatenate(exchange(taken, "h"), axis=0), "x"))
+        here = here.reshape(tokens, slots // 4, 2, 2).transpose(0, 3, 1, 2).reshape(-1, 1)
+        return turn + 1, jnp.where(here > 0, now, have)
+
+    _, dec = lax.while_loop(more, another, (jnp.int32(1), dec))
     dec_far = swap(dec)
 
     mine, theirs = contract(core_arg, pre, weight, dec, dec_far, half, tokens, features)

time: 171 us -> 152 us (0.89)
  waiting for transfers between devices: 40.3 us -> 28.8 us
  local copies, waits for them, and re-layouts: 15.3 us -> 9.96 us
    ppermute x3, waiting for transfers between devices: 10.5 us -> 0.01 us  [exchange(): lax.ppermute(value, axis, [(i, i ^ m) for i in range(4)])]
    unnamed x32 -> x20, local copies, waits for them, and re-layouts: 7.3 us -> 3.12 us
    all_to_all x1, waiting for transfers between devices: 5.75 us -> 2.72 us  [on_device(): lax.all_to_all(part.reshape(16, padded // 16, 128), ('y', 'l'), 0, 0, til...]
    all_to_all x1, blocking collectives: 19.6 us -> 17.8 us  [on_device(): lax.all_to_all(total.reshape(16, 2, 128), ('l', 'h'), 0, 0, tiled=True)]
    all_to_all x1, waiting for transfers between devices: 0.01 us -> 1.74 us  [on_device(): lax.all_to_all(jnp.broadcast_to(part[None], (16,) + part.shape), ('y', 'l...]
  transfers between devices with their start and end apart: 11 -> 11, of which waited for: 8 -> 7; matrix products, arithmetic and copies ran while one was open for 3% -> 4% of each run, Pallas kernels for 6% -> 7%
where the time goes in v7:
time: 152 us; the launch traced here: 151 us
  starting transfers between devices  55.7 us (37%)
  blocking collectives  31.7 us (21%)
  waiting for transfers between devices  28.8 us (19%)
  Pallas kernels  19.8 us (13%)
  local copies, waits for them, and re-layouts  9.96 us (7%)
  other arithmetic  3.7 us (2%)
    all_to_all x2, starting transfers between devices, tell(): lax.all_to_all(jnp.broadcast_to(value[None], (4,) + value.shape), axis, 0...  19.4 us
    all_to_all x2, waiting for transfers between devices, tell(): lax.all_to_all(jnp.broadcast_to(value[None], (4,) + value.shape), axis, 0...  17.9 us
    all_to_all x1, blocking collectives, on_device(): lax.all_to_all(total.reshape(16, 2, 128), ('l', 'h'), 0, 0, tiled=True)  17.8 us
    all_to_all x1, blocking collectives, on_device(): lax.all_to_all(total.reshape(16, 32, 128), ('x', 'y'), 0, 0, tiled=True)  13.9 us
    all_to_all x1, starting transfers between devices, on_device(): lax.all_to_all(part.reshape(16, padded // 16, 128), ('y', 'l'), 0, 0, til...  12.1 us
    ppermute x3, starting transfers between devices, exchange(): lax.ppermute(value, axis, [(i, i ^ m) for i in range(4)])  9.81 us
    pallas_call x1, Pallas kernels, contract(): pl.pallas_call(functools.partial(main_kernel, half, tokens, features, ste...  8.52 us
    ppermute x4, starting transfers between devices, swap(): return lax.ppermute(value, 'c', [(0, 1), (1, 0)])  7.68 us
  transfers between devices with their start and end apart: 11, of which 7 were waited for; matrix products, arithmetic and copies ran while one was open for 4% of the time, Pallas kernels for 7%

profile of v7, /device:TPU:8, one launch (start us, length us, event | category | flops | bytes accessed | tf_op | source)
XLA Modules:
  0.0 150.8 jit_solution(7622075237512464970)
XLA Ops:
  0.0 0.0 copy-start
  0.0 0.7 broadcast_subtract_fusion
  0.8 0.5 copy-done
  1.2 0.3 convolution_convert_fusion
  1.6 1.9 %collective-permute-start.6 = (bf16[32,128]{1,0:T(8,128)(2,1)S(1)}, bf16[32,128]{1,0:T(8,128)(2,1)S(1)}, u32[]{:S(2)}, u32[]{:S(2)}) collective-permute-start(bf16[32,128]{1,0:T(8,128)(2,1)S(1)} %convolution_convert_fusion), channel_id=1, source_target_pairs={{0,4},{4,0},{1,5},{5,1},{2,6},{6,2},{3,7},{7,3},{8,12},{12,8},{9,1... | collective-permute-start | bytes 24584 | tf_op jit(solution)/shard_map/ppermute | solution.py:261
  3.5 0.1 pad_add_fusion.1.where_ref
  3.6 3.4 %shard_map.91 = (s32[64,64]{1,0:T(8,128)S(1)}, s32[64,64]{1,0:T(8,128)}, s32[352,1]{1,0:T(8,128)S(1)}, s32[1]{0:T(128)}) custom-call(s32[3]{0:T(128)S(1)} %pad_add_fusion.1.where_ref, s32[64,64]{1,0:T(8,128)} %ids_ref.1), custom_call_target="tpu_custom_call" | custom-call | tf_op jit(solution)/shard_map/pallas_call | solution.py:66
  7.0 0.1 reduce.3
  7.2 0.0 copy-start.1
  7.2 0.0 copy-start.2
  7.2 0.0 collective-permute-done.6
  7.2 0.6 broadcast_in_dim.17
  7.8 4.3 %all-to-all-start = ((bf16[4,64,128]{2,1,0:T(8,128)(2,1)}), bf16[4,64,128]{2,1,0:T(8,128)(2,1)S(1)}, u32[]{:S(2)}, u32[]{:S(2)}) async-start(bf16[4,64,128]{2,1,0:T(8,128)(2,1)} %broadcast_in_dim.17), calls=%async_computation | async-start | bytes 131072 | tf_op jit(solution)/shard_map/all_to_all | solution.py:139
  12.2 3.0 %gather_fusion.1 = bf16[352,128]{1,0:T(8,128)(2,1)S(1)} fusion(bf16[8192,128]{1,0:T(8,128)(2,1)} %param.17, s32[1024]{0:T(1024)S(1)} %pad_clamp_fusion.1), kind=kCustom, calls=%fused_computation.1 | custom fusion | bytes 181632 | tf_op jit(solution)/shard_map/jit(_take)/gather | solution.py:310
  15.2 2.6 %all-to-all-done = bf16[4,64,128]{2,1,0:T(8,128)(2,1)S(1)} async-done(((bf16[4,64,128]{2,1,0:T(8,128)(2,1)}), bf16[4,64,128]{2,1,0:T(8,128)(2,1)S(1)}, u32[]{:S(2)}, u32[]{:S(2)}) %all-to-all-start) | async-done | bytes 65568 | tf_op jit(solution)/shard_map/all_to_all | solution.py:139
  17.8 0.8 broadcast_in_dim.19
  18.6 15.1 %all-to-all-start.1 = ((bf16[4,416,128]{2,1,0:T(8,128)(2,1)}), bf16[4,416,128]{2,1,0:T(8,128)(2,1)}, u32[]{:S(2)}, u32[]{:S(2)}) async-start(bf16[4,416,128]{2,1,0:T(8,128)(2,1)} %broadcast_in_dim.19), calls=%async_computation.1 | async-start | bytes 851968 | tf_op jit(solution)/shard_map/all_to_all | solution.py:139
  33.7 0.0 copy-done.1
  33.7 0.0 copy-done.2
  33.7 0.0 copy-start.4
  33.7 0.0 copy-start.6
  33.8 0.2 copy.34
  33.9 0.2 copy.29
  34.1 0.2 copy.33
  34.3 0.2 copy.27
  34.5 0.2 copy-done.4
  34.7 0.0 copy-done.6
  34.8 1.9 %collective-permute-start.7 = (bf16[2752,128]{1,0:T(8,128)(2,1)S(1)}, bf16[2752,128]{1,0:T(8,128)(2,1)S(1)}, u32[]{:S(2)}, u32[]{:S(2)}) collective-permute-start(bf16[2752,128]{1,0:T(8,128)(2,1)S(1)} %pad_maximum_fusion), channel_id=1, source_target_pairs={{0,4},{4,0},{1,5},{5,1},{2,6},{6,2},{3,7},{7,3},{8,12},{12,8},{9,1... | collective-permute-start | bytes 2113544 | tf_op jit(solution)/shard_map/ppermute | solution.py:261
  36.7 2.1 %collective-permute-done.7.rec_ref = bf16[2752,128]{1,0:T(8,128)(2,1)S(1)} collective-permute-done((bf16[2752,128]{1,0:T(8,128)(2,1)S(1)}, bf16[2752,128]{1,0:T(8,128)(2,1)S(1)}, u32[]{:S(2)}, u32[]{:S(2)}) %collective-permute-start.7) | collective-permute-done | bytes 704544 | tf_op jit(solution)/shard_map/ppermute | solution.py:261
  38.9 0.0 copy-start.3
  38.9 1.0 copy-done.3
  39.9 0.1 shard_map.92.weight_ref
  40.0 15.3 %all-to-all-done.1 = bf16[4,416,128]{2,1,0:T(8,128)(2,1)} async-done(((bf16[4,416,128]{2,1,0:T(8,128)(2,1)}), bf16[4,416,128]{2,1,0:T(8,128)(2,1)}, u32[]{:S(2)}, u32[]{:S(2)}) %all-to-all-start.1) | async-done | bytes 426016 | tf_op jit(solution)/shard_map/all_to_all | solution.py:139
  55.3 0.9 slice_reduce_fusion
  56.1 1.0 slice.23
  57.2 0.0 copy-start.5
  57.2 1.0 copy-done.5
  58.2 1.2 shard_map.93
  59.4 12.1 %all-to-all-start.2 = ((f32[16,72,128]{2,1,0:T(8,128)}), f32[16,72,128]{2,1,0:T(8,128)}, u32[]{:S(2)}, u32[]{:S(2)}) async-start(f32[16,72,128]{2,1,0:T(8,128)} %bitcast.13), calls=%async_computation.2 | async-start | bytes 1179648 | tf_op jit(solution)/shard_map/all_to_all | solution.py:338
  71.5 3.4 %collective-permute-start.10 = (bf16[1408,128]{1,0:T(8,128)(2,1)S(1)}, bf16[1408,128]{1,0:T(8,128)(2,1)S(1)}, u32[]{:S(2)}, u32[]{:S(2)}) collective-permute-start(bf16[1408,128]{1,0:T(8,128)(2,1)S(1)} %bitcast.34), channel_id=1, source_target_pairs={{0,384},{128,256},{256,128},{384,0},{1,385},{129,257},{257,129},{3... | collective-permute-start | bytes 1081352 | tf_op jit(solution)/shard_map/ppermute | solution.py:134
  74.9 3.1 %collective-permute-start.9 = (bf16[1408,128]{1,0:T(8,128)(2,1)S(1)}, bf16[1408,128]{1,0:T(8,128)(2,1)S(1)}, u32[]{:S(2)}, u32[]{:S(2)}) collective-permute-start(bf16[1408,128]{1,0:T(8,128)(2,1)S(1)} %bitcast.35), channel_id=1, source_target_pairs={{0,256},{128,384},{256,0},{384,128},{1,257},{129,385},{257,1},{385... | collective-permute-start | bytes 1081352 | tf_op jit(solution)/shard_map/ppermute | solution.py:134
  78.1 3.3 %collective-permute-start.8 = (bf16[1408,128]{1,0:T(8,128)(2,1)S(1)}, bf16[1408,128]{1,0:T(8,128)(2,1)}, u32[]{:S(2)}, u32[]{:S(2)}) collective-permute-start(bf16[1408,128]{1,0:T(8,128)(2,1)S(1)} %bitcast.36), channel_id=1, source_target_pairs={{0,128},{128,0},{256,384},{384,256},{1,129},{129,1},{257,385},{385... | collective-permute-start | bytes 1081352 | tf_op jit(solution)/shard_map/ppermute | solution.py:134
  81.3 2.7 %all-to-all-done.2 = f32[16,72,128]{2,1,0:T(8,128)} async-done(((f32[16,72,128]{2,1,0:T(8,128)}), f32[16,72,128]{2,1,0:T(8,128)}, u32[]{:S(2)}, u32[]{:S(2)}) %all-to-all-start.2) | async-done | bytes 589856 | tf_op jit(solution)/shard_map/all_to_all | solution.py:338
  84.1 1.1 reduce_sum.53
  85.2 0.9 broadcast_in_dim.20
  86.0 6.7 %all-to-all-start.3 = ((f32[16,72,128]{2,1,0:T(8,128)}), f32[16,72,128]{2,1,0:T(8,128)}, u32[]{:S(2)}, u32[]{:S(2)}) async-start(f32[16,72,128]{2,1,0:T(8,128)} %broadcast_in_dim.20), calls=%async_computation.3 | async-start | bytes 1179648 | tf_op jit(solution)/shard_map/all_to_all | solution.py:342
  92.7 0.0 collective-permute-done.10.refs_3_
  92.7 0.0 collective-permute-done.9.refs_2_
  92.7 0.0 collective-permute-done.8.refs_1_
  92.7 6.6 %shard_map.94 = bf16[4096,128]{1,0:T(8,128)(2,1)} custom-call(s32[64,64]{1,0:T(8,128)S(1)} %get-tuple-element.62.slot_ref, bf16[1408,128]{1,0:T(8,128)(2,1)S(1)} %bitcast.37, bf16[1408,128]{1,0:T(8,128)(2,1)} %collective-permute-done.8.refs_1_, bf16[1408,128]{1,0:T(8,128)(2,1)S(1)} %collective-permute-done.9.refs_2_, ...), custom_call_target="tpu_custom_call" | custom-call | tf_op jit(solution)/shard_map/pallas_call | solution.py:119
  99.3 0.0 copy-done.9
  99.3 0.6 while.10
  99.9 1.9 %collective-permute-start.11 = (bf16[4096,128]{1,0:T(8,128)(2,1)}, bf16[4096,128]{1,0:T(8,128)(2,1)S(1)}, u32[]{:S(2)}, u32[]{:S(2)}) collective-permute-start(bf16[4096,128]{1,0:T(8,128)(2,1)} %get-tuple-element.65.own_ref), channel_id=1, source_target_pairs={{0,4},{4,0},{1,5},{5,1},{2,6},{6,2},{3,7},{7,3},{8,12},{12,8},{9,1... | collective-permute-start | bytes 3145736 | tf_op jit(solution)/shard_map/ppermute | solution.py:261
  101.8 2.8 %collective-permute-done.11.far_ref = bf16[4096,128]{1,0:T(8,128)(2,1)S(1)} collective-permute-done((bf16[4096,128]{1,0:T(8,128)(2,1)}, bf16[4096,128]{1,0:T(8,128)(2,1)S(1)}, u32[]{:S(2)}, u32[]{:S(2)}) %collective-permute-start.11) | collective-permute-done | bytes 1048608 | tf_op jit(solution)/shard_map/ppermute | solution.py:261
  104.7 1.7 %all-to-all-done.3 = f32[16,72,128]{2,1,0:T(8,128)} async-done(((f32[16,72,128]{2,1,0:T(8,128)}), f32[16,72,128]{2,1,0:T(8,128)}, u32[]{:S(2)}, u32[]{:S(2)}) %all-to-all-start.3) | async-done | bytes 589856 | tf_op jit(solution)/shard_map/all_to_all | solution.py:342
  106.4 8.5 %shard_map.95 = (f32[512,128]{1,0:T(8,128)S(1)}, f32[512,128]{1,0:T(8,128)S(1)}) custom-call(s32[1]{0:T(128)} %bitcast.3.core_ref, f32[1152,128]{1,0:T(8,128)} %bitcast.14.pre_ref, bf16[256,1792]{1,0:T(8,128)(2,1)S(1)} %shard_map.92.weight_ref, bf16[4096,128]{1,0:T(8,128)(2,1)} %get-tuple-element.65.own_ref, ...), custom_call_target="tpu_custom_call" | custom-call | tf_op jit(solution)/shard_map/pallas_call | solution.py:246
  114.9 0.0 copy-start.10
  114.9 1.9 %collective-permute-start.12 = (f32[512,128]{1,0:T(8,128)S(1)}, f32[512,128]{1,0:T(8,128)S(1)}, u32[]{:S(2)}, u32[]{:S(2)}) collective-permute-start(f32[512,128]{1,0:T(8,128)S(1)} %get-tuple-element.67), channel_id=1, source_target_pairs={{0,4},{4,0},{1,5},{5,1},{2,6},{6,2},{3,7},{7,3},{8,12},{12,8},{9,1... | collective-permute-start | bytes 786440 | tf_op jit(solution)/shard_map/ppermute | solution.py:261
  116.9 1.5 collective-permute-done.12
  118.4 13.9 %all_to_all.30 = f32[16,32,128]{2,1,0:T(8,128)S(1)} all-to-all(f32[16,32,128]{2,1,0:T(8,128)S(1)} %bitcast.39), channel_id=1, replica_groups=mesh['x'=4,'h'=4,'y'=4,'c'=2,'l'=4] {'x','y'}, dimensions={0} | all-to-all | bytes 524288 | tf_op jit(solution)/shard_map/all_to_all | solution.py:365
  132.3 17.8 %all_to_all.31 = f32[16,2,128]{2,1,0:T(2,128)S(1)} all-to-all(f32[16,2,128]{2,1,0:T(2,128)S(1)} %bitcast.44), channel_id=1, replica_groups=mesh['x'=4,'h'=4,'y'=4,'c'=2,'l'=4] {'l','h'}, dimensions={0} | all-to-all | bytes 32768 | tf_op jit(solution)/shard_map/all_to_all | solution.py:366
  150.1 0.1 reshape.62
  150.2 0.0 copy-done.10
  150.2 0.6 copy_multiply_fusion
  (13 shorter events, 0.2 us)
Async XLA Ops:
  0.0 1.2 copy-start
  1.6 5.6 %collective-permute-start.6 = (bf16[32,128]{1,0:T(8,128)(2,1)S(1)}, bf16[32,128]{1,0:T(8,128)(2,1)S(1)}, u32[]{:S(2)}, u32[]{:S(2)}) collective-permute-start(bf16[32,128]{1,0:T(8,128)(2,1)S(1)} %convolution_convert_fusion), channel_id=1, source_target_pairs={{0,4},{4,0},{1,5},{5,1},{2,6},{6,2},{3,7},{7,3},{8,12},{12,8},{9,1... | collective-permute-start | bytes 24584 | tf_op jit(solution)/shard_map/ppermute | solution.py:261
  7.2 26.5 %copy-start.1 = (bf16[128,1792]{1,0:T(8,128)(2,1)S(1)}, bf16[128,1792]{1,0:T(8,128)(2,1)}, u32[]{:S(2)}) copy-start(bf16[128,1792]{1,0:T(8,128)(2,1)} %gate_ref.1) | copy-start | bytes 1376260
  7.2 26.5 %copy-start.2 = (bf16[128,1792]{1,0:T(8,128)(2,1)S(1)}, bf16[128,1792]{1,0:T(8,128)(2,1)}, u32[]{:S(2)}) copy-start(bf16[128,1792]{1,0:T(8,128)(2,1)} %up_ref.1) | copy-start | bytes 1376260
  7.8 9.9 %all-to-all-start = ((bf16[4,64,128]{2,1,0:T(8,128)(2,1)}), bf16[4,64,128]{2,1,0:T(8,128)(2,1)S(1)}, u32[]{:S(2)}, u32[]{:S(2)}) async-start(bf16[4,64,128]{2,1,0:T(8,128)(2,1)} %broadcast_in_dim.17), calls=%async_computation | async-start | bytes 131072 | tf_op jit(solution)/shard_map/all_to_all | solution.py:139
  18.6 36.7 %all-to-all-start.1 = ((bf16[4,416,128]{2,1,0:T(8,128)(2,1)}), bf16[4,416,128]{2,1,0:T(8,128)(2,1)}, u32[]{:S(2)}, u32[]{:S(2)}) async-start(bf16[4,416,128]{2,1,0:T(8,128)(2,1)} %broadcast_in_dim.19), calls=%async_computation.1 | async-start | bytes 851968 | tf_op jit(solution)/shard_map/all_to_all | solution.py:139
  33.7 1.0 copy-start.4
  33.7 1.0 copy-start.6
  34.8 4.1 %collective-permute-start.7 = (bf16[2752,128]{1,0:T(8,128)(2,1)S(1)}, bf16[2752,128]{1,0:T(8,128)(2,1)S(1)}, u32[]{:S(2)}, u32[]{:S(2)}) collective-permute-start(bf16[2752,128]{1,0:T(8,128)(2,1)S(1)} %pad_maximum_fusion), channel_id=1, source_target_pairs={{0,4},{4,0},{1,5},{5,1},{2,6},{6,2},{3,7},{7,3},{8,12},{12,8},{9,1... | collective-permute-start | bytes 2113544 | tf_op jit(solution)/shard_map/ppermute | solution.py:261
  38.9 1.0 copy-start.3
  57.2 1.0 copy-start.5
  59.4 24.7 %all-to-all-start.2 = ((f32[16,72,128]{2,1,0:T(8,128)}), f32[16,72,128]{2,1,0:T(8,128)}, u32[]{:S(2)}, u32[]{:S(2)}) async-start(f32[16,72,128]{2,1,0:T(8,128)} %bitcast.13), calls=%async_computation.2 | async-start | bytes 1179648 | tf_op jit(solution)/shard_map/all_to_all | solution.py:338
  71.5 21.2 %collective-permute-start.10 = (bf16[1408,128]{1,0:T(8,128)(2,1)S(1)}, bf16[1408,128]{1,0:T(8,128)(2,1)S(1)}, u32[]{:S(2)}, u32[]{:S(2)}) collective-permute-start(bf16[1408,128]{1,0:T(8,128)(2,1)S(1)} %bitcast.34), channel_id=1, source_target_pairs={{0,384},{128,256},{256,128},{384,0},{1,385},{129,257},{257,129},{3... | collective-permute-start | bytes 1081352 | tf_op jit(solution)/shard_map/ppermute | solution.py:134
  74.9 17.8 %collective-permute-start.9 = (bf16[1408,128]{1,0:T(8,128)(2,1)S(1)}, bf16[1408,128]{1,0:T(8,128)(2,1)S(1)}, u32[]{:S(2)}, u32[]{:S(2)}) collective-permute-start(bf16[1408,128]{1,0:T(8,128)(2,1)S(1)} %bitcast.35), channel_id=1, source_target_pairs={{0,256},{128,384},{256,0},{384,128},{1,257},{129,385},{257,1},{385... | collective-permute-start | bytes 1081352 | tf_op jit(solution)/shard_map/ppermute | solution.py:134
  78.1 14.7 %collective-permute-start.8 = (bf16[1408,128]{1,0:T(8,128)(2,1)S(1)}, bf16[1408,128]{1,0:T(8,128)(2,1)}, u32[]{:S(2)}, u32[]{:S(2)}) collective-permute-start(bf16[1408,128]{1,0:T(8,128)(2,1)S(1)} %bitcast.36), channel_id=1, source_target_pairs={{0,128},{128,0},{256,384},{384,256},{1,129},{129,1},{257,385},{385... | collective-permute-start | bytes 1081352 | tf_op jit(solution)/shard_map/ppermute | solution.py:134
  86.0 20.4 %all-to-all-start.3 = ((f32[16,72,128]{2,1,0:T(8,128)}), f32[16,72,128]{2,1,0:T(8,128)}, u32[]{:S(2)}, u32[]{:S(2)}) async-start(f32[16,72,128]{2,1,0:T(8,128)} %broadcast_in_dim.20), calls=%async_computation.3 | async-start | bytes 1179648 | tf_op jit(solution)/shard_map/all_to_all | solution.py:342
  92.7 6.6 %copy-start.9 = (s32[64,64]{1,0:T(8,128)S(1)}, s32[64,64]{1,0:T(8,128)}, u32[]{:S(2)}) copy-start(s32[64,64]{1,0:T(8,128)} %ids_ref.1) | copy-start | bytes 49156
  99.9 4.8 %collective-permute-start.11 = (bf16[4096,128]{1,0:T(8,128)(2,1)}, bf16[4096,128]{1,0:T(8,128)(2,1)S(1)}, u32[]{:S(2)}, u32[]{:S(2)}) collective-permute-start(bf16[4096,128]{1,0:T(8,128)(2,1)} %get-tuple-element.65.own_ref), channel_id=1, source_target_pairs={{0,4},{4,0},{1,5},{5,1},{2,6},{6,2},{3,7},{7,3},{8,12},{12,8},{9,1... | collective-permute-start | bytes 3145736 | tf_op jit(solution)/shard_map/ppermute | solution.py:261
  114.9 35.3 %copy-start.10 = (f32[16,4]{0,1:T(4,128)S(1)}, f32[16,4]{0,1:T(4,128)}, u32[]{:S(2)}) copy-start(f32[16,4]{0,1:T(4,128)} %param.19) | copy-start | bytes 772
  114.9 3.4 %collective-permute-start.12 = (f32[512,128]{1,0:T(8,128)S(1)}, f32[512,128]{1,0:T(8,128)S(1)}, u32[]{:S(2)}, u32[]{:S(2)}) collective-permute-start(f32[512,128]{1,0:T(8,128)S(1)} %get-tuple-element.67), channel_id=1, source_target_pairs={{0,4},{4,0},{1,5},{5,1},{2,6},{6,2},{3,7},{7,3},{8,12},{12,8},{9,1... | collective-permute-start | bytes 786440 | tf_op jit(solution)/shard_map/ppermute | solution.py:261

commit v8 on v7

--- a/solution.py
+++ b/solution.py
@@ -288,6 +288,7 @@
     chosen = jnp.dot(picker, down_encoder, preferred_element_type=F32).astype(BF16)
     chosen, other = lax.optimization_barrier((chosen, other))
     chosen = jnp.concatenate([chosen, swap(chosen)], axis=0)
+    told = chosen
     chosen = tell(chosen, "x")
 
     def columns(w):
@@ -306,6 +307,7 @@
     rec = swap(pack)
 
     dec_rows = up_decoder.shape[0]
+    latent_ids = lax.optimization_barrier((latent_ids, told))[0]
     slot, _, rows, rounds = plan(latent_ids, rank, jnp.int32(0), rank // 4 * 4, owners, dec_rows)
     picked = jnp.take(up_decoder, rows, axis=0, mode="clip")
     picked, chosen = lax.optimization_barrier((picked, chosen))
@@ -334,7 +336,7 @@
         out_specs=vmem,
         compiler_params=pltpu.CompilerParams(vmem_limit_bytes=8 * MIB),
     )(core_arg, mlp_input, cot, weight, down_weight, rec)
-    part, column = lax.optimization_barrier((part, column))
+    column = lax.optimization_barrier((column, part))[0]
     part = lax.all_to_all(part.reshape(16, padded // 16, 128), ("y", "l"), 0, 0, tiled=True)
     parts = exchange(column, "x")
     part = jnp.sum(part, axis=0)

time: 152 us -> 152 us (level)
    all_to_all x2, waiting for transfers between devices: 17.9 us -> 16 us  [tell(): lax.all_to_all(jnp.broadcast_to(value[None], (4,) + value.shape), axis, 0...]
    unnamed x20 -> x21, local copies, waits for them, and re-layouts: 3.12 us -> 3.12 us
  transfers between devices with their start and end apart: 11 -> 11, of which waited for: 7 -> 7; matrix products, arithmetic and copies ran while one was open for 4% -> 5% of each run, Pallas kernels for 7% -> 7%
where the time goes in v8:
time: 152 us; the launch traced here: 151 us
  starting transfers between devices  54.5 us (36%)
  blocking collectives  32.4 us (21%)
  waiting for transfers between devices  28.9 us (19%)
  Pallas kernels  19.8 us (13%)
  local copies, waits for them, and re-layouts  9.96 us (7%)
  other arithmetic  3.7 us (2%)
    all_to_all x2, starting transfers between devices, tell(): lax.all_to_all(jnp.broadcast_to(value[None], (4,) + value.shape), axis, 0...  19.5 us
    all_to_all x1, blocking collectives, on_device(): lax.all_to_all(total.reshape(16, 2, 128), ('l', 'h'), 0, 0, tiled=True)  17.9 us
    all_to_all x2, waiting for transfers between devices, tell(): lax.all_to_all(jnp.broadcast_to(value[None], (4,) + value.shape), axis, 0...  16 us
    all_to_all x1, blocking collectives, on_device(): lax.all_to_all(total.reshape(16, 32, 128), ('x', 'y'), 0, 0, tiled=True)  14.6 us
    all_to_all x1, starting transfers between devices, on_device(): lax.all_to_all(part.reshape(16, padded // 16, 128), ('y', 'l'), 0, 0, til...  10.8 us
    ppermute x3, starting transfers between devices, exchange(): lax.ppermute(value, axis, [(i, i ^ m) for i in range(4)])  9.82 us
    pallas_call x1, Pallas kernels, contract(): pl.pallas_call(functools.partial(main_kernel, half, tokens, features, ste...  8.52 us
    ppermute x4, starting transfers between devices, swap(): return lax.ppermute(value, 'c', [(0, 1), (1, 0)])  7.68 us
  transfers between devices with their start and end apart: 11, of which 7 were waited for; matrix products, arithmetic and copies ran while one was open for 5% of the time, Pallas kernels for 7%

profile of v8, /device:TPU:8, one launch (start us, length us, event | category | flops | bytes accessed | tf_op | source)
XLA Modules:
  0.0 150.6 jit_solution(422741832610311170)
XLA Ops:
  0.0 0.0 copy-start
  0.0 0.7 broadcast_subtract_fusion
  0.8 0.5 copy-done
  1.2 0.3 convolution_convert_fusion
  1.6 1.9 %collective-permute-start.6 = (bf16[32,128]{1,0:T(8,128)(2,1)S(1)}, bf16[32,128]{1,0:T(8,128)(2,1)S(1)}, u32[]{:S(2)}, u32[]{:S(2)}) collective-permute-start(bf16[32,128]{1,0:T(8,128)(2,1)S(1)} %convolution_convert_fusion), channel_id=1, source_target_pairs={{0,4},{4,0},{1,5},{5,1},{2,6},{6,2},{3,7},{7,3},{8,12},{12,8},{9,1... | collective-permute-start | bytes 24584 | tf_op jit(solution)/shard_map/ppermute | solution.py:261
  3.5 0.1 pad_add_fusion.1.where_ref
  3.6 1.0 collective-permute-done.6
  4.6 0.6 broadcast_in_dim.17
  5.3 0.0 copy-start.1
  5.3 0.0 copy-start.2
  5.3 4.4 %all-to-all-start = ((bf16[4,64,128]{2,1,0:T(8,128)(2,1)}), bf16[4,64,128]{2,1,0:T(8,128)(2,1)S(1)}, u32[]{:S(2)}, u32[]{:S(2)}) async-start(bf16[4,64,128]{2,1,0:T(8,128)(2,1)} %broadcast_in_dim.17), calls=%async_computation | async-start | bytes 131072 | tf_op jit(solution)/shard_map/all_to_all | solution.py:139
  9.7 3.4 %shard_map.91 = (s32[64,64]{1,0:T(8,128)S(1)}, s32[64,64]{1,0:T(8,128)}, s32[352,1]{1,0:T(8,128)S(1)}, s32[1]{0:T(128)}) custom-call(s32[3]{0:T(128)S(1)} %pad_add_fusion.1.where_ref, s32[64,64]{1,0:T(8,128)} %ids_ref), custom_call_target="tpu_custom_call" | custom-call | tf_op jit(solution)/shard_map/pallas_call | solution.py:66
  13.1 0.1 reduce.3
  13.3 3.0 %gather_fusion.1 = bf16[352,128]{1,0:T(8,128)(2,1)S(1)} fusion(bf16[8192,128]{1,0:T(8,128)(2,1)} %param.17, s32[1024]{0:T(1024)S(1)} %pad_clamp_fusion.1), kind=kCustom, calls=%fused_computation.1 | custom fusion | bytes 181632 | tf_op jit(solution)/shard_map/jit(_take)/gather | solution.py:312
  16.3 0.0 all-to-all-done
  16.4 0.8 broadcast_in_dim.19
  17.2 15.1 %all-to-all-start.1 = ((bf16[4,416,128]{2,1,0:T(8,128)(2,1)}), bf16[4,416,128]{2,1,0:T(8,128)(2,1)}, u32[]{:S(2)}, u32[]{:S(2)}) async-start(bf16[4,416,128]{2,1,0:T(8,128)(2,1)} %broadcast_in_dim.19), calls=%async_computation.1 | async-start | bytes 851968 | tf_op jit(solution)/shard_map/all_to_all | solution.py:139
  32.3 0.0 copy-done.1
  32.3 0.0 copy-done.2
  32.3 0.0 copy-start.4
  32.3 0.0 copy-start.6
  32.3 0.2 copy.34
  32.5 0.2 copy.29
  32.7 0.2 copy.33
  32.9 0.2 copy.27
  33.1 0.2 copy-done.4
  33.3 0.0 copy-done.6
  33.4 1.9 %collective-permute-start.7 = (bf16[2752,128]{1,0:T(8,128)(2,1)S(1)}, bf16[2752,128]{1,0:T(8,128)(2,1)S(1)}, u32[]{:S(2)}, u32[]{:S(2)}) collective-permute-start(bf16[2752,128]{1,0:T(8,128)(2,1)S(1)} %pad_maximum_fusion), channel_id=1, source_target_pairs={{0,4},{4,0},{1,5},{5,1},{2,6},{6,2},{3,7},{7,3},{8,12},{12,8},{9,1... | collective-permute-start | bytes 2113544 | tf_op jit(solution)/shard_map/ppermute | solution.py:261
  35.3 2.1 %collective-permute-done.7.rec_ref = bf16[2752,128]{1,0:T(8,128)(2,1)S(1)} collective-permute-done((bf16[2752,128]{1,0:T(8,128)(2,1)S(1)}, bf16[2752,128]{1,0:T(8,128)(2,1)S(1)}, u32[]{:S(2)}, u32[]{:S(2)}) %collective-permute-start.7) | collective-permute-done | bytes 704544 | tf_op jit(solution)/shard_map/ppermute | solution.py:261
  37.4 0.0 copy-start.3
  37.4 1.0 copy-done.3
  38.5 0.1 shard_map.92.weight_ref
  38.6 16.0 %all-to-all-done.1 = bf16[4,416,128]{2,1,0:T(8,128)(2,1)} async-done(((bf16[4,416,128]{2,1,0:T(8,128)(2,1)}), bf16[4,416,128]{2,1,0:T(8,128)(2,1)}, u32[]{:S(2)}, u32[]{:S(2)}) %all-to-all-start.1) | async-done | bytes 426016 | tf_op jit(solution)/shard_map/all_to_all | solution.py:139
  54.5 0.9 slice_reduce_fusion
  55.4 0.0 copy-start.5
  55.4 1.0 copy-done.5
  56.4 1.2 shard_map.93
  57.7 10.8 %all-to-all-start.2 = ((f32[16,72,128]{2,1,0:T(8,128)}), f32[16,72,128]{2,1,0:T(8,128)}, u32[]{:S(2)}, u32[]{:S(2)}) async-start(f32[16,72,128]{2,1,0:T(8,128)} %bitcast.12), calls=%async_computation.2 | async-start | bytes 1179648 | tf_op jit(solution)/shard_map/all_to_all | solution.py:340
  68.5 1.0 slice.23
  69.5 4.9 %collective-permute-start.10 = (bf16[1408,128]{1,0:T(8,128)(2,1)S(1)}, bf16[1408,128]{1,0:T(8,128)(2,1)S(1)}, u32[]{:S(2)}, u32[]{:S(2)}) collective-permute-start(bf16[1408,128]{1,0:T(8,128)(2,1)S(1)} %bitcast.34), channel_id=1, source_target_pairs={{0,384},{128,256},{256,128},{384,0},{1,385},{129,257},{257,129},{3... | collective-permute-start | bytes 1081352 | tf_op jit(solution)/shard_map/ppermute | solution.py:134
  74.4 2.8 %collective-permute-start.9 = (bf16[1408,128]{1,0:T(8,128)(2,1)S(1)}, bf16[1408,128]{1,0:T(8,128)(2,1)S(1)}, u32[]{:S(2)}, u32[]{:S(2)}) collective-permute-start(bf16[1408,128]{1,0:T(8,128)(2,1)S(1)} %bitcast.35), channel_id=1, source_target_pairs={{0,256},{128,384},{256,0},{384,128},{1,257},{129,385},{257,1},{385... | collective-permute-start | bytes 1081352 | tf_op jit(solution)/shard_map/ppermute | solution.py:134
  77.2 2.2 %collective-permute-start.8 = (bf16[1408,128]{1,0:T(8,128)(2,1)S(1)}, bf16[1408,128]{1,0:T(8,128)(2,1)S(1)}, u32[]{:S(2)}, u32[]{:S(2)}) collective-permute-start(bf16[1408,128]{1,0:T(8,128)(2,1)S(1)} %bitcast.36), channel_id=1, source_target_pairs={{0,128},{128,0},{256,384},{384,256},{1,129},{129,1},{257,385},{385... | collective-permute-start | bytes 1081352 | tf_op jit(solution)/shard_map/ppermute | solution.py:134
  79.4 3.1 %all-to-all-done.2 = f32[16,72,128]{2,1,0:T(8,128)} async-done(((f32[16,72,128]{2,1,0:T(8,128)}), f32[16,72,128]{2,1,0:T(8,128)}, u32[]{:S(2)}, u32[]{:S(2)}) %all-to-all-start.2) | async-done | bytes 589856 | tf_op jit(solution)/shard_map/all_to_all | solution.py:340
  82.5 1.1 reduce_sum.53
  83.6 0.9 broadcast_in_dim.20
  84.4 6.7 %all-to-all-start.3 = ((f32[16,72,128]{2,1,0:T(8,128)}), f32[16,72,128]{2,1,0:T(8,128)}, u32[]{:S(2)}, u32[]{:S(2)}) async-start(f32[16,72,128]{2,1,0:T(8,128)} %broadcast_in_dim.20), calls=%async_computation.3 | async-start | bytes 1179648 | tf_op jit(solution)/shard_map/all_to_all | solution.py:344
  91.1 0.0 collective-permute-done.10.refs_3_
  91.1 0.0 collective-permute-done.9.refs_2_
  91.1 0.0 collective-permute-done.8.refs_1_
  91.1 6.6 %shard_map.94 = bf16[4096,128]{1,0:T(8,128)(2,1)} custom-call(s32[64,64]{1,0:T(8,128)S(1)} %get-tuple-element.62.slot_ref, bf16[1408,128]{1,0:T(8,128)(2,1)S(1)} %bitcast.37, bf16[1408,128]{1,0:T(8,128)(2,1)S(1)} %collective-permute-done.8.refs_1_, bf16[1408,128]{1,0:T(8,128)(2,1)S(1)} %collective-permute-done.9.refs_2_, ...), custom_call_target="tpu_custom_call" | custom-call | tf_op jit(solution)/shard_map/pallas_call | solution.py:119
  97.7 0.0 copy-done.9
  97.7 0.6 while.10
  98.3 1.9 %collective-permute-start.11 = (bf16[4096,128]{1,0:T(8,128)(2,1)}, bf16[4096,128]{1,0:T(8,128)(2,1)S(1)}, u32[]{:S(2)}, u32[]{:S(2)}) collective-permute-start(bf16[4096,128]{1,0:T(8,128)(2,1)} %get-tuple-element.65.own_ref), channel_id=1, source_target_pairs={{0,4},{4,0},{1,5},{5,1},{2,6},{6,2},{3,7},{7,3},{8,12},{12,8},{9,1... | collective-permute-start | bytes 3145736 | tf_op jit(solution)/shard_map/ppermute | solution.py:261
  100.2 2.8 %collective-permute-done.11.far_ref = bf16[4096,128]{1,0:T(8,128)(2,1)S(1)} collective-permute-done((bf16[4096,128]{1,0:T(8,128)(2,1)}, bf16[4096,128]{1,0:T(8,128)(2,1)S(1)}, u32[]{:S(2)}, u32[]{:S(2)}) %collective-permute-start.11) | collective-permute-done | bytes 1048608 | tf_op jit(solution)/shard_map/ppermute | solution.py:261
  103.1 2.4 %all-to-all-done.3 = f32[16,72,128]{2,1,0:T(8,128)} async-done(((f32[16,72,128]{2,1,0:T(8,128)}), f32[16,72,128]{2,1,0:T(8,128)}, u32[]{:S(2)}, u32[]{:S(2)}) %all-to-all-start.3) | async-done | bytes 589856 | tf_op jit(solution)/shard_map/all_to_all | solution.py:344
  105.4 8.5 %shard_map.95 = (f32[512,128]{1,0:T(8,128)S(1)}, f32[512,128]{1,0:T(8,128)S(1)}) custom-call(s32[1]{0:T(128)} %bitcast.3.core_ref, f32[1152,128]{1,0:T(8,128)} %bitcast.13.pre_ref, bf16[256,1792]{1,0:T(8,128)(2,1)S(1)} %shard_map.92.weight_ref, bf16[4096,128]{1,0:T(8,128)(2,1)} %get-tuple-element.65.own_ref, ...), custom_call_target="tpu_custom_call" | custom-call | tf_op jit(solution)/shard_map/pallas_call | solution.py:246
  114.0 0.0 copy-start.10
  114.0 1.9 %collective-permute-start.12 = (f32[512,128]{1,0:T(8,128)S(1)}, f32[512,128]{1,0:T(8,128)S(1)}, u32[]{:S(2)}, u32[]{:S(2)}) collective-permute-start(f32[512,128]{1,0:T(8,128)S(1)} %get-tuple-element.67), channel_id=1, source_target_pairs={{0,4},{4,0},{1,5},{5,1},{2,6},{6,2},{3,7},{7,3},{8,12},{12,8},{9,1... | collective-permute-start | bytes 786440 | tf_op jit(solution)/shard_map/ppermute | solution.py:261
  115.9 1.5 collective-permute-done.12
  117.4 14.6 %all_to_all.30 = f32[16,32,128]{2,1,0:T(8,128)S(1)} all-to-all(f32[16,32,128]{2,1,0:T(8,128)S(1)} %bitcast.39), channel_id=1, replica_groups=mesh['x'=4,'h'=4,'y'=4,'c'=2,'l'=4] {'x','y'}, dimensions={0} | all-to-all | bytes 524288 | tf_op jit(solution)/shard_map/all_to_all | solution.py:367
  132.0 17.9 %all_to_all.31 = f32[16,2,128]{2,1,0:T(2,128)S(1)} all-to-all(f32[16,2,128]{2,1,0:T(2,128)S(1)} %bitcast.44), channel_id=1, replica_groups=mesh['x'=4,'h'=4,'y'=4,'c'=2,'l'=4] {'l','h'}, dimensions={0} | all-to-all | bytes 32768 | tf_op jit(solution)/shard_map/all_to_all | solution.py:368
  149.9 0.1 reshape.62
  150.0 0.0 copy-done.10
  150.0 0.6 copy_multiply_fusion
  (14 shorter events, 0.3 us)
Async XLA Ops:
  0.0 1.2 copy-start
  1.6 3.1 %collective-permute-start.6 = (bf16[32,128]{1,0:T(8,128)(2,1)S(1)}, bf16[32,128]{1,0:T(8,128)(2,1)S(1)}, u32[]{:S(2)}, u32[]{:S(2)}) collective-permute-start(bf16[32,128]{1,0:T(8,128)(2,1)S(1)} %convolution_convert_fusion), channel_id=1, source_target_pairs={{0,4},{4,0},{1,5},{5,1},{2,6},{6,2},{3,7},{7,3},{8,12},{12,8},{9,1... | collective-permute-start | bytes 24584 | tf_op jit(solution)/shard_map/ppermute | solution.py:261
  5.3 27.0 %copy-start.1 = (bf16[128,1792]{1,0:T(8,128)(2,1)S(1)}, bf16[128,1792]{1,0:T(8,128)(2,1)}, u32[]{:S(2)}) copy-start(bf16[128,1792]{1,0:T(8,128)(2,1)} %gate_ref.1) | copy-start | bytes 1376260
  5.3 27.0 %copy-start.2 = (bf16[128,1792]{1,0:T(8,128)(2,1)S(1)}, bf16[128,1792]{1,0:T(8,128)(2,1)}, u32[]{:S(2)}) copy-start(bf16[128,1792]{1,0:T(8,128)(2,1)} %up_ref.1) | copy-start | bytes 1376260
  5.3 11.0 %all-to-all-start = ((bf16[4,64,128]{2,1,0:T(8,128)(2,1)}), bf16[4,64,128]{2,1,0:T(8,128)(2,1)S(1)}, u32[]{:S(2)}, u32[]{:S(2)}) async-start(bf16[4,64,128]{2,1,0:T(8,128)(2,1)} %broadcast_in_dim.17), calls=%async_computation | async-start | bytes 131072 | tf_op jit(solution)/shard_map/all_to_all | solution.py:139
  17.2 37.4 %all-to-all-start.1 = ((bf16[4,416,128]{2,1,0:T(8,128)(2,1)}), bf16[4,416,128]{2,1,0:T(8,128)(2,1)}, u32[]{:S(2)}, u32[]{:S(2)}) async-start(bf16[4,416,128]{2,1,0:T(8,128)(2,1)} %broadcast_in_dim.19), calls=%async_computation.1 | async-start | bytes 851968 | tf_op jit(solution)/shard_map/all_to_all | solution.py:139
  32.3 1.0 copy-start.4
  32.3 1.0 copy-start.6
  33.4 4.1 %collective-permute-start.7 = (bf16[2752,128]{1,0:T(8,128)(2,1)S(1)}, bf16[2752,128]{1,0:T(8,128)(2,1)S(1)}, u32[]{:S(2)}, u32[]{:S(2)}) collective-permute-start(bf16[2752,128]{1,0:T(8,128)(2,1)S(1)} %pad_maximum_fusion), channel_id=1, source_target_pairs={{0,4},{4,0},{1,5},{5,1},{2,6},{6,2},{3,7},{7,3},{8,12},{12,8},{9,1... | collective-permute-start | bytes 2113544 | tf_op jit(solution)/shard_map/ppermute | solution.py:261
  37.4 1.0 copy-start.3
  55.4 1.0 copy-start.5
  57.7 24.8 %all-to-all-start.2 = ((f32[16,72,128]{2,1,0:T(8,128)}), f32[16,72,128]{2,1,0:T(8,128)}, u32[]{:S(2)}, u32[]{:S(2)}) async-start(f32[16,72,128]{2,1,0:T(8,128)} %bitcast.12), calls=%async_computation.2 | async-start | bytes 1179648 | tf_op jit(solution)/shard_map/all_to_all | solution.py:340
  69.5 21.6 %collective-permute-start.10 = (bf16[1408,128]{1,0:T(8,128)(2,1)S(1)}, bf16[1408,128]{1,0:T(8,128)(2,1)S(1)}, u32[]{:S(2)}, u32[]{:S(2)}) collective-permute-start(bf16[1408,128]{1,0:T(8,128)(2,1)S(1)} %bitcast.34), channel_id=1, source_target_pairs={{0,384},{128,256},{256,128},{384,0},{1,385},{129,257},{257,129},{3... | collective-permute-start | bytes 1081352 | tf_op jit(solution)/shard_map/ppermute | solution.py:134
  74.4 16.7 %collective-permute-start.9 = (bf16[1408,128]{1,0:T(8,128)(2,1)S(1)}, bf16[1408,128]{1,0:T(8,128)(2,1)S(1)}, u32[]{:S(2)}, u32[]{:S(2)}) collective-permute-start(bf16[1408,128]{1,0:T(8,128)(2,1)S(1)} %bitcast.35), channel_id=1, source_target_pairs={{0,256},{128,384},{256,0},{384,128},{1,257},{129,385},{257,1},{385... | collective-permute-start | bytes 1081352 | tf_op jit(solution)/shard_map/ppermute | solution.py:134
  77.2 13.9 %collective-permute-start.8 = (bf16[1408,128]{1,0:T(8,128)(2,1)S(1)}, bf16[1408,128]{1,0:T(8,128)(2,1)S(1)}, u32[]{:S(2)}, u32[]{:S(2)}) collective-permute-start(bf16[1408,128]{1,0:T(8,128)(2,1)S(1)} %bitcast.36), channel_id=1, source_target_pairs={{0,128},{128,0},{256,384},{384,256},{1,129},{129,1},{257,385},{385... | collective-permute-start | bytes 1081352 | tf_op jit(solution)/shard_map/ppermute | solution.py:134
  84.4 21.0 %all-to-all-start.3 = ((f32[16,72,128]{2,1,0:T(8,128)}), f32[16,72,128]{2,1,0:T(8,128)}, u32[]{:S(2)}, u32[]{:S(2)}) async-start(f32[16,72,128]{2,1,0:T(8,128)} %broadcast_in_dim.20), calls=%async_computation.3 | async-start | bytes 1179648 | tf_op jit(solution)/shard_map/all_to_all | solution.py:344
  91.1 6.6 %copy-start.9 = (s32[64,64]{1,0:T(8,128)S(1)}, s32[64,64]{1,0:T(8,128)}, u32[]{:S(2)}) copy-start(s32[64,64]{1,0:T(8,128)} %ids_ref) | copy-start | bytes 49156
  98.3 4.8 %collective-permute-start.11 = (bf16[4096,128]{1,0:T(8,128)(2,1)}, bf16[4096,128]{1,0:T(8,128)(2,1)S(1)}, u32[]{:S(2)}, u32[]{:S(2)}) collective-permute-start(bf16[4096,128]{1,0:T(8,128)(2,1)} %get-tuple-element.65.own_ref), channel_id=1, source_target_pairs={{0,4},{4,0},{1,5},{5,1},{2,6},{6,2},{3,7},{7,3},{8,12},{12,8},{9,1... | collective-permute-start | bytes 3145736 | tf_op jit(solution)/shard_map/ppermute | solution.py:261
  114.0 36.1 %copy-start.10 = (f32[16,4]{0,1:T(4,128)S(1)}, f32[16,4]{0,1:T(4,128)}, u32[]{:S(2)}) copy-start(f32[16,4]{0,1:T(4,128)} %param.19) | copy-start | bytes 772
  114.0 3.4 %collective-permute-start.12 = (f32[512,128]{1,0:T(8,128)S(1)}, f32[512,128]{1,0:T(8,128)S(1)}, u32[]{:S(2)}, u32[]{:S(2)}) collective-permute-start(f32[512,128]{1,0:T(8,128)S(1)} %get-tuple-element.67), channel_id=1, source_target_pairs={{0,4},{4,0},{1,5},{5,1},{2,6},{6,2},{3,7},{7,3},{8,12},{12,8},{9,1... | collective-permute-start | bytes 786440 | tf_op jit(solution)/shard_map/ppermute | solution.py:261
